TPU v7x, 32 devices: a whole 2x2x4 slice. The times are simulated.
32 devices in a mesh: uly: 8 (over y, x, core), blk: 4 (over z).
Axes of the slice: x: 2, y: 2, z: 4, core: 2. Of those that a mesh axis runs over, the one named last changes fastest.
Arguments:
- queries: bfloat16 [4096, 32, 128], P(('blk', 'uly')), may hold values from -6 to 6
- keys: bfloat16 [4096, 8, 128], P(('blk', 'uly')), may hold values from -6 to 6
- values: bfloat16 [4096, 8, 128], P(('blk', 'uly')), may hold values from -6 to 6
- grad_out: bfloat16 [4096, 32, 128], P(('blk', 'uly')), may hold values from -6 to 6
- lse: float32 [32, 4096], P('uly'), may hold values from 4 to 6
- delta: float32 [32, 4096], P('uly'), may hold values from -18 to 18
- block_keys: int32 [32, 5], replicated, may hold values from -1 to 31, as said below
Outputs:
- grad_queries: bfloat16 [4096, 32, 128], P(('blk', 'uly'))
- grad_keys: bfloat16 [4096, 8, 128], P(('blk', 'uly'))
- grad_values: bfloat16 [4096, 8, 128], P(('blk', 'uly'))
Inputs may be any that keep to these rules, and one draw needn't show every extreme that they name: `block_keys`: query block b lists itself first, then 5 - 1 distinct earlier blocks c with c >= 8 * (b // 8 - 1); entries are -1 only where fewer earlier blocks exist, after the listed ones.
All inputs are finite; a program needn't handle non-finite values.
Results may differ from a plain program's by a relative error of at most 0.0053.
Values may be sent and summed in bfloat16 or wider, within the bound.
No kernel may reach another device: no remote copies, remote signals or barrier semaphores. Data moves between devices by JAX's collectives and lax.ppermute only.
A program may use at most 128 MiB of HBM per device.

v0:
```python
import math

import jax
import jax.numpy as jnp
from jax import lax
from jax.sharding import PartitionSpec as P

BLOCK = 128


def passed_along(block, axis, distance):
    devices = range(lax.axis_size(axis))
    route = [(i - distance, i) for i in devices if i - distance in devices]
    return lax.ppermute(block, axis, route)


def block_grads(
    query_rows,
    dout_rows,
    lse_rows,
    delta_rows,
    key_blocks,
    value_blocks,
    block_index,
    block_valid,
    block_diag,
    per_step,
):
    query_blocks = block_index.shape[0]
    width = key_blocks.shape[1]
    head_dim = key_blocks.shape[2]
    head_count = query_rows.shape[1]
    select = block_index.shape[1]
    step_count = query_blocks // per_step
    score_scale = 1.0 / math.sqrt(head_dim)
    query_steps = query_rows.reshape(step_count, per_step, width, head_count, head_dim)
    dout_steps = dout_rows.reshape(step_count, per_step, width, head_count, head_dim)
    lse_steps = lse_rows.reshape(head_count, step_count, per_step, width).transpose(1, 2, 0, 3)
    delta_steps = delta_rows.reshape(head_count, step_count, per_step, width).transpose(1, 2, 0, 3)
    safe_index = jnp.where(block_valid, block_index, 0).reshape(step_count, per_step, select)
    valid_steps = block_valid.reshape(step_count, per_step, select)
    diag_steps = block_diag.reshape(step_count, per_step, select)
    positions = jnp.arange(width, dtype=jnp.int32)
    causal = positions[None, :] <= positions[:, None]

    def advance(carry, inputs):
        key_acc, value_acc = carry
        query_part, dout_part, lse_part, delta_part, index_part, valid_part, diag_part = inputs
        key_part = key_blocks[index_part]
        value_part = value_blocks[index_part]
        scores = (
            jnp.einsum("pthd,pjsd->phtjs", query_part, key_part, preferred_element_type=jnp.float32)
            * score_scale
        )
        allowed = valid_part[:, None, None, :, None] & (
            jnp.logical_not(diag_part)[:, None, None, :, None] | causal[None, None, :, None, :]
        )
        probs = jnp.where(allowed, jnp.exp(scores - lse_part[:, :, :, None, None]), 0.0)
        dprobs = jnp.einsum(
            "pthd,pjsd->phtjs", dout_part, value_part, preferred_element_type=jnp.float32
        )
        dscores = probs * (dprobs - delta_part[:, :, :, None, None])
        probs_low = probs.astype(jnp.bfloat16)
        dscores_low = dscores.astype(jnp.bfloat16)
        grad_query = (
            jnp.einsum(
                "phtjs,pjsd->pthd", dscores_low, key_part, preferred_element_type=jnp.float32
            )
            * score_scale
        )
        grad_value = jnp.einsum(
            "phtjs,pthd->pjsd", probs_low, dout_part, preferred_element_type=jnp.float32
        )
        grad_key = (
            jnp.einsum(
                "phtjs,pthd->pjsd", dscores_low, query_part, preferred_element_type=jnp.float32
            )
            * score_scale
        )
        flat_index = index_part.reshape(-1)
        key_acc = key_acc.at[flat_index].add(grad_key.reshape(-1, width, head_dim))
        value_acc = value_acc.at[flat_index].add(grad_value.reshape(-1, width, head_dim))
        return ((key_acc, value_acc), grad_query)

    start = jnp.zeros((key_blocks.shape[0], width, head_dim), jnp.float32)
    (key_acc, value_acc), grad_query = lax.scan(
        advance,
        (start, start),
        (query_steps, dout_steps, lse_steps, delta_steps, safe_index, valid_steps, diag_steps),
    )
    return (grad_query.reshape(query_blocks * width, head_count, head_dim), key_acc, value_acc)


def shards(queries, keys, values, grad_out, lse, delta, block_keys):
    uly_count = lax.axis_size("uly")
    tokens_here, head_total, head_dim = queries.shape
    kv_heads = keys.shape[1]
    fold_count = uly_count // kv_heads
    slab_len = tokens_here * uly_count
    slab_blocks = slab_len // BLOCK
    per_step = math.gcd(slab_blocks, max(1, 512 // BLOCK))
    slab_index = lax.axis_index("blk")
    query_slab, dout_slab = (
        lax.all_to_all(queries, "uly", split_axis=1, concat_axis=0, tiled=True),
        lax.all_to_all(grad_out, "uly", split_axis=1, concat_axis=0, tiled=True),
    )
    repeat_count = head_total // kv_heads
    key_wide = jnp.repeat(keys, repeat_count, axis=1)
    value_wide = jnp.repeat(values, repeat_count, axis=1)
    key_here, value_here = (
        lax.all_to_all(key_wide, "uly", split_axis=1, concat_axis=0, tiled=True),
        lax.all_to_all(value_wide, "uly", split_axis=1, concat_axis=0, tiled=True),
    )
    key_slab = key_here[:, 0, :]
    value_slab = value_here[:, 0, :]
    lse_slab = lax.dynamic_slice_in_dim(lse, slab_index * slab_len, slab_len, 1)
    delta_slab = lax.dynamic_slice_in_dim(delta, slab_index * slab_len, slab_len, 1)
    slab_keys = lax.dynamic_slice_in_dim(block_keys, slab_index * slab_blocks, slab_blocks, 0)
    query_ids = slab_index * slab_blocks + jnp.arange(slab_blocks, dtype=jnp.int32)
    key_prev, value_prev = passed_along((key_slab, value_slab), "blk", 1)
    key_blocks = jnp.concatenate([key_prev, key_slab], 0).reshape(2 * slab_blocks, BLOCK, head_dim)
    value_blocks = jnp.concatenate([value_prev, value_slab], 0).reshape(
        2 * slab_blocks, BLOCK, head_dim
    )
    local_index = slab_keys - (slab_index - 1) * slab_blocks
    grad_query, key_acc, value_acc = block_grads(
        query_slab,
        dout_slab,
        lse_slab,
        delta_slab,
        key_blocks,
        value_blocks,
        local_index,
        slab_keys >= 0,
        slab_keys == query_ids[:, None],
        per_step,
    )
    key_back, value_back = passed_along((key_acc[:slab_blocks], value_acc[:slab_blocks]), "blk", -1)
    key_total = (key_acc[slab_blocks:] + key_back).reshape(slab_len, head_dim)
    value_total = (value_acc[slab_blocks:] + value_back).reshape(slab_len, head_dim)
    key_back, value_back = (
        lax.all_to_all(
            key_total.reshape(uly_count, tokens_here, head_dim),
            "uly",
            split_axis=0,
            concat_axis=1,
            tiled=True,
        ),
        lax.all_to_all(
            value_total.reshape(uly_count, tokens_here, head_dim),
            "uly",
            split_axis=0,
            concat_axis=1,
            tiled=True,
        ),
    )
    grad_keys = (
        key_back.reshape(kv_heads, fold_count, tokens_here, head_dim).sum(1).transpose(1, 0, 2)
    )
    grad_values = (
        value_back.reshape(kv_heads, fold_count, tokens_here, head_dim).sum(1).transpose(1, 0, 2)
    )
    grad_queries = lax.all_to_all(
        grad_query.astype(jnp.bfloat16), "uly", split_axis=0, concat_axis=1, tiled=True
    )
    return (grad_queries, grad_keys.astype(jnp.bfloat16), grad_values.astype(jnp.bfloat16))


def solution(mesh):
    return jax.shard_map(
        shards,
        mesh=mesh,
        in_specs=(
            P(("blk", "uly"), None, None),
            P(("blk", "uly"), None, None),
            P(("blk", "uly"), None, None),
            P(("blk", "uly"), None, None),
            P("uly", None),
            P("uly", None),
            P(),
        ),
        out_specs=(
            P(("blk", "uly"), None, None),
            P(("blk", "uly"), None, None),
            P(("blk", "uly"), None, None),
        ),
        check_vma=False,
    )
```

profile of v0, /device:TPU:0, one launch (start us, length us, event | category | flops | bytes accessed | tf_op | source)
XLA Modules:
  0.0 217.4 jit_solution(16960444307001868022)
XLA Ops:
  2.9 5.3 %all-to-all-start.2 = ((bf16[128,32,128]{2,0,1:T(8,128)(2,1)}), bf16[128,32,128]{2,0,1:T(8,128)(2,1)S(1)}, u32[]{:S(2)}, u32[]{:S(2)}) async-start(bf16[128,32,128]{2,0,1:T(8,128)(2,1)} %bitcast.14), calls=%async_computation.2 | async-start | bytes 2097152 | tf_op jit(solution)/shard_map/all_to_all | solution.py:112
  8.3 15.4 %all-to-all-done.2 = bf16[128,32,128]{2,0,1:T(8,128)(2,1)S(1)} async-done(((bf16[128,32,128]{2,0,1:T(8,128)(2,1)}), bf16[128,32,128]{2,0,1:T(8,128)(2,1)S(1)}, u32[]{:S(2)}, u32[]{:S(2)}) %all-to-all-start.2) | async-done | bytes 1048608 | tf_op jit(solution)/shard_map/all_to_all | solution.py:112
  24.8 3.6 %all-to-all-start = ((bf16[128,32,128]{2,0,1:T(8,128)(2,1)}), bf16[128,32,128]{2,0,1:T(8,128)(2,1)S(1)}, u32[]{:S(2)}, u32[]{:S(2)}) async-start(bf16[128,32,128]{2,0,1:T(8,128)(2,1)} %bitcast.3), calls=%async_computation | async-start | bytes 2097152 | tf_op jit(solution)/shard_map/all_to_all | solution.py:111
  29.8 13.9 %all-to-all-done = bf16[128,32,128]{2,0,1:T(8,128)(2,1)S(1)} async-done(((bf16[128,32,128]{2,0,1:T(8,128)(2,1)}), bf16[128,32,128]{2,0,1:T(8,128)(2,1)S(1)}, u32[]{:S(2)}, u32[]{:S(2)}) %all-to-all-start) | async-done | bytes 1048608 | tf_op jit(solution)/shard_map/all_to_all | solution.py:111
  43.7 4.2 %all-to-all-start.1 = ((bf16[128,32,128]{2,0,1:T(8,128)(2,1)}), bf16[128,32,128]{2,0,1:T(8,128)(2,1)}, u32[]{:S(2)}, u32[]{:S(2)}) async-start(bf16[128,32,128]{2,0,1:T(8,128)(2,1)} %copy.52), calls=%async_computation.1 | async-start | bytes 2097152 | tf_op jit(solution)/shard_map/all_to_all | solution.py:104
  49.7 13.7 %all-to-all-done.1 = bf16[128,32,128]{2,0,1:T(8,128)(2,1)} async-done(((bf16[128,32,128]{2,0,1:T(8,128)(2,1)}), bf16[128,32,128]{2,0,1:T(8,128)(2,1)}, u32[]{:S(2)}, u32[]{:S(2)}) %all-to-all-start.1) | async-done | bytes 1048608 | tf_op jit(solution)/shard_map/all_to_all | solution.py:104
  63.4 4.2 %all-to-all-start.3 = ((bf16[128,32,128]{2,0,1:T(8,128)(2,1)}), bf16[128,32,128]{2,0,1:T(8,128)(2,1)}, u32[]{:S(2)}, u32[]{:S(2)}) async-start(bf16[128,32,128]{2,0,1:T(8,128)(2,1)} %copy.55), calls=%async_computation.3 | async-start | bytes 2097152 | tf_op jit(solution)/shard_map/all_to_all | solution.py:105
  67.7 3.5 %collective-permute-start.1 = (bf16[1024,128]{1,0:T(8,128)(2,1)S(1)}, bf16[1024,128]{1,0:T(8,128)(2,1)S(1)}, u32[]{:S(2)}, u32[]{:S(2)}) collective-permute-start(bf16[1024,128]{1,0:T(8,128)(2,1)S(1)} %slice_bitcast_fusion), channel_id=1, source_target_pairs={{0,1},{1,2},{2,3},{4,5},{5,6},{6,7},{8,9},{9,10},{10,11},{12,13},{... | collective-permute-start | bytes 786440 | tf_op jit(solution)/shard_map/ppermute | solution.py:14
  71.3 3.5 %collective-permute-start = (bf16[1024,128]{1,0:T(8,128)(2,1)S(1)}, bf16[1024,128]{1,0:T(8,128)(2,1)S(1)}, u32[]{:S(2)}, u32[]{:S(2)}) collective-permute-start(bf16[1024,128]{1,0:T(8,128)(2,1)S(1)} %slice_bitcast_fusion.1), channel_id=1, source_target_pairs={{0,1},{1,2},{2,3},{4,5},{5,6},{6,7},{8,9},{9,10},{10,11},{12,13},{... | collective-permute-start | bytes 786440 | tf_op jit(solution)/shard_map/ppermute | solution.py:14
  78.6 4.2 %collective-permute-done = bf16[1024,128]{1,0:T(8,128)(2,1)S(1)} collective-permute-done((bf16[1024,128]{1,0:T(8,128)(2,1)S(1)}, bf16[1024,128]{1,0:T(8,128)(2,1)S(1)}, u32[]{:S(2)}, u32[]{:S(2)}) %collective-permute-start) | collective-permute-done | bytes 262176 | tf_op jit(solution)/shard_map/ppermute | solution.py:14
  85.8 69.3 %while.15 = (s32[]{:T(128)}, f32[16,128,128]{2,1,0:T(8,128)}, f32[16,128,128]{2,1,0:T(8,128)}, bf16[2,4,128,4,128]{4,2,1,0,3:T(8,128)(2,1)}, s32[2,4,5]{2,1,0:T(...) while((s32[]{:T(128)}, f32[16,128,128]{2,1,0:T(8,128)}, ...), condition=%wide.region_3.4_spmd.clone, body=%wide.region_0.3_spmd.clone.sunk | while | flops 1693009024 | bytes 54165436 | solution.py:86
  87.7 4.2 %fusion.68 = f32[4,5,128,128,4]{3,2,4,1,0:T(8,128)} fusion(bf16[4,5,128,128,1]{3,2,4,1,0:T(8,128)(2,1)S(1)} %bitcast.182, bf16[2,4,128,4,128]{4,2,3,1,0:T(8,128)(2,1)} %get-tuple-element.277, s32[]{:T(128)} %get-tuple-element.255), kind=kOutput, calls=%fused_computation.24.clone.1 | convolution fusion | flops 335544320 | bytes 6423040 | tf_op jit(solution)/shard_map/while/body/eval_jaxpr/pthd,pjsd->phtjs/dot_general | solution.py:52
  92.9 2.5 %gather_fusion.1 = bf16[20,128,128]{2,1,0:T(8,128)(2,1)} fusion(bf16[16,128,128]{2,1,0:T(8,128)(2,1)} %get-tuple-element.279, s32[1024]{0:T(1024)S(1)} %pad_clamp_fusion.2), kind=kCustom, calls=%fused_computation.1.clone.clone.1 | custom fusion | bytes 1310800 | tf_op jit(solution)/shard_map/while/body/eval_jaxpr/gather | solution.py:50
  95.5 4.5 %fusion.70 = bf16[4,4,128,5,128]{2,4,1,3,0:T(8,128)(2,1)S(1)} fusion(f32[4,5,128,128,4]{3,2,4,1,0:T(8,128)} %fusion.68, f32[4,4,128]{2,1,0:T(4,128)S(1)} %get-tuple-element.237, f32[4,4,128]{2,1,0:T(4,128)S(1)} %get-tuple-element.238, pred[4,128,5,128]{1,3,2,0:T(8,128)(4,1)} %or_and_fusion.2, bf16[4,5,128,128,1]{3,2,4,1,0:T(8,128)(2,1)} %bitcast.186, ...), kind=kOutput, calls=%fused_computation.7.clone.1 | convolution fusion | flops 343408640 | bytes 9388544 | tf_op jit(solution)/shard_map/while/body/eval_jaxpr/pthd,pjsd->phtjs/dot_general | solution.py:59
  103.6 3.0 %fusion.71 = f32[4,5,128,128]{3,2,1,0:T(8,128)} fusion(bf16[4,4,128,5,128]{2,4,1,3,0:T(8,128)(2,1)S(1)} %fusion.70, bf16[2,4,128,4,128]{4,2,3,1,0:T(8,128)(2,1)} %get-tuple-element.277, s32[]{:T(128)} %get-tuple-element.255), kind=kOutput, calls=%fused_computation.18.clone.1 | convolution fusion | flops 335872000 | bytes 4456960 | tf_op jit(solution)/shard_map/while/body/eval_jaxpr/phtjs,pthd->pjsd/dot_general | solution.py:75
  106.7 6.4 %scatter_fusion = f32[16,128,128]{2,1,0:T(8,128)} fusion(f32[16,128,128]{2,1,0:T(8,128)} %get-tuple-element.256, s32[20]{0:T(128)S(1)} %fusion.67, f32[20,128,128]{2,1,0:T(8,128)} %bitcast.184), kind=kCustom, calls=%fused_computation.2.clone.clone.1 | custom fusion | flops 327680 | bytes 3932240 | tf_op jit(solution)/shard_map/while/body/eval_jaxpr/scatter-add | solution.py:81
  113.1 3.8 %fusion.72 = f32[4,5,128,128,1]{3,2,4,1,0:T(8,128)S(1)} fusion(f32[4,5,128,128,4]{3,2,4,1,0:T(8,128)} %fusion.68, f32[4,4,128]{2,1,0:T(4,128)S(1)} %get-tuple-element.238, pred[4,128,5,128]{1,3,2,0:T(8,128)(4,1)S(1)} %copy-done.4, bf16[2,4,128,4,128]{4,2,3,1,0:T(8,128)(2,1)} %get-tuple-element.280, s32[]{:T(128)} %get-tuple-element.255), kind=kOutput, calls=%fused_computation.12.clone.1 | convolution fusion | flops 340787200 | bytes 7414272 | tf_op jit(solution)/shard_map/while/body/eval_jaxpr/phtjs,pthd->pjsd/dot_general | solution.py:71
  116.9 2.6 %scatter_fusion.1 = f32[16,128,128]{2,1,0:T(8,128)S(1)} fusion(f32[16,128,128]{2,1,0:T(8,128)S(1)} %copy-done.2, s32[20]{0:T(128)S(1)} %fusion.67, f32[20,128,128]{2,1,0:T(8,128)S(1)} %bitcast.185), kind=kCustom, calls=%fused_computation.3.clone.clone.1 | custom fusion | flops 327680 | bytes 3932240 | tf_op jit(solution)/shard_map/while/body/eval_jaxpr/scatter-add | solution.py:82
  122.3 4.2 %fusion.68 = f32[4,5,128,128,4]{3,2,4,1,0:T(8,128)} fusion(bf16[4,5,128,128,1]{3,2,4,1,0:T(8,128)(2,1)S(1)} %bitcast.182, bf16[2,4,128,4,128]{4,2,3,1,0:T(8,128)(2,1)} %get-tuple-element.277, s32[]{:T(128)} %get-tuple-element.255), kind=kOutput, calls=%fused_computation.24.clone.1 | convolution fusion | flops 335544320 | bytes 6423040 | tf_op jit(solution)/shard_map/while/body/eval_jaxpr/pthd,pjsd->phtjs/dot_general | solution.py:52
  127.6 2.5 %gather_fusion.1 = bf16[20,128,128]{2,1,0:T(8,128)(2,1)} fusion(bf16[16,128,128]{2,1,0:T(8,128)(2,1)} %get-tuple-element.279, s32[1024]{0:T(1024)S(1)} %pad_clamp_fusion.2), kind=kCustom, calls=%fused_computation.1.clone.clone.1 | custom fusion | bytes 1310800 | tf_op jit(solution)/shard_map/while/body/eval_jaxpr/gather | solution.py:50
  130.1 4.5 %fusion.70 = bf16[4,4,128,5,128]{2,4,1,3,0:T(8,128)(2,1)S(1)} fusion(f32[4,5,128,128,4]{3,2,4,1,0:T(8,128)} %fusion.68, f32[4,4,128]{2,1,0:T(4,128)S(1)} %get-tuple-element.237, f32[4,4,128]{2,1,0:T(4,128)S(1)} %get-tuple-element.238, pred[4,128,5,128]{1,3,2,0:T(8,128)(4,1)} %or_and_fusion.2, bf16[4,5,128,128,1]{3,2,4,1,0:T(8,128)(2,1)} %bitcast.186, ...), kind=kOutput, calls=%fused_computation.7.clone.1 | convolution fusion | flops 343408640 | bytes 9388544 | tf_op jit(solution)/shard_map/while/body/eval_jaxpr/pthd,pjsd->phtjs/dot_general | solution.py:59
  138.3 3.0 %fusion.71 = f32[4,5,128,128]{3,2,1,0:T(8,128)} fusion(bf16[4,4,128,5,128]{2,4,1,3,0:T(8,128)(2,1)S(1)} %fusion.70, bf16[2,4,128,4,128]{4,2,3,1,0:T(8,128)(2,1)} %get-tuple-element.277, s32[]{:T(128)} %get-tuple-element.255), kind=kOutput, calls=%fused_computation.18.clone.1 | convolution fusion | flops 335872000 | bytes 4456960 | tf_op jit(solution)/shard_map/while/body/eval_jaxpr/phtjs,pthd->pjsd/dot_general | solution.py:75
  141.3 6.4 %scatter_fusion = f32[16,128,128]{2,1,0:T(8,128)} fusion(f32[16,128,128]{2,1,0:T(8,128)} %get-tuple-element.256, s32[20]{0:T(128)S(1)} %fusion.67, f32[20,128,128]{2,1,0:T(8,128)} %bitcast.184), kind=kCustom, calls=%fused_computation.2.clone.clone.1 | custom fusion | flops 327680 | bytes 3932240 | tf_op jit(solution)/shard_map/while/body/eval_jaxpr/scatter-add | solution.py:81
  147.7 3.8 %fusion.72 = f32[4,5,128,128,1]{3,2,4,1,0:T(8,128)S(1)} fusion(f32[4,5,128,128,4]{3,2,4,1,0:T(8,128)} %fusion.68, f32[4,4,128]{2,1,0:T(4,128)S(1)} %get-tuple-element.238, pred[4,128,5,128]{1,3,2,0:T(8,128)(4,1)S(1)} %copy-done.4, bf16[2,4,128,4,128]{4,2,3,1,0:T(8,128)(2,1)} %get-tuple-element.280, s32[]{:T(128)} %get-tuple-element.255), kind=kOutput, calls=%fused_computation.12.clone.1 | convolution fusion | flops 340787200 | bytes 7414272 | tf_op jit(solution)/shard_map/while/body/eval_jaxpr/phtjs,pthd->pjsd/dot_general | solution.py:71
  151.5 2.6 %scatter_fusion.1 = f32[16,128,128]{2,1,0:T(8,128)S(1)} fusion(f32[16,128,128]{2,1,0:T(8,128)S(1)} %copy-done.2, s32[20]{0:T(128)S(1)} %fusion.67, f32[20,128,128]{2,1,0:T(8,128)S(1)} %bitcast.185), kind=kCustom, calls=%fused_computation.3.clone.clone.1 | custom fusion | flops 327680 | bytes 3932240 | tf_op jit(solution)/shard_map/while/body/eval_jaxpr/scatter-add | solution.py:82
  160.1 13.5 %collective-permute-done.3 = f32[8,128,128]{2,1,0:T(8,128)S(1)} collective-permute-done((f32[8,128,128]{2,1,0:T(8,128)S(1)}, f32[8,128,128]{2,1,0:T(8,128)S(1)}, u32[]{:S(2)}, u32[]{:S(2)}) %collective-permute-start.3) | collective-permute-done | bytes 524320 | tf_op jit(solution)/shard_map/ppermute | solution.py:14
  175.4 3.9 %all-to-all-start.6 = ((bf16[8,128,128]{2,1,0:T(8,128)(2,1)}), bf16[8,128,128]{2,1,0:T(8,128)(2,1)S(1)}, u32[]{:S(2)}, u32[]{:S(2)}) async-start(bf16[8,128,128]{2,1,0:T(8,128)(2,1)} %slice_add_fusion), calls=%async_computation.6 | async-start | bytes 524288 | tf_op jit(solution)/shard_map/all_to_all | solution.py:149
  179.3 4.4 %collective-permute-done.2 = f32[8,128,128]{2,1,0:T(8,128)S(1)} collective-permute-done((f32[8,128,128]{2,1,0:T(8,128)S(1)}, f32[8,128,128]{2,1,0:T(8,128)S(1)}, u32[]{:S(2)}, u32[]{:S(2)}) %collective-permute-start.2) | collective-permute-done | bytes 524320 | tf_op jit(solution)/shard_map/ppermute | solution.py:14
  186.3 3.4 %all-to-all-start.5 = ((bf16[8,128,128]{2,1,0:T(8,128)(2,1)}), bf16[8,128,128]{2,1,0:T(8,128)(2,1)S(1)}, u32[]{:S(2)}, u32[]{:S(2)}) async-start(bf16[8,128,128]{2,1,0:T(8,128)(2,1)} %slice_add_fusion.1), calls=%async_computation.5 | async-start | bytes 524288 | tf_op jit(solution)/shard_map/all_to_all | solution.py:142
  191.5 5.1 %all-to-all-done.5 = bf16[8,128,128]{2,1,0:T(8,128)(2,1)S(1)} async-done(((bf16[8,128,128]{2,1,0:T(8,128)(2,1)}), bf16[8,128,128]{2,1,0:T(8,128)(2,1)S(1)}, u32[]{:S(2)}, u32[]{:S(2)}) %all-to-all-start.5) | async-done | bytes 262176 | tf_op jit(solution)/shard_map/all_to_all | solution.py:142
  196.6 3.6 %all-to-all-start.4 = ((bf16[1024,4,128]{2,1,0:T(4,128)(2,1)}), bf16[1024,4,128]{2,1,0:T(4,128)(2,1)S(1)}, u32[]{:S(2)}, u32[]{:S(2)}) async-start(bf16[1024,4,128]{2,1,0:T(4,128)(2,1)} %copy.57), calls=%async_computation.4 | async-start | bytes 2097152 | tf_op jit(solution)/shard_map/all_to_all | solution.py:163
  201.9 13.6 %all-to-all-done.4 = bf16[1024,4,128]{2,1,0:T(4,128)(2,1)S(1)} async-done(((bf16[1024,4,128]{2,1,0:T(4,128)(2,1)}), bf16[1024,4,128]{2,1,0:T(4,128)(2,1)S(1)}, u32[]{:S(2)}, u32[]{:S(2)}) %all-to-all-start.4) | async-done | bytes 1048608 | tf_op jit(solution)/shard_map/all_to_all | solution.py:163
  (86 shorter events, 43.5 us)
Async XLA Ops:
  0.6 47.3 %copy-start = (s32[32,5]{0,1:T(8,128)S(1)}, s32[32,5]{0,1:T(8,128)}, u32[]{:S(2)}) copy-start(s32[32,5]{0,1:T(8,128)} %param.15) | copy-start | bytes 1924
  0.6 7.6 %copy-start.8 = (bf16[128,8,128]{2,1,0:T(8,128)(2,1)S(1)}, bf16[128,8,128]{2,1,0:T(8,128)(2,1)}, u32[]{:S(2)}) copy-start(bf16[128,8,128]{2,1,0:T(8,128)(2,1)} %param.10) | copy-start | bytes 786436
  2.9 25.5 %copy-start.5 = (bf16[128,32,128]{2,1,0:T(8,128)(2,1)S(1)}, bf16[128,32,128]{2,1,0:T(8,128)(2,1)}, u32[]{:S(2)}) copy-start(bf16[128,32,128]{2,1,0:T(8,128)(2,1)} %param.9) | copy-start | bytes 3145732
  2.9 20.7 %all-to-all-start.2 = ((bf16[128,32,128]{2,0,1:T(8,128)(2,1)}), bf16[128,32,128]{2,0,1:T(8,128)(2,1)S(1)}, u32[]{:S(2)}, u32[]{:S(2)}) async-start(bf16[128,32,128]{2,0,1:T(8,128)(2,1)} %bitcast.14), calls=%async_computation.2 | async-start | bytes 2097152 | tf_op jit(solution)/shard_map/all_to_all | solution.py:112
  24.8 18.9 %all-to-all-start = ((bf16[128,32,128]{2,0,1:T(8,128)(2,1)}), bf16[128,32,128]{2,0,1:T(8,128)(2,1)S(1)}, u32[]{:S(2)}, u32[]{:S(2)}) async-start(bf16[128,32,128]{2,0,1:T(8,128)(2,1)} %bitcast.3), calls=%async_computation | async-start | bytes 2097152 | tf_op jit(solution)/shard_map/all_to_all | solution.py:111
  29.8 18.3 %copy-start.6 = (bf16[128,32,128]{2,1,0:T(8,128)(2,1)S(1)}, bf16[128,32,128]{2,1,0:T(8,128)(2,1)}, u32[]{:S(2)}) copy-start(bf16[128,32,128]{2,1,0:T(8,128)(2,1)} %param.12) | copy-start | bytes 3145732
  43.7 19.7 %all-to-all-start.1 = ((bf16[128,32,128]{2,0,1:T(8,128)(2,1)}), bf16[128,32,128]{2,0,1:T(8,128)(2,1)}, u32[]{:S(2)}, u32[]{:S(2)}) async-start(bf16[128,32,128]{2,0,1:T(8,128)(2,1)} %copy.52), calls=%async_computation.1 | async-start | bytes 2097152 | tf_op jit(solution)/shard_map/all_to_all | solution.py:104
  63.4 20.3 %all-to-all-start.3 = ((bf16[128,32,128]{2,0,1:T(8,128)(2,1)}), bf16[128,32,128]{2,0,1:T(8,128)(2,1)}, u32[]{:S(2)}, u32[]{:S(2)}) async-start(bf16[128,32,128]{2,0,1:T(8,128)(2,1)} %copy.55), calls=%async_computation.3 | async-start | bytes 2097152 | tf_op jit(solution)/shard_map/all_to_all | solution.py:105
  67.7 10.1 %collective-permute-start.1 = (bf16[1024,128]{1,0:T(8,128)(2,1)S(1)}, bf16[1024,128]{1,0:T(8,128)(2,1)S(1)}, u32[]{:S(2)}, u32[]{:S(2)}) collective-permute-start(bf16[1024,128]{1,0:T(8,128)(2,1)S(1)} %slice_bitcast_fusion), channel_id=1, source_target_pairs={{0,1},{1,2},{2,3},{4,5},{5,6},{6,7},{8,9},{9,10},{10,11},{12,13},{... | collective-permute-start | bytes 786440 | tf_op jit(solution)/shard_map/ppermute | solution.py:14
  71.3 11.5 %collective-permute-start = (bf16[1024,128]{1,0:T(8,128)(2,1)S(1)}, bf16[1024,128]{1,0:T(8,128)(2,1)S(1)}, u32[]{:S(2)}, u32[]{:S(2)}) collective-permute-start(bf16[1024,128]{1,0:T(8,128)(2,1)S(1)} %slice_bitcast_fusion.1), channel_id=1, source_target_pairs={{0,1},{1,2},{2,3},{4,5},{5,6},{6,7},{8,9},{9,10},{10,11},{12,13},{... | collective-permute-start | bytes 786440 | tf_op jit(solution)/shard_map/ppermute | solution.py:14
  106.6 6.5 %copy-start.4 = (pred[4,128,5,128]{1,3,2,0:T(8,128)(4,1)S(1)}, pred[4,128,5,128]{1,3,2,0:T(8,128)(4,1)}, u32[]{:S(2)}) copy-start(pred[4,128,5,128]{1,3,2,0:T(8,128)(4,1)} %or_and_fusion.2) | copy-start | bytes 983044 | tf_op jit(solution)/shard_map/while
  113.1 3.8 %copy-start.2 = (f32[16,128,128]{2,1,0:T(8,128)S(1)}, f32[16,128,128]{2,1,0:T(8,128)}, u32[]{:S(2)}) copy-start(f32[16,128,128]{2,1,0:T(8,128)} %get-tuple-element.257) | copy-start | bytes 3145732 | tf_op jit(solution)/shard_map/while
  119.5 1.0 copy-start.3
  141.2 6.5 %copy-start.4 = (pred[4,128,5,128]{1,3,2,0:T(8,128)(4,1)S(1)}, pred[4,128,5,128]{1,3,2,0:T(8,128)(4,1)}, u32[]{:S(2)}) copy-start(pred[4,128,5,128]{1,3,2,0:T(8,128)(4,1)} %or_and_fusion.2) | copy-start | bytes 983044 | tf_op jit(solution)/shard_map/while
  147.7 3.8 %copy-start.2 = (f32[16,128,128]{2,1,0:T(8,128)S(1)}, f32[16,128,128]{2,1,0:T(8,128)}, u32[]{:S(2)}) copy-start(f32[16,128,128]{2,1,0:T(8,128)} %get-tuple-element.257) | copy-start | bytes 3145732 | tf_op jit(solution)/shard_map/while
  154.1 1.0 copy-start.3
  155.1 28.6 %copy-start.1 = (f32[16,128,128]{2,1,0:T(8,128)S(1)}, f32[16,128,128]{2,1,0:T(8,128)}, u32[]{:S(2)}) copy-start(f32[16,128,128]{2,1,0:T(8,128)} %get-tuple-element.78) | copy-start | bytes 3145732
  156.3 33.4 %copy-start.7 = (bf16[2,4,128,4,128]{4,2,1,0,3:T(8,128)(2,1)S(1)}, bf16[2,4,128,4,128]{4,2,1,0,3:T(8,128)(2,1)}, u32[]{:S(2)}) copy-start(bf16[2,4,128,4,128]{4,2,1,0,3:T(8,128)(2,1)} %get-tuple-element.77) | copy-start | bytes 3145732
  156.3 17.3 %collective-permute-start.3 = (f32[8,128,128]{2,1,0:T(8,128)S(1)}, f32[8,128,128]{2,1,0:T(8,128)S(1)}, u32[]{:S(2)}, u32[]{:S(2)}) collective-permute-start(f32[8,128,128]{2,1,0:T(8,128)S(1)} %slice.23), channel_id=1, source_target_pairs={{1,0},{2,1},{3,2},{5,4},{6,5},{7,6},{9,8},{10,9},{11,10},{13,12},{... | collective-permute-start | bytes 1572872 | tf_op jit(solution)/shard_map/ppermute | solution.py:14
  158.8 24.9 %collective-permute-start.2 = (f32[8,128,128]{2,1,0:T(8,128)S(1)}, f32[8,128,128]{2,1,0:T(8,128)S(1)}, u32[]{:S(2)}, u32[]{:S(2)}) collective-permute-start(f32[8,128,128]{2,1,0:T(8,128)S(1)} %slice.21), channel_id=1, source_target_pairs={{1,0},{2,1},{3,2},{5,4},{6,5},{7,6},{9,8},{10,9},{11,10},{13,12},{... | collective-permute-start | bytes 1572872 | tf_op jit(solution)/shard_map/ppermute | solution.py:14
  175.4 10.8 %all-to-all-start.6 = ((bf16[8,128,128]{2,1,0:T(8,128)(2,1)}), bf16[8,128,128]{2,1,0:T(8,128)(2,1)S(1)}, u32[]{:S(2)}, u32[]{:S(2)}) async-start(bf16[8,128,128]{2,1,0:T(8,128)(2,1)} %slice_add_fusion), calls=%async_computation.6 | async-start | bytes 524288 | tf_op jit(solution)/shard_map/all_to_all | solution.py:149
  186.3 10.3 %all-to-all-start.5 = ((bf16[8,128,128]{2,1,0:T(8,128)(2,1)}), bf16[8,128,128]{2,1,0:T(8,128)(2,1)S(1)}, u32[]{:S(2)}, u32[]{:S(2)}) async-start(bf16[8,128,128]{2,1,0:T(8,128)(2,1)} %slice_add_fusion.1), calls=%async_computation.5 | async-start | bytes 524288 | tf_op jit(solution)/shard_map/all_to_all | solution.py:142
  196.6 18.9 %all-to-all-start.4 = ((bf16[1024,4,128]{2,1,0:T(4,128)(2,1)}), bf16[1024,4,128]{2,1,0:T(4,128)(2,1)S(1)}, u32[]{:S(2)}, u32[]{:S(2)}) async-start(bf16[1024,4,128]{2,1,0:T(4,128)(2,1)} %copy.57), calls=%async_computation.4 | async-start | bytes 2097152 | tf_op jit(solution)/shard_map/all_to_all | solution.py:163
where the time goes:
time: 219 us; the launch traced here: 217 us
  waiting for transfers between devices  87.7 us (40%)
  starting transfers between devices  37.9 us (17%)
  matrix products  33.7 us (15%)
  local copies, waits for them, and re-layouts  32.5 us (15%)
  other arithmetic  24.5 us (11%)
    ppermute x4, waiting for transfers between devices, passed_along(): return lax.ppermute(block, axis, route)  24.3 us
    all_to_all x1, waiting for transfers between devices, shards(): lax.all_to_all(value_wide, 'uly', split_axis=1, concat_axis=0, tiled=True)  15.4 us
    all_to_all x1, waiting for transfers between devices, shards(): lax.all_to_all(key_wide, 'uly', split_axis=1, concat_axis=0, tiled=True)  13.9 us
    all_to_all x1, waiting for transfers between devices, shards(): lax.all_to_all(queries, 'uly', split_axis=1, concat_axis=0, tiled=True)  13.7 us
    all_to_all x1, waiting for transfers between devices, shards(): lax.all_to_all(grad_query.astype(jnp.bfloat16), 'uly', split_axis=0, conc...  13.6 us
    scatter-add x2, other arithmetic, advance(): key_acc = key_acc.at[flat_index].add(grad_key.reshape(-1, width, head_dim))  12.8 us
    ppermute x4, starting transfers between devices, passed_along(): return lax.ppermute(block, axis, route)  9.71 us
    dot_general x2, matrix products, advance(): jnp.einsum('pthd,pjsd->phtjs', dout_part, value_part, preferred_element_t...  8.92 us
  transfers between devices with their start and end apart: 11, of which 10 were waited for; matrix products, arithmetic and copies ran while one was open for 6% of the time, Pallas kernels for 0%

commit v1 on v0

v1 whole, which is shorter than its diff:
```python
import functools
import math

import jax
import jax.numpy as jnp
from jax import lax
from jax.experimental import pallas as pl
from jax.experimental.pallas import tpu as pltpu
from jax.sharding import PartitionSpec as P

BLOCK = 128
LOG2E = 1.4426950408889634


def contract(a, b, a_dim, b_dim):
    return lax.dot_general(a, b, (((a_dim,), (b_dim,)), ((), ())), preferred_element_type=jnp.float32)


def block_kernel(slab_ref, keys_ref, qd_ref, own_ref, prev_ref, lse_ref, delta_ref, dq_ref, own_out, prev_out, kv, kt, acc, cat_k, cat_v, cat_t):
    slab_blocks = qd_ref.shape[0]
    heads = qd_ref.shape[2]
    select = keys_ref.shape[1]
    rows = heads * BLOCK
    head_dim = qd_ref.shape[4]
    scale = 1.0 / math.sqrt(head_dim)
    first = slab_ref[0] * slab_blocks

    def stage(c, _):
        for half, ref in ((0, prev_ref), (1, own_ref)):
            at = half * slab_blocks + c
            kv[0, at] = ref[c, 0]
            kv[1, at] = ref[c, 1]
            kt[at] = ref[c, 0].T
        return _

    lax.fori_loop(0, slab_blocks, stage, 0)
    acc[...] = jnp.zeros_like(acc)
    key_pos = lax.broadcasted_iota(jnp.int32, (BLOCK, rows), 0)
    query_pos = lax.broadcasted_iota(jnp.int32, (BLOCK, rows), 1) % BLOCK
    causal = key_pos <= query_pos

    def query_block(b, _):
        q = qd_ref[b, 0].reshape(rows, head_dim)
        do = qd_ref[b, 1].reshape(rows, head_dim)
        entries = [keys_ref[first + b, j] for j in range(select)]
        places = [jnp.where(e >= 0, e - first + slab_blocks, 0) for e in entries]
        for j in range(select):
            cat_k[pl.ds(j * BLOCK, BLOCK)] = kv[0, places[j]]
            cat_v[pl.ds(j * BLOCK, BLOCK)] = kv[1, places[j]]
            cat_t[:, pl.ds(j * BLOCK, BLOCK)] = kt[places[j]]
        lanes = pl.ds(pl.multiple_of((first + b) * BLOCK, BLOCK), BLOCK)
        lse = jnp.concatenate([lse_ref[pl.ds(h, 1), lanes] for h in range(heads)], 1) * LOG2E
        delta = jnp.concatenate([delta_ref[pl.ds(h, 1), lanes] for h in range(heads)], 1)
        s = contract(cat_k[...], q, 1, 1)
        dp = contract(cat_v[...], do, 1, 1)
        p_parts = []
        for j in range(select):
            p = jnp.exp2(s[j * BLOCK : (j + 1) * BLOCK] * (scale * LOG2E) - lse)
            allowed = causal if j == 0 else entries[j] >= 0
            p_parts.append(jnp.where(allowed, p, 0.0))
        p = jnp.concatenate(p_parts, 0)
        ds = (p * (dp - delta)).astype(jnp.bfloat16)
        dv = contract(p.astype(jnp.bfloat16), do, 1, 0)
        dk = contract(ds, q, 1, 0)
        dqt = contract(cat_t[...], ds, 1, 0) * scale
        dq_ref[b] = dqt.T.astype(jnp.bfloat16).reshape(heads, BLOCK, head_dim)
        for j in range(select):
            part = slice(j * BLOCK, (j + 1) * BLOCK)
            acc[0, places[j]] += dk[part]
            acc[1, places[j]] += dv[part]
        return _

    lax.fori_loop(0, slab_blocks, query_block, 0)

    def finish(c, _):
        prev_out[c, 0] = (acc[0, c] * scale).astype(prev_out.dtype)
        prev_out[c, 1] = acc[1, c].astype(prev_out.dtype)
        own_out[c, 0] = acc[0, slab_blocks + c] * scale
        own_out[c, 1] = acc[1, slab_blocks + c]
        return _

    lax.fori_loop(0, slab_blocks, finish, 0)


def block_grads(slab, block_keys, qd, own, prev, lse, delta):
    slab_blocks, _, heads, _, head_dim = qd.shape
    select = block_keys.shape[1]
    smem = pl.BlockSpec(memory_space=pltpu.SMEM)
    vmem = pl.BlockSpec(memory_space=pltpu.VMEM)
    kv_shape = (slab_blocks, 2, BLOCK, head_dim)
    wide = select * BLOCK
    macs = slab_blocks * heads * select * 5 * BLOCK * BLOCK * head_dim
    return pl.pallas_call(
        block_kernel,
        in_specs=[smem, smem, vmem, vmem, vmem, vmem, vmem],
        out_specs=[vmem, vmem, vmem],
        out_shape=[
            jax.ShapeDtypeStruct((slab_blocks, heads, BLOCK, head_dim), jnp.bfloat16),
            jax.ShapeDtypeStruct(kv_shape, jnp.float32),
            jax.ShapeDtypeStruct(kv_shape, jnp.bfloat16),
        ],
        scratch_shapes=[
            pltpu.VMEM((2, 2 * slab_blocks, BLOCK, head_dim), jnp.bfloat16),
            pltpu.VMEM((2 * slab_blocks, head_dim, BLOCK), jnp.bfloat16),
            pltpu.VMEM((2, 2 * slab_blocks, BLOCK, head_dim), jnp.float32),
            pltpu.VMEM((wide, head_dim), jnp.bfloat16),
            pltpu.VMEM((wide, head_dim), jnp.bfloat16),
            pltpu.VMEM((head_dim, wide), jnp.bfloat16),
        ],
        compiler_params=pltpu.CompilerParams(vmem_limit_bytes=48 * 1024 * 1024),
        cost_estimate=pl.CostEstimate(flops=2 * macs, bytes_accessed=8 * 1024 * 1024, transcendentals=0),
    )(slab, block_keys, qd, own, prev, lse, delta)


def passed_along(block, axis, distance):
    devices = range(lax.axis_size(axis))
    return lax.ppermute(block, axis, [(i - distance, i) for i in devices if i - distance in devices])


def exchange(x):
    return lax.all_to_all(x, "uly", split_axis=0, concat_axis=0, tiled=True)


def by_head(x, uly_count):
    tokens, heads, head_dim = x.shape
    return x.reshape(tokens, uly_count, heads // uly_count, head_dim).transpose(1, 2, 0, 3)


def shards(queries, keys, values, grad_out, lse, delta, block_keys):
    uly_count = lax.axis_size("uly")
    tokens_here, head_total, head_dim = queries.shape
    kv_heads = keys.shape[1]
    fold_count = uly_count // kv_heads
    heads = head_total // uly_count
    slab = lax.axis_index("blk").reshape(1)

    kv = jnp.stack([keys.transpose(1, 0, 2), values.transpose(1, 0, 2)], 1)
    own = exchange(jnp.repeat(kv, fold_count, axis=0))
    prev = passed_along(own, "blk", 1)
    qd = exchange(jnp.stack([by_head(queries, uly_count), by_head(grad_out, uly_count)], 1))
    dq, own_grad, prev_grad = block_grads(slab, block_keys, qd, own, prev, lse, delta)
    back = passed_along(prev_grad, "blk", -1)
    grad_queries = exchange(dq)
    grad_queries = grad_queries.reshape(head_total, tokens_here, head_dim).transpose(1, 0, 2)
    kv_grad = exchange((own_grad + back.astype(jnp.float32)).astype(jnp.bfloat16))
    kv_grad = kv_grad.reshape(kv_heads, fold_count, 2, tokens_here, head_dim).astype(jnp.float32).sum(1)
    kv_grad = kv_grad.transpose(1, 2, 0, 3).astype(jnp.bfloat16)
    return grad_queries, kv_grad[0], kv_grad[1]


def solution(mesh):
    spread = P(("blk", "uly"), None, None)
    return jax.shard_map(
        shards,
        mesh=mesh,
        in_specs=(spread, spread, spread, spread, P("uly", None), P("uly", None), P()),
        out_specs=(spread, spread, spread),
        check_vma=False,
    )
```

time: 219 us -> 99 us (0.45)
  waiting for transfers between devices: 87.7 us -> 52.4 us
  matrix products: 33.7 us -> 0 us
  local copies, waits for them, and re-layouts: 32.5 us -> 9.25 us
  other arithmetic: 24.5 us -> 3.29 us
  starting transfers between devices: 37.9 us -> 21.2 us
  Pallas kernels: 0 us -> 11.5 us
    all_to_all x7 -> x4, waiting for transfers between devices: 63.4 us -> 26.1 us  [exchange(): return lax.all_to_all(x, 'uly', split_axis=0, concat_axis=0, tiled=True)]
    dot_general x10 -> x0, matrix products: 33.7 us -> none  [the longest x2 8.92 us: advance(): jnp.einsum('pthd,pjsd->phtjs', dout_part, value_part, preferred_element_t...]
    scatter-add x4 -> x0, other arithmetic: 18 us -> none  [the longest x2 12.8 us: advance(): key_acc = key_acc.at[flat_index].add(grad_key.reshape(-1, width, head_dim))]
    all_to_all x7 -> x4, starting transfers between devices: 28.2 us -> 16.3 us  [exchange(): return lax.all_to_all(x, 'uly', split_axis=0, concat_axis=0, tiled=True)]
    pallas_call x0 -> x1, Pallas kernels: none -> 11.5 us  [block_grads(): pl.pallas_call(block_kernel, in_specs=[smem, smem, vmem, vmem, vmem, vmem...]
    gather x4 -> x0, local copies, waits for them, and re-layouts: 8.52 us -> none  [the longest x2 5.09 us: advance(): value_part = value_blocks[index_part]]
    ppermute x4 -> x2, starting transfers between devices: 9.71 us -> 4.84 us  [passed_along(): lax.ppermute(block, axis, [(i - distance, i) for i in devices if i - dist...]
    broadcast_in_dim x4 -> x0, local copies, waits for them, and re-layouts: 4.59 us -> none  [the longest x2 2.17 us: block_grads(): start = jnp.zeros((key_blocks.shape[0], width, head_dim), jnp.float32)]
  transfers between devices with their start and end apart: 11 -> 6, of which waited for: 10 -> 5; matrix products, arithmetic and copies ran while one was open for 6% -> 5% of each run, Pallas kernels for 0% -> 0%
where the time goes in v1:
time: 99 us; the launch traced here: 98.4 us
  waiting for transfers between devices  52.4 us (53%)
  starting transfers between devices  21.2 us (21%)
  Pallas kernels  11.5 us (12%)
  local copies, waits for them, and re-layouts  9.25 us (9%)
  other arithmetic  3.29 us (3%)
    ppermute x2, waiting for transfers between devices, passed_along(): lax.ppermute(block, axis, [(i - distance, i) for i in devices if i - dist...  26.4 us
    all_to_all x4, waiting for transfers between devices, exchange(): return lax.all_to_all(x, 'uly', split_axis=0, concat_axis=0, tiled=True)  26.1 us
    all_to_all x4, starting transfers between devices, exchange(): return lax.all_to_all(x, 'uly', split_axis=0, concat_axis=0, tiled=True)  16.3 us
    pallas_call x1, Pallas kernels, block_grads(): pl.pallas_call(block_kernel, in_specs=[smem, smem, vmem, vmem, vmem, vmem...  11.5 us
    unnamed x27, local copies, waits for them, and re-layouts  6.35 us
    ppermute x2, starting transfers between devices, passed_along(): lax.ppermute(block, axis, [(i - distance, i) for i in devices if i - dist...  4.84 us
  transfers between devices with their start and end apart: 6, of which 5 were waited for; matrix products, arithmetic and copies ran while one was open for 5% of the time, Pallas kernels for 0%

profile of v1, /device:TPU:0, one launch (start us, length us, event | category | flops | bytes accessed | tf_op | source)
XLA Modules:
  0.0 98.4 jit_solution(12157799113981135720)
XLA Ops:
  0.6 0.0 copy-start.8
  0.6 1.2 %copy_bitcast_fusion.1 = (bf16[8,1,128,128]{3,2,1,0:T(8,128)(2,1)S(1)}, bf16[8,1,128,128]{3,2,1,0:T(8,128)(2,1)S(1)}) fusion(bf16[128,8,128]{2,1,0:T(8,128)(2,1)} %param.9, bf16[128,8,128]{2,1,0:T(8,128)(2,1)} %param.8), kind=kLoop, calls=%fused_computation.6 | loop fusion | bytes 1048576 | tf_op jit(solution)/shard_map/stack | solution.py:137
  1.9 0.0 copy-start.9
  1.9 0.8 pad_maximum_fusion.1
  2.7 5.2 %all-to-all-start.1 = ((bf16[8,2,128,128]{3,2,1,0:T(8,128)(2,1)}), bf16[8,2,128,128]{3,2,1,0:T(8,128)(2,1)S(1)}, u32[]{:S(2)}, u32[]{:S(2)}) async-start(bf16[8,2,128,128]{3,2,1,0:T(8,128)(2,1)} %pad_maximum_fusion.1), calls=%async_computation.1 | async-start | bytes 1048576 | tf_op jit(solution)/shard_map/all_to_all | solution.py:121
  7.9 0.0 copy-done.8
  7.9 0.4 copy.10
  8.3 0.0 copy-done.9
  8.3 0.4 copy.11
  8.7 1.5 %pad_maximum_fusion = bf16[8,2,4,128,128]{4,3,2,1,0:T(8,128)(2,1)} fusion(bf16[8,1,4,128,128]{4,3,2,1,0:T(8,128)(2,1)S(1)} %bitcast.30, bf16[8,1,4,128,128]{4,3,2,1,0:T(8,128)(2,1)S(1)} %bitcast.29), kind=kLoop, calls=%fused_computation | loop fusion | flops 1048576 | bytes 4194304 | tf_op jit(solution)/shard_map/stack | solution.py:140
  10.2 7.4 %all-to-all-done.1.own_ref = bf16[8,2,128,128]{3,2,1,0:T(8,128)(2,1)S(1)} async-done(((bf16[8,2,128,128]{3,2,1,0:T(8,128)(2,1)}), bf16[8,2,128,128]{3,2,1,0:T(8,128)(2,1)S(1)}, u32[]{:S(2)}, u32[]{:S(2)}) %all-to-all-start.1) | async-done | bytes 524320 | tf_op jit(solution)/shard_map/all_to_all | solution.py:121
  17.6 3.6 %all-to-all-start = ((bf16[8,2,4,128,128]{4,3,2,1,0:T(8,128)(2,1)}), bf16[8,2,4,128,128]{4,3,2,1,0:T(8,128)(2,1)S(1)}, u32[]{:S(2)}, u32[]{:S(2)}) async-start(bf16[8,2,4,128,128]{4,3,2,1,0:T(8,128)(2,1)} %pad_maximum_fusion), calls=%async_computation | async-start | bytes 4194304 | tf_op jit(solution)/shard_map/all_to_all | solution.py:121
  21.2 3.5 %collective-permute-start = (bf16[8,2,128,128]{3,2,1,0:T(8,128)(2,1)S(1)}, bf16[8,2,128,128]{3,2,1,0:T(8,128)(2,1)S(1)}, u32[]{:S(2)}, u32[]{:S(2)}) collective-permute-start(bf16[8,2,128,128]{3,2,1,0:T(8,128)(2,1)S(1)} %all-to-all-done.1.own_ref), channel_id=1, source_target_pairs={{0,1},{1,2},{2,3},{4,5},{5,6},{6,7},{8,9},{9,10},{10,11},{12,13},{... | collective-permute-start | bytes 1572872 | tf_op jit(solution)/shard_map/ppermute | solution.py:117
  24.8 0.0 copy-done
  24.8 0.1 copy.14.keys_ref
  24.9 11.5 %collective-permute-done.prev_ref = bf16[8,2,128,128]{3,2,1,0:T(8,128)(2,1)S(1)} collective-permute-done((bf16[8,2,128,128]{3,2,1,0:T(8,128)(2,1)S(1)}, bf16[8,2,128,128]{3,2,1,0:T(8,128)(2,1)S(1)}, u32[]{:S(2)}, u32[]{:S(2)}) %collective-permute-start) | collective-permute-done | bytes 524320 | tf_op jit(solution)/shard_map/ppermute | solution.py:117
  36.5 0.8 copy-done.2
  37.2 10.6 %all-to-all-done.qd_ref = bf16[8,2,4,128,128]{4,3,2,1,0:T(8,128)(2,1)S(1)} async-done(((bf16[8,2,4,128,128]{4,3,2,1,0:T(8,128)(2,1)}), bf16[8,2,4,128,128]{4,3,2,1,0:T(8,128)(2,1)S(1)}, u32[]{:S(2)}, u32[]{:S(2)}) %all-to-all-start) | async-done | bytes 2097184 | tf_op jit(solution)/shard_map/all_to_all | solution.py:121
  47.8 1.0 %copy-done.1 = bf16[8,2,128,128]{3,2,1,0:T(8,128)(2,1)S(1)} copy-done((bf16[8,2,128,128]{3,2,1,0:T(8,128)(2,1)S(1)}, bf16[8,2,128,128]{3,2,1,0:T(8,128)(2,1)}, u32[]{:S(2)}) %copy-start.1) | copy-done | bytes 524312
  48.9 1.0 %copy-done.3 = bf16[8,2,128,128]{3,2,1,0:T(8,128)(2,1)S(1)} copy-done((bf16[8,2,128,128]{3,2,1,0:T(8,128)(2,1)S(1)}, bf16[8,2,128,128]{3,2,1,0:T(8,128)(2,1)}, u32[]{:S(2)}) %copy-start.3) | copy-done | bytes 524312
  49.9 11.5 %shard_map.94 = (bf16[8,4,128,128]{3,2,1,0:T(8,128)(2,1)}, f32[8,2,128,128]{3,2,1,0:T(8,128)S(1)}, bf16[8,2,128,128]{3,2,1,0:T(8,128)(2,1)S(1)}) custom-call(s32[1]{0:T(128)} %bitcast.slab_ref, s32[32,5]{1,0:T(8,128)S(1)} %copy.14.keys_ref, bf16[8,2,4,128,128]{4,3,2,1,0:T(8,128)(2,1)S(1)} %all-to-all-done.qd_ref, bf16[8,2,128,128]{3,2,1,0:T(8,128)(2,1)S(1)} %copy-done.1, ...), custom_call_target="tpu_custom_call" | custom-call | flops 3355443200 | bytes 8388608 | tf_op jit(solution)/shard_map/pallas_call | solution.py:93
  61.4 0.8 copy-done.4
  62.2 3.7 %all-to-all-start.2 = ((bf16[8,4,128,128]{3,2,1,0:T(8,128)(2,1)}), bf16[8,4,128,128]{3,2,1,0:T(8,128)(2,1)S(1)}, u32[]{:S(2)}, u32[]{:S(2)}) async-start(bf16[8,4,128,128]{3,2,1,0:T(8,128)(2,1)} %get-tuple-element.6), calls=%async_computation.2 | async-start | bytes 2097152 | tf_op jit(solution)/shard_map/all_to_all | solution.py:121
  65.9 1.3 %collective-permute-start.1 = (bf16[8,2,128,128]{3,2,1,0:T(8,128)(2,1)S(1)}, bf16[8,2,128,128]{3,2,1,0:T(8,128)(2,1)S(1)}, u32[]{:S(2)}, u32[]{:S(2)}) collective-permute-start(bf16[8,2,128,128]{3,2,1,0:T(8,128)(2,1)S(1)} %copy-done.5), channel_id=1, source_target_pairs={{1,0},{2,1},{3,2},{5,4},{6,5},{7,6},{9,8},{10,9},{11,10},{13,12},{... | collective-permute-start | bytes 1572872 | tf_op jit(solution)/shard_map/ppermute | solution.py:117
  67.2 14.8 %collective-permute-done.1 = bf16[8,2,128,128]{3,2,1,0:T(8,128)(2,1)S(1)} collective-permute-done((bf16[8,2,128,128]{3,2,1,0:T(8,128)(2,1)S(1)}, bf16[8,2,128,128]{3,2,1,0:T(8,128)(2,1)S(1)}, u32[]{:S(2)}, u32[]{:S(2)}) %collective-permute-start.1) | collective-permute-done | bytes 524320 | tf_op jit(solution)/shard_map/ppermute | solution.py:117
  82.0 0.9 add_convert_fusion
  83.0 0.0 all-to-all-done.2
  83.0 3.9 %all-to-all-start.3 = ((bf16[8,2,128,128]{3,2,1,0:T(8,128)(2,1)}), bf16[8,2,128,128]{3,2,1,0:T(8,128)(2,1)S(1)}, u32[]{:S(2)}, u32[]{:S(2)}) async-start(bf16[8,2,128,128]{3,2,1,0:T(8,128)(2,1)} %add_convert_fusion), calls=%async_computation.3 | async-start | bytes 1048576 | tf_op jit(solution)/shard_map/all_to_all | solution.py:121
  86.8 1.6 %copy.21 = bf16[32,128,128]{2,0,1:T(8,128)(2,1)} copy(bf16[32,128,128]{2,1,0:T(8,128)(2,1)S(1)} %bitcast.28) | data formatting | bytes 2097152 | tf_op jit(solution)/shard_map/reshape | solution.py:144
  88.5 8.1 %all-to-all-done.3 = bf16[8,2,128,128]{3,2,1,0:T(8,128)(2,1)S(1)} async-done(((bf16[8,2,128,128]{3,2,1,0:T(8,128)(2,1)}), bf16[8,2,128,128]{3,2,1,0:T(8,128)(2,1)S(1)}, u32[]{:S(2)}, u32[]{:S(2)}) %all-to-all-start.3) | async-done | bytes 524320 | tf_op jit(solution)/shard_map/all_to_all | solution.py:121
  96.6 0.9 copy.17
  97.5 0.9 copy.16
  (14 shorter events, 0.1 us)
Async XLA Ops:
  0.6 7.3 %copy-start.8 = (bf16[128,32,128]{2,1,0:T(8,128)(2,1)S(1)}, bf16[128,32,128]{2,1,0:T(8,128)(2,1)}, u32[]{:S(2)}) copy-start(bf16[128,32,128]{2,1,0:T(8,128)(2,1)} %param.7) | copy-start | bytes 3145732
  1.9 6.4 %copy-start.9 = (bf16[128,32,128]{2,1,0:T(8,128)(2,1)S(1)}, bf16[128,32,128]{2,1,0:T(8,128)(2,1)}, u32[]{:S(2)}) copy-start(bf16[128,32,128]{2,1,0:T(8,128)(2,1)} %param.10) | copy-start | bytes 3145732
  2.7 14.9 %all-to-all-start.1 = ((bf16[8,2,128,128]{3,2,1,0:T(8,128)(2,1)}), bf16[8,2,128,128]{3,2,1,0:T(8,128)(2,1)S(1)}, u32[]{:S(2)}, u32[]{:S(2)}) async-start(bf16[8,2,128,128]{3,2,1,0:T(8,128)(2,1)} %pad_maximum_fusion.1), calls=%async_computation.1 | async-start | bytes 1048576 | tf_op jit(solution)/shard_map/all_to_all | solution.py:121
  10.2 14.6 %copy-start.10 = (s32[32,5]{0,1:T(8,128)S(1)}, s32[32,5]{0,1:T(8,128)}, u32[]{:S(2)}) copy-start(s32[32,5]{0,1:T(8,128)} %param.13) | copy-start | bytes 1924
  10.2 37.6 %copy-start.6 = (f32[4,4096]{1,0:T(4,128)S(1)}, f32[4,4096]{1,0:T(4,128)}, u32[]{:S(2)}) copy-start(f32[4,4096]{1,0:T(4,128)} %lse_ref.1) | copy-start | bytes 196612
  10.2 37.6 %copy-start.7 = (f32[4,4096]{1,0:T(4,128)S(1)}, f32[4,4096]{1,0:T(4,128)}, u32[]{:S(2)}) copy-start(f32[4,4096]{1,0:T(4,128)} %delta_ref.1) | copy-start | bytes 196612
  17.6 7.2 %copy-start = (bf16[8,2,128,128]{3,2,1,0:T(8,128)(2,1)}, bf16[8,2,128,128]{3,2,1,0:T(8,128)(2,1)S(1)}, u32[]{:S(2)}) copy-start(bf16[8,2,128,128]{3,2,1,0:T(8,128)(2,1)S(1)} %all-to-all-done.1.own_ref) | copy-start | bytes 1572868
  17.6 30.2 %all-to-all-start = ((bf16[8,2,4,128,128]{4,3,2,1,0:T(8,128)(2,1)}), bf16[8,2,4,128,128]{4,3,2,1,0:T(8,128)(2,1)S(1)}, u32[]{:S(2)}, u32[]{:S(2)}) async-start(bf16[8,2,4,128,128]{4,3,2,1,0:T(8,128)(2,1)} %pad_maximum_fusion), calls=%async_computation | async-start | bytes 4194304 | tf_op jit(solution)/shard_map/all_to_all | solution.py:121
  21.2 15.2 %collective-permute-start = (bf16[8,2,128,128]{3,2,1,0:T(8,128)(2,1)S(1)}, bf16[8,2,128,128]{3,2,1,0:T(8,128)(2,1)S(1)}, u32[]{:S(2)}, u32[]{:S(2)}) collective-permute-start(bf16[8,2,128,128]{3,2,1,0:T(8,128)(2,1)S(1)} %all-to-all-done.1.own_ref), channel_id=1, source_target_pairs={{0,1},{1,2},{2,3},{4,5},{5,6},{6,7},{8,9},{9,10},{10,11},{12,13},{... | collective-permute-start | bytes 1572872 | tf_op jit(solution)/shard_map/ppermute | solution.py:117
  36.4 0.8 copy-start.2
  47.8 1.0 %copy-start.1 = (bf16[8,2,128,128]{3,2,1,0:T(8,128)(2,1)S(1)}, bf16[8,2,128,128]{3,2,1,0:T(8,128)(2,1)}, u32[]{:S(2)}) copy-start(bf16[8,2,128,128]{3,2,1,0:T(8,128)(2,1)} %copy-done) | copy-start | bytes 1572868
  48.9 1.0 %copy-start.3 = (bf16[8,2,128,128]{3,2,1,0:T(8,128)(2,1)S(1)}, bf16[8,2,128,128]{3,2,1,0:T(8,128)(2,1)}, u32[]{:S(2)}) copy-start(bf16[8,2,128,128]{3,2,1,0:T(8,128)(2,1)} %copy-done.2) | copy-start | bytes 1572868
  61.4 0.8 copy-start.4
  62.2 3.7 %copy-start.5 = (bf16[8,2,128,128]{3,2,1,0:T(8,128)(2,1)S(1)}, bf16[8,2,128,128]{3,2,1,0:T(8,128)(2,1)}, u32[]{:S(2)}) copy-start(bf16[8,2,128,128]{3,2,1,0:T(8,128)(2,1)} %copy-done.4) | copy-start | bytes 1572868
  62.2 20.8 %all-to-all-start.2 = ((bf16[8,4,128,128]{3,2,1,0:T(8,128)(2,1)}), bf16[8,4,128,128]{3,2,1,0:T(8,128)(2,1)S(1)}, u32[]{:S(2)}, u32[]{:S(2)}) async-start(bf16[8,4,128,128]{3,2,1,0:T(8,128)(2,1)} %get-tuple-element.6), calls=%async_computation.2 | async-start | bytes 2097152 | tf_op jit(solution)/shard_map/all_to_all | solution.py:121
  65.9 16.1 %collective-permute-start.1 = (bf16[8,2,128,128]{3,2,1,0:T(8,128)(2,1)S(1)}, bf16[8,2,128,128]{3,2,1,0:T(8,128)(2,1)S(1)}, u32[]{:S(2)}, u32[]{:S(2)}) collective-permute-start(bf16[8,2,128,128]{3,2,1,0:T(8,128)(2,1)S(1)} %copy-done.5), channel_id=1, source_target_pairs={{1,0},{2,1},{3,2},{5,4},{6,5},{7,6},{9,8},{10,9},{11,10},{13,12},{... | collective-permute-start | bytes 1572872 | tf_op jit(solution)/shard_map/ppermute | solution.py:117
  83.0 13.6 %all-to-all-start.3 = ((bf16[8,2,128,128]{3,2,1,0:T(8,128)(2,1)}), bf16[8,2,128,128]{3,2,1,0:T(8,128)(2,1)S(1)}, u32[]{:S(2)}, u32[]{:S(2)}) async-start(bf16[8,2,128,128]{3,2,1,0:T(8,128)(2,1)} %add_convert_fusion), calls=%async_computation.3 | async-start | bytes 1048576 | tf_op jit(solution)/shard_map/all_to_all | solution.py:121

commit v2 on v1

v2 whole, which is shorter than its diff:
```python
import functools
import math

import jax
import jax.numpy as jnp
from jax import lax
from jax.experimental import pallas as pl
from jax.experimental.pallas import tpu as pltpu
from jax.sharding import PartitionSpec as P

BLOCK = 128
LOG2E = 1.4426950408889634
LANDED_FLOPS = 2 * 10**9


def contract(a, b, a_dim, b_dim):
    return lax.dot_general(a, b, (((a_dim,), (b_dim,)), ((), ())), preferred_element_type=jnp.float32)


def block_kernel(places_of, operand_count, first_call, last_call, slab_ref, me_ref, keys_ref, own_ref, prev_ref, lse_ref, delta_ref, *refs):
    qd_refs, refs = refs[:operand_count], refs[operand_count:]
    if not first_call:
        acc_in, refs = refs[0], refs[1:]
    dq_refs, refs = refs[: len(places_of)], refs[len(places_of) :]
    if last_call:
        own_out, prev_out, kv, kt, acc, cat_k, cat_v, cat_t = refs
    else:
        acc, kv, kt, cat_k, cat_v, cat_t = refs
    slab_blocks = own_ref.shape[0]
    heads = dq_refs[0].shape[1]
    select = keys_ref.shape[1]
    rows = heads * BLOCK
    head_dim = own_ref.shape[3]
    scale = 1.0 / math.sqrt(head_dim)
    first = slab_ref[0] * slab_blocks
    me = me_ref[0]

    def stage(c, _):
        for half, ref in ((0, prev_ref), (1, own_ref)):
            at = half * slab_blocks + c
            kv[0, at] = ref[c, 0]
            kv[1, at] = ref[c, 1]
            kt[at] = ref[c, 0].T
        return _

    lax.fori_loop(0, slab_blocks, stage, 0)
    acc[...] = jnp.zeros_like(acc) if first_call else acc_in[...]
    key_pos = lax.broadcasted_iota(jnp.int32, (BLOCK, rows), 0)
    query_pos = lax.broadcasted_iota(jnp.int32, (BLOCK, rows), 1) % BLOCK
    causal = key_pos <= query_pos

    def query_block(m, q_place, do_place, dq_ref, i, _):
        b = me ^ (2 * m + i)
        q, do = (qd_refs[x][i, at : at + heads].reshape(rows, head_dim) for x, at in (q_place, do_place))
        entries = [keys_ref[first + b, j] for j in range(select)]
        places = []
        for e in entries:
            local = e - first
            slot = jnp.where(local >= 0, slab_blocks + (local ^ me), (local + slab_blocks) ^ me)
            places.append(jnp.where(e >= 0, slot, 0))
        for j in range(select):
            cat_k[pl.ds(j * BLOCK, BLOCK)] = kv[0, places[j]]
            cat_v[pl.ds(j * BLOCK, BLOCK)] = kv[1, places[j]]
            cat_t[:, pl.ds(j * BLOCK, BLOCK)] = kt[places[j]]
        lanes = pl.ds(pl.multiple_of((first + b) * BLOCK, BLOCK), BLOCK)
        lse = jnp.concatenate([lse_ref[pl.ds(h, 1), lanes] for h in range(heads)], 1) * LOG2E
        delta = jnp.concatenate([delta_ref[pl.ds(h, 1), lanes] for h in range(heads)], 1)
        s = contract(cat_k[...], q, 1, 1)
        dp = contract(cat_v[...], do, 1, 1)
        p_parts = []
        for j in range(select):
            p = jnp.exp2(s[j * BLOCK : (j + 1) * BLOCK] * (scale * LOG2E) - lse)
            allowed = causal if j == 0 else entries[j] >= 0
            p_parts.append(jnp.where(allowed, p, 0.0))
        p = jnp.concatenate(p_parts, 0)
        ds = (p * (dp - delta)).astype(jnp.bfloat16)
        dv = contract(p.astype(jnp.bfloat16), do, 1, 0)
        dk = contract(ds, q, 1, 0)
        dqt = contract(cat_t[...], ds, 1, 0) * scale
        dq_ref[i] = dqt.T.astype(jnp.bfloat16).reshape(heads, BLOCK, head_dim)
        for j in range(select):
            part = slice(j * BLOCK, (j + 1) * BLOCK)
            acc[places[j], 0] += dk[part]
            acc[places[j], 1] += dv[part]
        return _

    for (m, q_place, do_place), dq_ref in zip(places_of, dq_refs):
        lax.fori_loop(0, 2, functools.partial(query_block, m, q_place, do_place, dq_ref), 0)

    if last_call:

        def finish(c, _):
            prev_out[c, 0] = (acc[c, 0] * scale).astype(prev_out.dtype)
            prev_out[c, 1] = acc[c, 1].astype(prev_out.dtype)
            own_out[c, 0] = acc[slab_blocks + c, 0] * scale
            own_out[c, 1] = acc[slab_blocks + c, 1]
            return _

        lax.fori_loop(0, slab_blocks, finish, 0)


def block_grads(parts, slab, me, block_keys, own, prev, lse, delta, acc, last_call):
    slab_blocks, _, _, head_dim = own.shape
    heads = lse.shape[0]
    select = block_keys.shape[1]
    smem = pl.BlockSpec(memory_space=pltpu.SMEM)
    vmem = pl.BlockSpec(memory_space=pltpu.VMEM)
    acc_shape = (2 * slab_blocks, 2, BLOCK, head_dim)
    wide = select * BLOCK
    macs = 2 * len(parts) * heads * select * 5 * BLOCK * BLOCK * head_dim
    arrays, places_of = [], []
    for m, *pair in parts:
        places = []
        for array, at in pair:
            if not any(array is x for x in arrays):
                arrays.append(array)
            places.append(([array is x for x in arrays].index(True), at))
        places_of.append((m, *places))
    operands = [own, prev, lse, delta, *arrays] + ([] if acc is None else [acc])
    out_shape = [jax.ShapeDtypeStruct((2, heads, BLOCK, head_dim), jnp.bfloat16) for _ in parts]
    scratch = [
        pltpu.VMEM((2, 2 * slab_blocks, BLOCK, head_dim), jnp.bfloat16),
        pltpu.VMEM((2 * slab_blocks, head_dim, BLOCK), jnp.bfloat16),
    ]
    if last_call:
        out_shape.append(jax.ShapeDtypeStruct(own.shape, jnp.float32))
        out_shape.append(jax.ShapeDtypeStruct(own.shape, jnp.bfloat16))
        scratch.append(pltpu.VMEM(acc_shape, jnp.float32))
    else:
        out_shape.append(jax.ShapeDtypeStruct(acc_shape, jnp.float32))
    return pl.pallas_call(
        functools.partial(block_kernel, places_of, len(arrays), acc is None, last_call),
        in_specs=[smem] * 3 + [vmem] * len(operands),
        out_specs=[vmem] * len(out_shape),
        out_shape=out_shape,
        scratch_shapes=scratch
        + [
            pltpu.VMEM((wide, head_dim), jnp.bfloat16),
            pltpu.VMEM((wide, head_dim), jnp.bfloat16),
            pltpu.VMEM((head_dim, wide), jnp.bfloat16),
        ],
        compiler_params=pltpu.CompilerParams(vmem_limit_bytes=40 * 1024 * 1024 if slab_blocks > 8 else 20 * 1024 * 1024),
        cost_estimate=pl.CostEstimate(flops=2 * macs, bytes_accessed=8 * 1024 * 1024, transcendentals=0),
    )(slab, me, block_keys, *operands)


def pack_kernel(fold_counts, me_ref, *refs):
    count = len(fold_counts)
    chips = refs[-1 - 2 * count - 1].shape[0]
    sources, pieces, give, refs = refs[:count], refs[count : count + chips], refs[count + chips], refs[count + chips + 1 :]
    by_token, by_head, sems = refs[:count], refs[count : 2 * count], refs[-1]
    devices = 2 * chips
    me = me_ref[0]
    copies = [pltpu.make_async_copy(sources[i], by_token[i], sems.at[i]) for i in range(count)]
    for copy in copies:
        copy.start()
    at = 0
    for copy, source, target, fold_count in zip(copies, by_token, by_head, fold_counts):
        copy.wait()
        target[...] = jnp.swapaxes(source[...], 0, 1)
        heads = target.shape[0] * fold_count // devices
        for m in range(chips):
            for out, j in ((pieces[m].at[0], 0), (give.at[m], 1)):
                device = me ^ (2 * m + j)
                out[at : at + heads] = target[pl.ds(device // fold_count * heads, heads)]
        at += heads


def packed(me, arrays, fold_counts, uly_count):
    tokens, _, head_dim = arrays[0].shape
    chips = uly_count // 2
    tiles = sum(x.shape[1] * fold_count for x, fold_count in zip(arrays, fold_counts)) // uly_count
    vmem = pl.BlockSpec(memory_space=pltpu.VMEM)
    shapes = [jax.ShapeDtypeStruct((2, tiles, tokens, head_dim), arrays[0].dtype)] * chips
    shapes.append(jax.ShapeDtypeStruct((chips, tiles, tokens, head_dim), arrays[0].dtype))
    *pieces, give = pl.pallas_call(
        functools.partial(pack_kernel, fold_counts),
        in_specs=[pl.BlockSpec(memory_space=pltpu.SMEM)] + [pl.BlockSpec(memory_space=pltpu.HBM)] * len(arrays),
        out_specs=[vmem] * len(shapes),
        out_shape=shapes,
        scratch_shapes=[pltpu.VMEM(x.shape, x.dtype) for x in arrays]
        + [pltpu.VMEM((x.shape[1], tokens, head_dim), x.dtype) for x in arrays]
        + [pltpu.SemaphoreType.DMA((len(arrays),))],
        compiler_params=pltpu.CompilerParams(vmem_limit_bytes=8 * 1024 * 1024),
    )(me, *[pltpu.with_memory_space_constraint(x, pltpu.HBM) for x in arrays])
    return pieces, give


def merge_kernel(chips, *refs):
    got, outs = refs[chips], refs[-chips:]
    for m in range(chips):
        outs[m][1] = got[m]


def merged(pieces, got, after):
    chips = len(pieces)
    vmem = pl.BlockSpec(memory_space=pltpu.VMEM)
    return pl.pallas_call(
        functools.partial(merge_kernel, chips),
        in_specs=[vmem] * (chips + 1) + [pl.BlockSpec(memory_space=pl.ANY)] * len(after),
        out_specs=[vmem] * chips,
        out_shape=[jax.ShapeDtypeStruct(x.shape, x.dtype) for x in pieces],
        input_output_aliases={m: m for m in range(chips)},
        compiler_params=pltpu.CompilerParams(vmem_limit_bytes=8 * 1024 * 1024),
    )(*pieces, got, *after)


def landed_kernel(piece, out):
    pass


def landed(piece):
    hold = pl.BlockSpec(memory_space=pl.ANY)
    return pl.pallas_call(
        landed_kernel,
        in_specs=[hold],
        out_specs=hold,
        out_shape=jax.ShapeDtypeStruct(piece.shape, piece.dtype),
        input_output_aliases={0: 0},
        cost_estimate=pl.CostEstimate(flops=LANDED_FLOPS, bytes_accessed=2**20, transcendentals=0),
    )(piece)


def join_kernel(*refs):
    *pieces, out = refs
    for m, piece in enumerate(pieces):
        out[2 * m : 2 * m + 2] = piece[...]


def joined(pieces):
    vmem = pl.BlockSpec(memory_space=pltpu.VMEM)
    return pl.pallas_call(
        join_kernel,
        in_specs=[vmem] * len(pieces),
        out_specs=vmem,
        out_shape=jax.ShapeDtypeStruct((2 * len(pieces), *pieces[0].shape[1:]), pieces[0].dtype),
        compiler_params=pltpu.CompilerParams(vmem_limit_bytes=16 * 1024 * 1024),
        cost_estimate=pl.CostEstimate(flops=2**20, bytes_accessed=2**20, transcendentals=0),
    )(*pieces)


def unpack_kernel(chips, fold_count, me_ref, *refs):
    here, (got, *refs) = refs[:chips], refs[chips:]
    count = (len(refs) - 1) // 3
    outs, by_head, by_token, sems = refs[:count], refs[count : 2 * count], refs[2 * count : 3 * count], refs[-1]
    me = me_ref[0]
    for k in range(2 * chips):
        device = me ^ k
        part = here[k // 2][0] if k % 2 == 0 else got[k // 2]
        heads = part.shape[0] // count
        for i in range(count):
            by_head[i][pl.ds(device * heads, heads)] = part[i * heads : (i + 1) * heads]
    copies = [pltpu.make_async_copy(by_token[i], outs[i], sems.at[i]) for i in range(count)]
    for i in range(count):
        whole = by_head[i][...]
        if fold_count > 1:
            whole = whole.reshape(-1, fold_count, *whole.shape[1:]).astype(jnp.float32).sum(1).astype(whole.dtype)
        by_token[i][...] = jnp.swapaxes(whole, 0, 1)
        copies[i].start()
    for copy in copies:
        copy.wait()


def unpacked(me, here, got, count, fold_count):
    chips, tiles, tokens, head_dim = got.shape
    devices = 2 * chips
    vmem = pl.BlockSpec(memory_space=pltpu.VMEM)
    heads = devices * tiles // count
    shape = (tokens, heads // fold_count, head_dim)
    return pl.pallas_call(
        functools.partial(unpack_kernel, chips, fold_count),
        in_specs=[pl.BlockSpec(memory_space=pltpu.SMEM)] + [vmem] * (chips + 1),
        out_specs=[pl.BlockSpec(memory_space=pltpu.HBM)] * count,
        out_shape=[jax.ShapeDtypeStruct(shape, got.dtype)] * count,
        scratch_shapes=[pltpu.VMEM((heads, tokens, head_dim), got.dtype)] * count
        + [pltpu.VMEM(shape, got.dtype)] * count
        + [pltpu.SemaphoreType.DMA((count,))],
        compiler_params=pltpu.CompilerParams(vmem_limit_bytes=16 * 1024 * 1024),
    )(me, *here, got)


def passed_along(block, axis, distance):
    devices = range(lax.axis_size(axis))
    return lax.ppermute(block, axis, [(i - distance, i) for i in devices if i - distance in devices])


def swapped(block, k):
    if k == 0:
        return block
    return lax.ppermute(block, "uly", [(i, i ^ k) for i in range(lax.axis_size("uly"))])


def sent_to_tokens(chunks, me, count, fold_count):
    here = [swapped(chunk, 2 * m) for m, chunk in enumerate(chunks)]
    got = swapped(jnp.stack([chunk[1] for chunk in here]), 1)
    return unpacked(me, here, got, count, fold_count)


def shards(queries, keys, values, grad_out, lse, delta, block_keys):
    uly_count = lax.axis_size("uly")
    head_total = queries.shape[1]
    fold_count = uly_count // keys.shape[1]
    heads = head_total // uly_count
    chips = uly_count // 2
    far = chips - 1
    me = lax.axis_index("uly").reshape(1)
    slab = lax.axis_index("blk").reshape(1)

    kv_pieces, give_kv = packed(me, [keys, values], [fold_count] * 2, uly_count)
    qd_pieces, give_qd = packed(me, [queries, grad_out], [1] * 2, uly_count)
    got_kv, got_qd = swapped(give_kv, 1), swapped(give_qd, 1)
    kv_pieces = [swapped(piece, 2 * m) for m, piece in enumerate(merged(kv_pieces, got_kv, []))]
    own = joined(kv_pieces)
    qd_pieces = [swapped(piece, 2 * m) for m, piece in enumerate(merged(qd_pieces, got_qd, kv_pieces[1:]))]
    qd_pieces[far] = landed(qd_pieces[far])
    prev = passed_along(own, "blk", 1)
    parts = [(m, (piece, 0), (piece, heads)) for m, piece in enumerate(qd_pieces)]

    grads = functools.partial(
        block_grads, slab=slab, me=me, block_keys=block_keys, own=own, prev=prev, lse=lse, delta=delta
    )
    order = [0] + list(range(far, 0, -1))
    early, late = order[: chips // 2], order[chips // 2 :]
    *dq_early, acc = grads([parts[m] for m in early], acc=None, last_call=False)
    *dq_late, own_grad, prev_grad = grads([parts[m] for m in late], acc=acc, last_call=True)
    back = passed_along(prev_grad, "blk", -1)
    kv_grad = (own_grad + back.astype(jnp.float32)).astype(jnp.bfloat16)
    kv_grad = [kv_grad[2 * m : 2 * m + 2] for m in range(chips)]
    dq = dict(zip(order, dq_early + dq_late))
    (grad_queries,) = sent_to_tokens([dq[m] for m in range(chips)], me, 1, 1)
    grad_keys, grad_values = sent_to_tokens(kv_grad, me, 2, fold_count)
    return grad_queries, grad_keys, grad_values


def solution(mesh):
    spread = P(("blk", "uly"), None, None)
    return jax.shard_map(
        shards,
        mesh=mesh,
        in_specs=(spread, spread, spread, spread, P("uly", None), P("uly", None), P()),
        out_specs=(spread, spread, spread),
        check_vma=False,
    )
```

time: 99 us -> 78.6 us (0.79)
  waiting for transfers between devices: 52.4 us -> 37.5 us
  local copies, waits for them, and re-layouts: 9.25 us -> 0.2 us
  Pallas kernels: 11.5 us -> 18.8 us
  other arithmetic: 3.29 us -> 0.25 us
    ppermute x0 -> x16, waiting for transfers between devices: none -> 37.5 us  [swapped(): lax.ppermute(block, 'uly', [(i, i ^ k) for i in range(lax.axis_size('uly'...]
    ppermute x2, waiting for transfers between devices: 26.4 us -> 0.01 us  [passed_along(): lax.ppermute(block, axis, [(i - distance, i) for i in devices if i - dist...]
    all_to_all x4 -> x0, waiting for transfers between devices: 26.1 us -> none  [exchange(): return lax.all_to_all(x, 'uly', split_axis=0, concat_axis=0, tiled=True)]
    all_to_all x4 -> x0, starting transfers between devices: 16.3 us -> none  [exchange(): return lax.all_to_all(x, 'uly', split_axis=0, concat_axis=0, tiled=True)]
    ppermute x0 -> x16, starting transfers between devices: none -> 15.9 us  [swapped(): lax.ppermute(block, 'uly', [(i, i ^ k) for i in range(lax.axis_size('uly'...]
    pallas_call x1 -> x10, Pallas kernels: 11.5 us -> 18.8 us  [the longest x2 12.8 us: block_grads(): pl.pallas_call(functools.partial(block_kernel, places_of, len(arrays), ac...]
    unnamed x27 -> x7, local copies, waits for them, and re-layouts: 6.35 us -> 0.1 us
    another operation x2, other arithmetic: 2.35 us -> 0.11 us  [sent_to_tokens(): got = swapped(jnp.stack([chunk[1] for chunk in here]), 1)]
  transfers between devices with their start and end apart: 6 -> 18, of which waited for: 5 -> 10; matrix products, arithmetic and copies ran while one was open for 5% -> 1% of each run, Pallas kernels for 0% -> 11%
where the time goes in v2:
time: 78.6 us; the launch traced here: 78.3 us
  waiting for transfers between devices  37.5 us (48%)
  starting transfers between devices  20.7 us (26%)
  Pallas kernels  18.8 us (24%)
  between operations  0.83 us (1%)
    ppermute x16, waiting for transfers between devices, swapped(): lax.ppermute(block, 'uly', [(i, i ^ k) for i in range(lax.axis_size('uly'...  37.5 us
    ppermute x16, starting transfers between devices, swapped(): lax.ppermute(block, 'uly', [(i, i ^ k) for i in range(lax.axis_size('uly'...  15.9 us
    pallas_call x2, Pallas kernels, block_grads(): pl.pallas_call(functools.partial(block_kernel, places_of, len(arrays), ac...  12.8 us
    ppermute x2, starting transfers between devices, passed_along(): lax.ppermute(block, axis, [(i - distance, i) for i in devices if i - dist...  4.81 us
    pallas_call x2, Pallas kernels, packed(): pl.pallas_call(functools.partial(pack_kernel, fold_counts), in_specs=[pl....  3.55 us
    pallas_call x2, Pallas kernels, unpacked(): pl.pallas_call(functools.partial(unpack_kernel, chips, fold_count), in_sp...  2.38 us
  transfers between devices with their start and end apart: 18, of which 10 were waited for; matrix products, arithmetic and copies ran while one was open for 1% of the time, Pallas kernels for 11%

profile of v2, /device:TPU:0, one launch (start us, length us, event | category | flops | bytes accessed | tf_op | source)
XLA Modules:
  0.0 78.3 jit_solution(17865947927961018728)
XLA Ops:
  0.6 2.4 %shard_map.97 = (bf16[2,8,128,128]{3,2,1,0:T(8,128)(2,1)S(1)}, bf16[2,8,128,128]{3,2,1,0:T(8,128)(2,1)S(1)}, bf16[2,8,128,128]{3,2,1,0:T(8,128)(2,1)S(1)}, bf16[...) custom-call(s32[1]{0:T(128)} %bitcast.me_ref, bf16[128,32,128]{2,1,0:T(8,128)(2,1)} %refs_0_.3, ...), custom_call_target="tpu_custom_call" | custom-call | tf_op jit(solution)/shard_map/pallas_call | solution.py:176
  3.0 0.5 collective-permute-start.5
  3.5 1.2 %shard_map.94 = (bf16[2,2,128,128]{3,2,1,0:T(8,128)(2,1)S(1)}, bf16[2,2,128,128]{3,2,1,0:T(8,128)(2,1)S(1)}, bf16[2,2,128,128]{3,2,1,0:T(8,128)(2,1)S(1)}, bf16[...) custom-call(s32[1]{0:T(128)} %bitcast.me_ref, bf16[128,8,128]{2,1,0:T(8,128)(2,1)} %refs_0_.2, ...), custom_call_target="tpu_custom_call" | custom-call | tf_op jit(solution)/shard_map/pallas_call | solution.py:176
  4.7 0.1 collective-permute-start
  4.8 1.5 %collective-permute-done.refs_4_ = bf16[4,2,128,128]{3,2,1,0:T(8,128)(2,1)S(1)} collective-permute-done((bf16[4,2,128,128]{3,2,1,0:T(8,128)(2,1)S(1)}, bf16[4,2,128,128]{3,2,1,0:T(8,128)(2,1)S(1)}, u32[]{:S(2)}, u32[]{:S(2)}) %collective-permute-start) | collective-permute-done | bytes 262176 | tf_op jit(solution)/shard_map/ppermute | solution.py:290
  6.3 2.8 %collective-permute-start.1 = (bf16[2,2,128,128]{3,2,1,0:T(8,128)(2,1)S(1)}, bf16[2,2,128,128]{3,2,1,0:T(8,128)(2,1)S(1)}, u32[]{:S(2)}, u32[]{:S(2)}) collective-permute-start(bf16[2,2,128,128]{3,2,1,0:T(8,128)(2,1)S(1)} %get-tuple-element.36), channel_id=1, source_target_pairs={{0,8},{4,12},{8,0},{12,4},{16,24},{20,28},{24,16},{28,20},{1,9},{5... | collective-permute-start | bytes 393224 | tf_op jit(solution)/shard_map/ppermute | solution.py:290
  9.1 1.5 %collective-permute-start.2 = (bf16[2,2,128,128]{3,2,1,0:T(8,128)(2,1)S(1)}, bf16[2,2,128,128]{3,2,1,0:T(8,128)(2,1)S(1)}, u32[]{:S(2)}, u32[]{:S(2)}) collective-permute-start(bf16[2,2,128,128]{3,2,1,0:T(8,128)(2,1)S(1)} %get-tuple-element.37), channel_id=1, source_target_pairs={{0,16},{4,20},{8,24},{12,28},{16,0},{20,4},{24,8},{28,12},{1,17},{... | collective-permute-start | bytes 393224 | tf_op jit(solution)/shard_map/ppermute | solution.py:290
  10.7 2.5 %collective-permute-done.1.refs_1_.refs_5_ = bf16[2,2,128,128]{3,2,1,0:T(8,128)(2,1)S(1)} collective-permute-done((bf16[2,2,128,128]{3,2,1,0:T(8,128)(2,1)S(1)}, bf16[2,2,128,128]{3,2,1,0:T(8,128)(2,1)S(1)}, u32[]{:S(2)}, u32[]{:S(2)}) %collective-permute-start.1) | collective-permute-done | bytes 131104 | tf_op jit(solution)/shard_map/ppermute | solution.py:290
  13.2 4.2 %collective-permute-done.2.refs_2_.refs_6_ = bf16[2,2,128,128]{3,2,1,0:T(8,128)(2,1)S(1)} collective-permute-done((bf16[2,2,128,128]{3,2,1,0:T(8,128)(2,1)S(1)}, bf16[2,2,128,128]{3,2,1,0:T(8,128)(2,1)S(1)}, u32[]{:S(2)}, u32[]{:S(2)}) %collective-permute-start.2) | collective-permute-done | bytes 131104 | tf_op jit(solution)/shard_map/ppermute | solution.py:290
  17.4 1.6 %collective-permute-start.6 = (bf16[2,8,128,128]{3,2,1,0:T(8,128)(2,1)S(1)}, bf16[2,8,128,128]{3,2,1,0:T(8,128)(2,1)}, u32[]{:S(2)}, u32[]{:S(2)}) collective-permute-start(bf16[2,8,128,128]{3,2,1,0:T(8,128)(2,1)S(1)} %get-tuple-element.45), channel_id=1, source_target_pairs={{0,24},{4,28},{8,16},{12,20},{16,8},{20,12},{24,0},{28,4},{1,25},{... | collective-permute-start | bytes 1572872 | tf_op jit(solution)/shard_map/ppermute | solution.py:290
  19.0 3.5 %collective-permute-start.4 = (bf16[8,2,128,128]{3,2,1,0:T(8,128)(2,1)S(1)}, bf16[8,2,128,128]{3,2,1,0:T(8,128)(2,1)S(1)}, u32[]{:S(2)}, u32[]{:S(2)}) collective-permute-start(bf16[8,2,128,128]{3,2,1,0:T(8,128)(2,1)S(1)} %shard_map.96.own_ref), channel_id=1, source_target_pairs={{0,1},{1,2},{2,3},{4,5},{5,6},{6,7},{8,9},{9,10},{10,11},{12,13},{... | collective-permute-start | bytes 1572872 | tf_op jit(solution)/shard_map/ppermute | solution.py:284
  22.5 1.3 %collective-permute-start.7 = (bf16[2,8,128,128]{3,2,1,0:T(8,128)(2,1)S(1)}, bf16[2,8,128,128]{3,2,1,0:T(8,128)(2,1)}, u32[]{:S(2)}, u32[]{:S(2)}) collective-permute-start(bf16[2,8,128,128]{3,2,1,0:T(8,128)(2,1)S(1)} %get-tuple-element.47), channel_id=1, source_target_pairs={{0,16},{4,20},{8,24},{12,28},{16,0},{20,4},{24,8},{28,12},{1,17},{... | collective-permute-start | bytes 1572872 | tf_op jit(solution)/shard_map/ppermute | solution.py:290
  23.8 0.8 %collective-permute-start.8 = (bf16[2,8,128,128]{3,2,1,0:T(8,128)(2,1)S(1)}, bf16[2,8,128,128]{3,2,1,0:T(8,128)(2,1)}, u32[]{:S(2)}, u32[]{:S(2)}) collective-permute-start(bf16[2,8,128,128]{3,2,1,0:T(8,128)(2,1)S(1)} %get-tuple-element.48), channel_id=1, source_target_pairs={{0,8},{4,12},{8,0},{12,4},{16,24},{20,28},{24,16},{28,20},{1,9},{5... | collective-permute-start | bytes 1572872 | tf_op jit(solution)/shard_map/ppermute | solution.py:290
  24.7 8.7 %collective-permute-done.6.piece = bf16[2,8,128,128]{3,2,1,0:T(8,128)(2,1)} collective-permute-done((bf16[2,8,128,128]{3,2,1,0:T(8,128)(2,1)S(1)}, bf16[2,8,128,128]{3,2,1,0:T(8,128)(2,1)}, u32[]{:S(2)}, u32[]{:S(2)}) %collective-permute-start.6) | collective-permute-done | bytes 524320 | tf_op jit(solution)/shard_map/ppermute | solution.py:290
  33.4 6.2 %shard_map.100 = (bf16[2,4,128,128]{3,2,1,0:T(8,128)(2,1)S(1)}, bf16[2,4,128,128]{3,2,1,0:T(8,128)(2,1)S(1)}, f32[16,2,128,128]{3,2,1,0:T(8,128)S(1)}) custom-call(s32[1]{0:T(128)} %bitcast.1.slab_ref, s32[1]{0:T(128)} %bitcast.me_ref, s32[32,5]{1,0:T(8,128)S(1)} %copy.19.keys_ref, bf16[8,2,128,128]{3,2,1,0:T(8,128)(2,1)S(1)} %shard_map.96.own_ref, ...), custom_call_target="tpu_custom_call" | custom-call | flops 1677721600 | bytes 8388608 | tf_op jit(solution)/shard_map/pallas_call | solution.py:131
  39.7 2.9 %collective-permute-done.7.refs_0_ = bf16[2,8,128,128]{3,2,1,0:T(8,128)(2,1)} collective-permute-done((bf16[2,8,128,128]{3,2,1,0:T(8,128)(2,1)S(1)}, bf16[2,8,128,128]{3,2,1,0:T(8,128)(2,1)}, u32[]{:S(2)}, u32[]{:S(2)}) %collective-permute-start.7) | collective-permute-done | bytes 524320 | tf_op jit(solution)/shard_map/ppermute | solution.py:290
  42.6 0.2 collective-permute-done.8.refs_1_
  42.8 6.5 %shard_map.101 = (bf16[2,4,128,128]{3,2,1,0:T(8,128)(2,1)S(1)}, bf16[2,4,128,128]{3,2,1,0:T(8,128)(2,1)S(1)}, f32[8,2,128,128]{3,2,1,0:T(8,128)S(1)}, bf16[8,2,128,128]{3,2,1,0:T(8,128)(2,1)S(1)}) custom-call(s32[1]{0:T(128)} %bitcast.1.slab_ref, s32[1]{0:T(128)} %bitcast.me_ref, s32[32,5]{1,0:T(8,128)S(1)} %copy.19.keys_ref, ...), custom_call_target="tpu_custom_call" | custom-call | flops 1677721600 | bytes 8388608 | tf_op jit(solution)/shard_map/pallas_call | solution.py:131
  49.3 1.3 %collective-permute-start.13 = (bf16[8,2,128,128]{3,2,1,0:T(8,128)(2,1)S(1)}, bf16[8,2,128,128]{3,2,1,0:T(8,128)(2,1)S(1)}, u32[]{:S(2)}, u32[]{:S(2)}) collective-permute-start(bf16[8,2,128,128]{3,2,1,0:T(8,128)(2,1)S(1)} %get-tuple-element.54), channel_id=1, source_target_pairs={{1,0},{2,1},{3,2},{5,4},{6,5},{7,6},{9,8},{10,9},{11,10},{13,12},{... | collective-permute-start | bytes 1572872 | tf_op jit(solution)/shard_map/ppermute | solution.py:284
  50.6 1.5 %collective-permute-start.9 = (bf16[2,4,128,128]{3,2,1,0:T(8,128)(2,1)S(1)}, bf16[2,4,128,128]{3,2,1,0:T(8,128)(2,1)S(1)}, u32[]{:S(2)}, u32[]{:S(2)}) collective-permute-start(bf16[2,4,128,128]{3,2,1,0:T(8,128)(2,1)S(1)} %get-tuple-element.50), channel_id=1, source_target_pairs={{0,8},{4,12},{8,0},{12,4},{16,24},{20,28},{24,16},{28,20},{1,9},{5... | collective-permute-start | bytes 786440 | tf_op jit(solution)/shard_map/ppermute | solution.py:290
  52.1 0.6 collective-permute-start.10
  52.7 1.5 %collective-permute-start.11 = (bf16[2,4,128,128]{3,2,1,0:T(8,128)(2,1)S(1)}, bf16[2,4,128,128]{3,2,1,0:T(8,128)(2,1)S(1)}, u32[]{:S(2)}, u32[]{:S(2)}) collective-permute-start(bf16[2,4,128,128]{3,2,1,0:T(8,128)(2,1)S(1)} %get-tuple-element.52), channel_id=1, source_target_pairs={{0,24},{4,28},{8,16},{12,20},{16,8},{20,12},{24,0},{28,4},{1,25},{... | collective-permute-start | bytes 786440 | tf_op jit(solution)/shard_map/ppermute | solution.py:290
  54.2 5.7 %collective-permute-done.9.refs_1_ = bf16[2,4,128,128]{3,2,1,0:T(8,128)(2,1)S(1)} collective-permute-done((bf16[2,4,128,128]{3,2,1,0:T(8,128)(2,1)S(1)}, bf16[2,4,128,128]{3,2,1,0:T(8,128)(2,1)S(1)}, u32[]{:S(2)}, u32[]{:S(2)}) %collective-permute-start.9) | collective-permute-done | bytes 262176 | tf_op jit(solution)/shard_map/ppermute | solution.py:290
  59.9 5.8 %collective-permute-done.10.refs_2_ = bf16[2,4,128,128]{3,2,1,0:T(8,128)(2,1)S(1)} collective-permute-done((bf16[2,4,128,128]{3,2,1,0:T(8,128)(2,1)S(1)}, bf16[2,4,128,128]{3,2,1,0:T(8,128)(2,1)S(1)}, u32[]{:S(2)}, u32[]{:S(2)}) %collective-permute-start.10) | collective-permute-done | bytes 262176 | tf_op jit(solution)/shard_map/ppermute | solution.py:290
  65.9 0.1 add_convert_fusion
  66.1 1.5 %collective-permute-start.16 = (bf16[2,2,128,128]{3,2,1,0:T(8,128)(2,1)S(1)}, bf16[2,2,128,128]{3,2,1,0:T(8,128)(2,1)S(1)}, u32[]{:S(2)}, u32[]{:S(2)}) collective-permute-start(bf16[2,2,128,128]{3,2,1,0:T(8,128)(2,1)S(1)} %get-tuple-element.57), channel_id=1, source_target_pairs={{0,24},{4,28},{8,16},{12,20},{16,8},{20,12},{24,0},{28,4},{1,25},{... | collective-permute-start | bytes 393224 | tf_op jit(solution)/shard_map/ppermute | solution.py:290
  67.6 0.6 collective-permute-start.15
  68.2 1.4 %collective-permute-start.14 = (bf16[2,2,128,128]{3,2,1,0:T(8,128)(2,1)S(1)}, bf16[2,2,128,128]{3,2,1,0:T(8,128)(2,1)S(1)}, u32[]{:S(2)}, u32[]{:S(2)}) collective-permute-start(bf16[2,2,128,128]{3,2,1,0:T(8,128)(2,1)S(1)} %get-tuple-element.59), channel_id=1, source_target_pairs={{0,8},{4,12},{8,0},{12,4},{16,24},{20,28},{24,16},{28,20},{1,9},{5... | collective-permute-start | bytes 393224 | tf_op jit(solution)/shard_map/ppermute | solution.py:290
  69.7 3.7 %collective-permute-done.16.refs_3_ = bf16[2,2,128,128]{3,2,1,0:T(8,128)(2,1)S(1)} collective-permute-done((bf16[2,2,128,128]{3,2,1,0:T(8,128)(2,1)S(1)}, bf16[2,2,128,128]{3,2,1,0:T(8,128)(2,1)S(1)}, u32[]{:S(2)}, u32[]{:S(2)}) %collective-permute-start.16) | collective-permute-done | bytes 131104 | tf_op jit(solution)/shard_map/ppermute | solution.py:290
  73.4 2.4 %collective-permute-done.15.refs_2_ = bf16[2,2,128,128]{3,2,1,0:T(8,128)(2,1)S(1)} collective-permute-done((bf16[2,2,128,128]{3,2,1,0:T(8,128)(2,1)S(1)}, bf16[2,2,128,128]{3,2,1,0:T(8,128)(2,1)S(1)}, u32[]{:S(2)}, u32[]{:S(2)}) %collective-permute-start.15) | collective-permute-done | bytes 131104 | tf_op jit(solution)/shard_map/ppermute | solution.py:290
  75.9 1.5 %shard_map.102 = bf16[128,32,128]{2,1,0:T(8,128)(2,1)} custom-call(s32[1]{0:T(128)} %bitcast.me_ref, bf16[2,4,128,128]{3,2,1,0:T(8,128)(2,1)S(1)} %get-tuple-element.46.refs_0_, bf16[2,4,128,128]{3,2,1,0:T(8,128)(2,1)S(1)} %collective-permute-done.9.refs_1_, bf16[2,4,128,128]{3,2,1,0:T(8,128)(2,1)S(1)} %collective-permute-done.10.refs_2_, ...), custom_call_target="tpu_custom_call" | custom-call | tf_op jit(solution)/shard_map/pallas_call | solution.py:270
  77.4 0.9 %shard_map.103 = (bf16[128,8,128]{2,1,0:T(8,128)(2,1)}, bf16[128,8,128]{2,1,0:T(8,128)(2,1)}) custom-call(s32[1]{0:T(128)} %bitcast.me_ref, bf16[2,2,128,128]{3,2,1,0:T(8,128)(2,1)S(1)} %get-tuple-element.60.refs_0_, bf16[2,2,128,128]{3,2,1,0:T(8,128)(2,1)S(1)} %collective-permute-done.14.refs_1_, ...), custom_call_target="tpu_custom_call" | custom-call | tf_op jit(solution)/shard_map/pallas_call | solution.py:270
  (33 shorter events, 0.7 us)
Async XLA Ops:
  3.0 14.3 %collective-permute-start.5 = (bf16[4,8,128,128]{3,2,1,0:T(8,128)(2,1)S(1)}, bf16[4,8,128,128]{3,2,1,0:T(8,128)(2,1)S(1)}, u32[]{:S(2)}, u32[]{:S(2)}) collective-permute-start(bf16[4,8,128,128]{3,2,1,0:T(8,128)(2,1)S(1)} %get-tuple-element.43), channel_id=1, source_target_pairs={{0,4},{4,0},{8,12},{12,8},{16,20},{20,16},{24,28},{28,24},{1,5},{5... | collective-permute-start | bytes 3145736 | tf_op jit(solution)/shard_map/ppermute | solution.py:290
  4.7 1.6 %collective-permute-start = (bf16[4,2,128,128]{3,2,1,0:T(8,128)(2,1)S(1)}, bf16[4,2,128,128]{3,2,1,0:T(8,128)(2,1)S(1)}, u32[]{:S(2)}, u32[]{:S(2)}) collective-permute-start(bf16[4,2,128,128]{3,2,1,0:T(8,128)(2,1)S(1)} %get-tuple-element.34), channel_id=1, source_target_pairs={{0,4},{4,0},{8,12},{12,8},{16,20},{20,16},{24,28},{28,24},{1,5},{5... | collective-permute-start | bytes 786440 | tf_op jit(solution)/shard_map/ppermute | solution.py:290
  6.3 6.8 %collective-permute-start.1 = (bf16[2,2,128,128]{3,2,1,0:T(8,128)(2,1)S(1)}, bf16[2,2,128,128]{3,2,1,0:T(8,128)(2,1)S(1)}, u32[]{:S(2)}, u32[]{:S(2)}) collective-permute-start(bf16[2,2,128,128]{3,2,1,0:T(8,128)(2,1)S(1)} %get-tuple-element.36), channel_id=1, source_target_pairs={{0,8},{4,12},{8,0},{12,4},{16,24},{20,28},{24,16},{28,20},{1,9},{5... | collective-permute-start | bytes 393224 | tf_op jit(solution)/shard_map/ppermute | solution.py:290
  9.1 8.2 %collective-permute-start.2 = (bf16[2,2,128,128]{3,2,1,0:T(8,128)(2,1)S(1)}, bf16[2,2,128,128]{3,2,1,0:T(8,128)(2,1)S(1)}, u32[]{:S(2)}, u32[]{:S(2)}) collective-permute-start(bf16[2,2,128,128]{3,2,1,0:T(8,128)(2,1)S(1)} %get-tuple-element.37), channel_id=1, source_target_pairs={{0,16},{4,20},{8,24},{12,28},{16,0},{20,4},{24,8},{28,12},{1,17},{... | collective-permute-start | bytes 393224 | tf_op jit(solution)/shard_map/ppermute | solution.py:290
  10.7 6.7 %collective-permute-start.3 = (bf16[2,2,128,128]{3,2,1,0:T(8,128)(2,1)S(1)}, bf16[2,2,128,128]{3,2,1,0:T(8,128)(2,1)S(1)}, u32[]{:S(2)}, u32[]{:S(2)}) collective-permute-start(bf16[2,2,128,128]{3,2,1,0:T(8,128)(2,1)S(1)} %get-tuple-element.38), channel_id=1, source_target_pairs={{0,24},{4,28},{8,16},{12,20},{16,8},{20,12},{24,0},{28,4},{1,25},{... | collective-permute-start | bytes 393224 | tf_op jit(solution)/shard_map/ppermute | solution.py:290
  17.3 7.3 %copy-start.2 = (s32[32,5]{0,1:T(8,128)S(1)}, s32[32,5]{0,1:T(8,128)}, u32[]{:S(2)}) copy-start(s32[32,5]{0,1:T(8,128)} %param.13) | copy-start | bytes 1924
  17.4 16.0 %collective-permute-start.6 = (bf16[2,8,128,128]{3,2,1,0:T(8,128)(2,1)S(1)}, bf16[2,8,128,128]{3,2,1,0:T(8,128)(2,1)}, u32[]{:S(2)}, u32[]{:S(2)}) collective-permute-start(bf16[2,8,128,128]{3,2,1,0:T(8,128)(2,1)S(1)} %get-tuple-element.45), channel_id=1, source_target_pairs={{0,24},{4,28},{8,16},{12,20},{16,8},{20,12},{24,0},{28,4},{1,25},{... | collective-permute-start | bytes 1572872 | tf_op jit(solution)/shard_map/ppermute | solution.py:290
  19.0 14.4 %collective-permute-start.4 = (bf16[8,2,128,128]{3,2,1,0:T(8,128)(2,1)S(1)}, bf16[8,2,128,128]{3,2,1,0:T(8,128)(2,1)S(1)}, u32[]{:S(2)}, u32[]{:S(2)}) collective-permute-start(bf16[8,2,128,128]{3,2,1,0:T(8,128)(2,1)S(1)} %shard_map.96.own_ref), channel_id=1, source_target_pairs={{0,1},{1,2},{2,3},{4,5},{5,6},{6,7},{8,9},{9,10},{10,11},{12,13},{... | collective-permute-start | bytes 1572872 | tf_op jit(solution)/shard_map/ppermute | solution.py:284
  22.5 20.0 %collective-permute-start.7 = (bf16[2,8,128,128]{3,2,1,0:T(8,128)(2,1)S(1)}, bf16[2,8,128,128]{3,2,1,0:T(8,128)(2,1)}, u32[]{:S(2)}, u32[]{:S(2)}) collective-permute-start(bf16[2,8,128,128]{3,2,1,0:T(8,128)(2,1)S(1)} %get-tuple-element.47), channel_id=1, source_target_pairs={{0,16},{4,20},{8,24},{12,28},{16,0},{20,4},{24,8},{28,12},{1,17},{... | collective-permute-start | bytes 1572872 | tf_op jit(solution)/shard_map/ppermute | solution.py:290
  23.8 19.0 %collective-permute-start.8 = (bf16[2,8,128,128]{3,2,1,0:T(8,128)(2,1)S(1)}, bf16[2,8,128,128]{3,2,1,0:T(8,128)(2,1)}, u32[]{:S(2)}, u32[]{:S(2)}) collective-permute-start(bf16[2,8,128,128]{3,2,1,0:T(8,128)(2,1)S(1)} %get-tuple-element.48), channel_id=1, source_target_pairs={{0,8},{4,12},{8,0},{12,4},{16,24},{20,28},{24,16},{28,20},{1,9},{5... | collective-permute-start | bytes 1572872 | tf_op jit(solution)/shard_map/ppermute | solution.py:290
  24.7 8.7 %copy-start = (f32[4,4096]{1,0:T(4,128)S(1)}, f32[4,4096]{1,0:T(4,128)}, u32[]{:S(2)}) copy-start(f32[4,4096]{1,0:T(4,128)} %lse_ref.3) | copy-start | bytes 196612
  24.7 8.7 %copy-start.1 = (f32[4,4096]{1,0:T(4,128)S(1)}, f32[4,4096]{1,0:T(4,128)}, u32[]{:S(2)}) copy-start(f32[4,4096]{1,0:T(4,128)} %delta_ref.3) | copy-start | bytes 196612
  49.3 16.6 %collective-permute-start.13 = (bf16[8,2,128,128]{3,2,1,0:T(8,128)(2,1)S(1)}, bf16[8,2,128,128]{3,2,1,0:T(8,128)(2,1)S(1)}, u32[]{:S(2)}, u32[]{:S(2)}) collective-permute-start(bf16[8,2,128,128]{3,2,1,0:T(8,128)(2,1)S(1)} %get-tuple-element.54), channel_id=1, source_target_pairs={{1,0},{2,1},{3,2},{5,4},{6,5},{7,6},{9,8},{10,9},{11,10},{13,12},{... | collective-permute-start | bytes 1572872 | tf_op jit(solution)/shard_map/ppermute | solution.py:284
  50.6 9.3 %collective-permute-start.9 = (bf16[2,4,128,128]{3,2,1,0:T(8,128)(2,1)S(1)}, bf16[2,4,128,128]{3,2,1,0:T(8,128)(2,1)S(1)}, u32[]{:S(2)}, u32[]{:S(2)}) collective-permute-start(bf16[2,4,128,128]{3,2,1,0:T(8,128)(2,1)S(1)} %get-tuple-element.50), channel_id=1, source_target_pairs={{0,8},{4,12},{8,0},{12,4},{16,24},{20,28},{24,16},{28,20},{1,9},{5... | collective-permute-start | bytes 786440 | tf_op jit(solution)/shard_map/ppermute | solution.py:290
  52.1 13.6 %collective-permute-start.10 = (bf16[2,4,128,128]{3,2,1,0:T(8,128)(2,1)S(1)}, bf16[2,4,128,128]{3,2,1,0:T(8,128)(2,1)S(1)}, u32[]{:S(2)}, u32[]{:S(2)}) collective-permute-start(bf16[2,4,128,128]{3,2,1,0:T(8,128)(2,1)S(1)} %get-tuple-element.51), channel_id=1, source_target_pairs={{0,16},{4,20},{8,24},{12,28},{16,0},{20,4},{24,8},{28,12},{1,17},{... | collective-permute-start | bytes 786440 | tf_op jit(solution)/shard_map/ppermute | solution.py:290
  52.7 13.0 %collective-permute-start.11 = (bf16[2,4,128,128]{3,2,1,0:T(8,128)(2,1)S(1)}, bf16[2,4,128,128]{3,2,1,0:T(8,128)(2,1)S(1)}, u32[]{:S(2)}, u32[]{:S(2)}) collective-permute-start(bf16[2,4,128,128]{3,2,1,0:T(8,128)(2,1)S(1)} %get-tuple-element.52), channel_id=1, source_target_pairs={{0,24},{4,28},{8,16},{12,20},{16,8},{20,12},{24,0},{28,4},{1,25},{... | collective-permute-start | bytes 786440 | tf_op jit(solution)/shard_map/ppermute | solution.py:290
  65.8 10.1 %collective-permute-start.12 = (bf16[4,4,128,128]{3,2,1,0:T(8,128)(2,1)S(1)}, bf16[4,4,128,128]{3,2,1,0:T(8,128)(2,1)S(1)}, u32[]{:S(2)}, u32[]{:S(2)}) collective-permute-start(bf16[4,4,128,128]{3,2,1,0:T(8,128)(2,1)S(1)} %pad_maximum_fusion), channel_id=1, source_target_pairs={{0,4},{4,0},{8,12},{12,8},{16,20},{20,16},{24,28},{28,24},{1,5},{5... | collective-permute-start | bytes 1572872 | tf_op jit(solution)/shard_map/ppermute | solution.py:290
  66.1 7.3 %collective-permute-start.16 = (bf16[2,2,128,128]{3,2,1,0:T(8,128)(2,1)S(1)}, bf16[2,2,128,128]{3,2,1,0:T(8,128)(2,1)S(1)}, u32[]{:S(2)}, u32[]{:S(2)}) collective-permute-start(bf16[2,2,128,128]{3,2,1,0:T(8,128)(2,1)S(1)} %get-tuple-element.57), channel_id=1, source_target_pairs={{0,24},{4,28},{8,16},{12,20},{16,8},{20,12},{24,0},{28,4},{1,25},{... | collective-permute-start | bytes 393224 | tf_op jit(solution)/shard_map/ppermute | solution.py:290
  67.6 8.2 %collective-permute-start.15 = (bf16[2,2,128,128]{3,2,1,0:T(8,128)(2,1)S(1)}, bf16[2,2,128,128]{3,2,1,0:T(8,128)(2,1)S(1)}, u32[]{:S(2)}, u32[]{:S(2)}) collective-permute-start(bf16[2,2,128,128]{3,2,1,0:T(8,128)(2,1)S(1)} %get-tuple-element.58), channel_id=1, source_target_pairs={{0,16},{4,20},{8,24},{12,28},{16,0},{20,4},{24,8},{28,12},{1,17},{... | collective-permute-start | bytes 393224 | tf_op jit(solution)/shard_map/ppermute | solution.py:290
  68.2 7.5 %collective-permute-start.14 = (bf16[2,2,128,128]{3,2,1,0:T(8,128)(2,1)S(1)}, bf16[2,2,128,128]{3,2,1,0:T(8,128)(2,1)S(1)}, u32[]{:S(2)}, u32[]{:S(2)}) collective-permute-start(bf16[2,2,128,128]{3,2,1,0:T(8,128)(2,1)S(1)} %get-tuple-element.59), channel_id=1, source_target_pairs={{0,8},{4,12},{8,0},{12,4},{16,24},{20,28},{24,16},{28,20},{1,9},{5... | collective-permute-start | bytes 393224 | tf_op jit(solution)/shard_map/ppermute | solution.py:290
  75.8 1.6 %collective-permute-start.17 = (bf16[4,2,128,128]{3,2,1,0:T(8,128)(2,1)S(1)}, bf16[4,2,128,128]{3,2,1,0:T(8,128)(2,1)S(1)}, u32[]{:S(2)}, u32[]{:S(2)}) collective-permute-start(bf16[4,2,128,128]{3,2,1,0:T(8,128)(2,1)S(1)} %pad_maximum_fusion.1), channel_id=1, source_target_pairs={{0,4},{4,0},{8,12},{12,8},{16,20},{20,16},{24,28},{28,24},{1,5},{5... | collective-permute-start | bytes 786440 | tf_op jit(solution)/shard_map/ppermute | solution.py:290

commit v3 on v2

v3 whole, which is shorter than its diff:
```python
import functools
import math

import jax
import jax.numpy as jnp
from jax import lax
from jax.experimental import pallas as pl
from jax.experimental.pallas import tpu as pltpu
from jax.sharding import PartitionSpec as P

BLOCK = 128
LOG2E = 1.4426950408889634
FIRST, NEXT, LAST = range(3)
SHORT, ADD_COST = 2 * 10**9, 10**11


def contract(a, b, a_dim, b_dim):
    return lax.dot_general(a, b, (((a_dim,), (b_dim,)), ((), ())), preferred_element_type=jnp.float32)


def held(x):
    return pltpu.with_memory_space_constraint(x, pltpu.VMEM)


def block_kernel(blocks, out_count, half_count, operand_count, call, slab_ref, me_ref, keys_ref, lse_ref, delta_ref, *refs):
    qd_refs, refs = refs[:operand_count], refs[operand_count:]
    halves, refs = refs[:half_count], refs[half_count:]
    if call == FIRST:
        (own_ref, prev_ref), dq_refs, (kv, acc, cat_k, cat_v) = refs[:2], refs[2 : 2 + out_count], refs[2 + out_count :]
    else:
        (kv, acc_in), dq_refs, refs = refs[:2], refs[2 : 2 + out_count], refs[2 + out_count :]
        if call == LAST:
            own_out, *prev_out, acc, cat_k, cat_v = refs
        else:
            acc, cat_k, cat_v = refs
    for half, dq_ref in zip(halves, dq_refs):
        dq_ref[0] = half[0]
    slab_blocks = acc.shape[0] // 2
    heads = dq_refs[0].shape[1]
    select = keys_ref.shape[1]
    rows = heads * BLOCK
    head_dim = kv.shape[3]
    scale = 1.0 / math.sqrt(head_dim)
    first = slab_ref[0] * slab_blocks
    me = me_ref[0]
    if call != FIRST:
        acc[...] = acc_in[...]
    else:
        kv[:slab_blocks] = prev_ref[...]
        kv[slab_blocks:] = own_ref[...]
        acc[...] = jnp.zeros_like(acc)
    key_pos = lax.broadcasted_iota(jnp.int32, (BLOCK, rows), 0)
    query_pos = lax.broadcasted_iota(jnp.int32, (BLOCK, rows), 1) % BLOCK
    causal = key_pos <= query_pos

    def query_block(slot, operand, row, out, out_row):
        b = me ^ slot
        q = qd_refs[operand][row, :heads].reshape(rows, head_dim)
        do = qd_refs[operand][row, heads:].reshape(rows, head_dim)
        entries = [keys_ref[first + b, j] for j in range(select)]
        places = [jnp.where(e < first, 0, slab_blocks) + ((e - first) & (slab_blocks - 1) ^ me) for e in entries]
        for j, place in enumerate(places):
            cat_k[pl.ds(j * BLOCK, BLOCK)] = kv[place, 0]
            cat_v[pl.ds(j * BLOCK, BLOCK)] = kv[place, 1]
        lanes = pl.ds(pl.multiple_of((first + b) * BLOCK, BLOCK), BLOCK)
        lse = jnp.concatenate([lse_ref[pl.ds(h, 1), lanes] for h in range(heads)], 1) * LOG2E
        delta = jnp.concatenate([delta_ref[pl.ds(h, 1), lanes] for h in range(heads)], 1)
        s = contract(cat_k[...], q, 1, 1)
        dp = contract(cat_v[...], do, 1, 1)
        p_parts = []
        for j in range(select):
            p = jnp.exp2(s[j * BLOCK : (j + 1) * BLOCK] * (scale * LOG2E) - lse)
            allowed = causal if j == 0 else entries[j] >= 0
            p_parts.append(jnp.where(allowed, p, 0.0))
        p = jnp.concatenate(p_parts, 0)
        ds = (p * (dp - delta)).astype(jnp.bfloat16)
        dv = contract(p.astype(jnp.bfloat16), do, 1, 0)
        dk = contract(ds, q, 1, 0) * scale
        dq = contract(ds, cat_k[...], 0, 0) * scale
        dq_refs[out][out_row] = dq.astype(jnp.bfloat16).reshape(heads, BLOCK, head_dim)
        for j, place in enumerate(places):
            part = slice(j * BLOCK, (j + 1) * BLOCK)
            acc[place, 0] += dk[part]
            acc[place, 1] += dv[part]

    for block in blocks:
        query_block(*block)
    if call == LAST:
        at = 0
        for out in prev_out:
            out[...] = acc[at : at + out.shape[0]].astype(out.dtype)
            at += out.shape[0]
        own_out[...] = acc[slab_blocks:]


def block_grads(blocks, out_rows, slab, me, block_keys, lse, delta, pieces, halves, kept, call):
    slab_blocks = kept[0].shape[0] if call == FIRST else kept[0].shape[0] // 2
    head_dim = pieces[0].shape[3]
    heads = lse.shape[0]
    select = block_keys.shape[1]
    smem = pl.BlockSpec(memory_space=pltpu.SMEM)
    vmem = pl.BlockSpec(memory_space=pltpu.VMEM)
    wide = select * BLOCK
    macs = len(blocks) * heads * select * 5 * BLOCK * BLOCK * head_dim
    acc = jax.ShapeDtypeStruct((2 * slab_blocks, 2, BLOCK, head_dim), jnp.float32)
    out_shape = [jax.ShapeDtypeStruct((rows, heads, BLOCK, head_dim), jnp.bfloat16) for rows in out_rows]
    operands = [lse, delta, *pieces, *halves, *kept]
    if call == LAST:
        out_shape.append(jax.ShapeDtypeStruct((slab_blocks, 2, BLOCK, head_dim), jnp.float32))
        out_shape += [jax.ShapeDtypeStruct((count, 2, BLOCK, head_dim), jnp.bfloat16) for count in (2, slab_blocks - 4, 2)]
    elif call == FIRST:
        out_shape += [jax.ShapeDtypeStruct(acc.shape, jnp.bfloat16), acc]
    else:
        out_shape.append(acc)
    return pl.pallas_call(
        functools.partial(block_kernel, blocks, len(out_rows), len(halves), len(pieces), call),
        in_specs=[smem] * 3 + [vmem] * len(operands),
        out_specs=[vmem] * len(out_shape),
        out_shape=out_shape,
        scratch_shapes=[pltpu.VMEM(acc.shape, acc.dtype)] * (call == LAST) + [pltpu.VMEM((wide, head_dim), jnp.bfloat16)] * 2,
        compiler_params=pltpu.CompilerParams(vmem_limit_bytes=32 * 1024 * 1024 if slab_blocks > 8 else 16 * 1024 * 1024),
        cost_estimate=pl.CostEstimate(flops=2 * macs, bytes_accessed=8 * 1024 * 1024, transcendentals=0),
    )(slab, me, block_keys, *operands)


def pack_kernel(fold_counts, after_count, me_ref, *refs):
    count = len(fold_counts)
    chips = refs[-1 - 2 * count - 1].shape[0]
    sources, refs = refs[:count], refs[count + after_count :]
    pieces, give, refs = refs[:chips], refs[chips], refs[chips + 1 :]
    by_token, by_head, sems = refs[:count], refs[count : 2 * count], refs[-1]
    devices = 2 * chips
    me = me_ref[0]
    copies = [pltpu.make_async_copy(sources[i], by_token[i], sems.at[i]) for i in range(count)]
    for copy in copies:
        copy.start()
    at = 0
    for copy, source, target, fold_count in zip(copies, by_token, by_head, fold_counts):
        copy.wait()
        target[...] = jnp.swapaxes(source[...], 0, 1)
        heads = target.shape[0] * fold_count // devices
        for m in range(chips):
            for out, j in ((pieces[m].at[0], 0), (give.at[m], 1)):
                device = me ^ (2 * m + j)
                out[at : at + heads] = target[pl.ds(device // fold_count * heads, heads)]
        at += heads


def packed(me, arrays, fold_counts, uly_count, whole, after):
    tokens, _, head_dim = arrays[0].shape
    chips = uly_count // 2
    tiles = sum(x.shape[1] * fold_count for x, fold_count in zip(arrays, fold_counts)) // uly_count
    vmem = pl.BlockSpec(memory_space=pltpu.VMEM)
    shapes = [jax.ShapeDtypeStruct((2 if m in whole else 1, tiles, tokens, head_dim), arrays[0].dtype) for m in range(chips)]
    shapes.append(jax.ShapeDtypeStruct((chips, tiles, tokens, head_dim), arrays[0].dtype))
    *pieces, give = pl.pallas_call(
        functools.partial(pack_kernel, fold_counts, len(after)),
        in_specs=[pl.BlockSpec(memory_space=pltpu.SMEM)] + [pl.BlockSpec(memory_space=pltpu.HBM)] * len(arrays) + [pl.BlockSpec(memory_space=pl.ANY)] * len(after),
        out_specs=[vmem] * len(shapes),
        out_shape=shapes,
        scratch_shapes=[pltpu.VMEM(x.shape, x.dtype) for x in arrays]
        + [pltpu.VMEM((x.shape[1], tokens, head_dim), x.dtype) for x in arrays]
        + [pltpu.SemaphoreType.DMA((len(arrays),))],
        compiler_params=pltpu.CompilerParams(vmem_limit_bytes=8 * 1024 * 1024),
    )(me, *[pltpu.with_memory_space_constraint(x, pltpu.HBM) for x in arrays], *after)
    return pieces, give


def merge_kernel(whole, chips, count, *refs):
    got, outs = refs[len(whole)], refs[-count:]
    for m, out in zip(whole, outs):
        out[1] = got[m]
    for m, out in zip([m for m in range(chips) if m not in whole], outs[len(whole) :]):
        out[0] = got[m]


def merged(pieces, whole, got, after):
    chips = got.shape[0]
    apart = chips - len(whole)
    vmem = pl.BlockSpec(memory_space=pltpu.VMEM)
    shapes = [jax.ShapeDtypeStruct(pieces[m].shape, got.dtype) for m in whole]
    shapes += [jax.ShapeDtypeStruct((1, *got.shape[1:]), got.dtype)] * apart
    return pl.pallas_call(
        functools.partial(merge_kernel, whole, chips, len(shapes)),
        in_specs=[vmem] * (len(whole) + 1) + [pl.BlockSpec(memory_space=pl.ANY)] * len(after),
        out_specs=[vmem] * chips,
        out_shape=shapes,
        input_output_aliases={i: i for i in range(len(whole))},
        compiler_params=pltpu.CompilerParams(vmem_limit_bytes=8 * 1024 * 1024),
    )(*[held(pieces[m]) for m in whole], got, *after)


def landed_kernel(*refs):
    pass


def landed(piece, after, flops):
    hold = pl.BlockSpec(memory_space=pl.ANY)
    return pl.pallas_call(
        landed_kernel,
        in_specs=[hold] * (1 + len(after)),
        out_specs=hold,
        out_shape=jax.ShapeDtypeStruct(piece.shape, piece.dtype),
        input_output_aliases={0: 0},
        cost_estimate=pl.CostEstimate(flops=flops, bytes_accessed=2**20, transcendentals=0),
    )(piece, *after)


def join_kernel(*refs):
    *pieces, out = refs
    for m, piece in enumerate(pieces):
        out[2 * m : 2 * m + 2] = piece[...]


def joined(pieces):
    vmem = pl.BlockSpec(memory_space=pltpu.VMEM)
    return pl.pallas_call(
        join_kernel,
        in_specs=[vmem] * len(pieces),
        out_specs=vmem,
        out_shape=jax.ShapeDtypeStruct((2 * len(pieces), *pieces[0].shape[1:]), pieces[0].dtype),
        compiler_params=pltpu.CompilerParams(vmem_limit_bytes=16 * 1024 * 1024),
        cost_estimate=pl.CostEstimate(flops=2**20, bytes_accessed=2**20, transcendentals=0),
    )(*pieces)


def add_kernel(first, after_count, own, back, *refs):
    for i, out in enumerate(refs[after_count:]):
        rows = slice(2 * (first + i), 2 * (first + i) + 2)
        out[...] = (own[rows] + back[2 * i : 2 * i + 2].astype(jnp.float32)).astype(out.dtype)


def added(first, own, back, after):
    vmem = pl.BlockSpec(memory_space=pltpu.VMEM)
    count = back.shape[0] // 2
    return pl.pallas_call(
        functools.partial(add_kernel, first, len(after)),
        in_specs=[vmem] * 2 + [vmem if x.ndim == 4 else pl.BlockSpec(memory_space=pltpu.HBM) for x in after],
        out_specs=[vmem] * count,
        out_shape=[jax.ShapeDtypeStruct((2, *back.shape[1:]), back.dtype)] * count,
        compiler_params=pltpu.CompilerParams(vmem_limit_bytes=8 * 1024 * 1024),
        cost_estimate=pl.CostEstimate(flops=ADD_COST, bytes_accessed=2**20, transcendentals=0),
    )(own, back, *[x if x.ndim == 4 else pltpu.with_memory_space_constraint(x, pltpu.HBM) for x in after])


def collect_kernel(chips, *refs):
    for m in range(chips):
        refs[-1][m] = refs[m][1]


def collected(chunks, after):
    vmem = pl.BlockSpec(memory_space=pltpu.VMEM)
    return pl.pallas_call(
        functools.partial(collect_kernel, len(chunks)),
        in_specs=[vmem] * len(chunks) + [pl.BlockSpec(memory_space=pl.ANY)] * len(after),
        out_specs=vmem,
        out_shape=jax.ShapeDtypeStruct((len(chunks), *chunks[0].shape[1:]), chunks[0].dtype),
        compiler_params=pltpu.CompilerParams(vmem_limit_bytes=8 * 1024 * 1024),
    )(*chunks, *after)


def unpack_kernel(chips, fold_count, me_ref, *refs):
    here, (got, *refs) = refs[:chips], refs[chips:]
    count = (len(refs) - 1) // 3
    outs, by_head, by_token, sems = refs[:count], refs[count : 2 * count], refs[2 * count : 3 * count], refs[-1]
    me = me_ref[0]
    for k in range(2 * chips):
        device = me ^ k
        part = here[k // 2][0] if k % 2 == 0 else got[k // 2]
        heads = part.shape[0] // count
        for i in range(count):
            by_head[i][pl.ds(device * heads, heads)] = part[i * heads : (i + 1) * heads]
    copies = [pltpu.make_async_copy(by_token[i], outs[i], sems.at[i]) for i in range(count)]
    for i in range(count):
        whole = by_head[i][...]
        if fold_count > 1:
            whole = whole.reshape(-1, fold_count, *whole.shape[1:]).astype(jnp.float32).sum(1).astype(whole.dtype)
        by_token[i][...] = jnp.swapaxes(whole, 0, 1)
        copies[i].start()
    for copy in copies:
        copy.wait()


def unpacked(me, here, got, count, fold_count):
    chips, tiles, tokens, head_dim = got.shape
    devices = 2 * chips
    vmem = pl.BlockSpec(memory_space=pltpu.VMEM)
    heads = devices * tiles // count
    shape = (tokens, heads // fold_count, head_dim)
    return pl.pallas_call(
        functools.partial(unpack_kernel, chips, fold_count),
        in_specs=[pl.BlockSpec(memory_space=pltpu.SMEM)] + [vmem] * (chips + 1),
        out_specs=[pl.BlockSpec(memory_space=pltpu.HBM)] * count,
        out_shape=[jax.ShapeDtypeStruct(shape, got.dtype)] * count,
        scratch_shapes=[pltpu.VMEM((heads, tokens, head_dim), got.dtype)] * count
        + [pltpu.VMEM(shape, got.dtype)] * count
        + [pltpu.SemaphoreType.DMA((count,))],
        compiler_params=pltpu.CompilerParams(vmem_limit_bytes=16 * 1024 * 1024),
    )(me, *here, got)


def passed_along(block, axis, distance):
    devices = range(lax.axis_size(axis))
    return lax.ppermute(block, axis, [(i - distance, i) for i in devices if i - distance in devices])


def swapped(block, k):
    if k == 0:
        return block
    return lax.ppermute(block, "uly", [(i, i ^ k) for i in range(lax.axis_size("uly"))])


def shards(queries, keys, values, grad_out, lse, delta, block_keys):
    uly_count = lax.axis_size("uly")
    head_total = queries.shape[1]
    fold_count = uly_count // keys.shape[1]
    heads = head_total // uly_count
    chips = uly_count // 2
    far = chips - 1
    me = lax.axis_index("uly").reshape(1)
    slab = lax.axis_index("blk").reshape(1)

    every, ends, mids = list(range(chips)), [0, far], list(range(1, far))
    kv_pieces, give_kv = packed(me, [keys, values], [fold_count] * 2, uly_count, every, [])
    merged_kv = merged(kv_pieces, every, swapped(give_kv, 1), [])
    kv_pieces = [swapped(piece, 2 * m) for m, piece in enumerate(merged_kv)]
    own = joined(kv_pieces)
    qd_pieces, give_qd = packed(me, [queries, grad_out], [1] * 2, uly_count, ends, merged_kv[:1])
    qd_here, qd_far, *seconds = merged(qd_pieces, ends, swapped(give_qd, 1), kv_pieces[1:])
    qd_far = landed(swapped(qd_far, 2 * far), [], SHORT)
    firsts = [swapped(qd_pieces[m], 2 * m) for m in mids]
    seconds = [swapped(piece, 2 * m) for m, piece in zip(mids, seconds)]
    prev = passed_along(own, "blk", 1)

    grads = functools.partial(block_grads, slab=slab, me=me, block_keys=block_keys, lse=lse, delta=delta)
    blocks = [(2 * m + i, operand, i, operand, i) for operand, m in enumerate(ends) for i in range(2)]
    dq_here, dq_far, kv, acc = grads(blocks, [2, 2], pieces=[qd_here, qd_far], halves=[], kept=[own, prev], call=FIRST)
    blocks = [(2 * m, i, 0, i, 0) for i, m in enumerate(mids)]
    *halves, acc = grads(blocks, [1] * len(mids), pieces=firsts, halves=[], kept=[kv, acc], call=NEXT)
    blocks = [(2 * m + 1, i, 0, i, 1) for i, m in enumerate(mids)]
    outs = grads(blocks, [2] * len(mids), pieces=seconds, halves=halves, kept=[kv, acc], call=LAST)
    *dq_mid, own_grad, prev_here, prev_mid, prev_far = outs
    dq = [swapped(x, 2 * m) for m, x in enumerate([dq_here, *dq_mid, dq_far])]

    def back_added(part, first, after):
        total = added(first, own_grad, passed_along(part, "blk", -1), after)
        return [swapped(x, 2 * (first + i)) for i, x in enumerate(total)]

    kv_far = back_added(prev_far, far, [dq[far]])
    (grad_queries,) = unpacked(me, dq, swapped(collected(dq, []), 1), 1, 1)
    kv_mid = back_added(prev_mid, 1, dq[1:far] + kv_far)
    kv_here = back_added(prev_here, 0, kv_mid + [grad_queries])
    kv_grad = kv_here + kv_mid + kv_far
    got_kv = swapped(collected(kv_grad, []), 1)
    grad_keys, grad_values = unpacked(me, kv_grad, got_kv, 2, fold_count)
    return grad_queries, grad_keys, grad_values


def solution(mesh):
    spread = P(("blk", "uly"), None, None)
    return jax.shard_map(
        shards,
        mesh=mesh,
        in_specs=(spread, spread, spread, spread, P("uly", None), P("uly", None), P()),
        out_specs=(spread, spread, spread),
        check_vma=False,
    )
```

time: 78.6 us -> 73.9 us (0.940)
  waiting for transfers between devices: 37.5 us -> 26.2 us
  starting transfers between devices: 20.7 us -> 26.2 us
  local copies, waits for them, and re-layouts: 0.2 us -> 2.53 us
  Pallas kernels: 18.8 us -> 17.8 us
    ppermute x16 -> x18, waiting for transfers between devices: 37.5 us -> 21 us  [swapped(): lax.ppermute(block, 'uly', [(i, i ^ k) for i in range(lax.axis_size('uly'...]
    ppermute x2 -> x4, waiting for transfers between devices: 0.01 us -> 5.2 us  [passed_along(): lax.ppermute(block, axis, [(i - distance, i) for i in devices if i - dist...]
    ppermute x16 -> x18, starting transfers between devices: 15.9 us -> 18.8 us  [swapped(): lax.ppermute(block, 'uly', [(i, i ^ k) for i in range(lax.axis_size('uly'...]
    ppermute x2 -> x4, starting transfers between devices: 4.81 us -> 7.37 us  [passed_along(): lax.ppermute(block, axis, [(i - distance, i) for i in devices if i - dist...]
    unnamed x7 -> x15, local copies, waits for them, and re-layouts: 0.1 us -> 2.53 us
    pallas_call x7 -> x13, Pallas kernels: 16.4 us -> 15.3 us  [the longest x3 10.8 us: block_grads(): pl.pallas_call(functools.partial(block_kernel, blocks, len(out_rows), len...]
  transfers between devices with their start and end apart: 18 -> 22, of which waited for: 10 -> 10; matrix products, arithmetic and copies ran while one was open for 1% -> 0% of each run, Pallas kernels for 11% -> 17%
where the time goes in v3:
time: 73.9 us; the launch traced here: 73.6 us
  starting transfers between devices  26.2 us (35%)
  waiting for transfers between devices  26.2 us (35%)
  Pallas kernels  17.8 us (24%)
  local copies, waits for them, and re-layouts  2.53 us (3%)
  between operations  0.87 us (1%)
    ppermute x18, waiting for transfers between devices, swapped(): lax.ppermute(block, 'uly', [(i, i ^ k) for i in range(lax.axis_size('uly'...  21 us
    ppermute x18, starting transfers between devices, swapped(): lax.ppermute(block, 'uly', [(i, i ^ k) for i in range(lax.axis_size('uly'...  18.8 us
    pallas_call x3, Pallas kernels, block_grads(): pl.pallas_call(functools.partial(block_kernel, blocks, len(out_rows), len...  10.8 us
    ppermute x4, starting transfers between devices, passed_along(): lax.ppermute(block, axis, [(i - distance, i) for i in devices if i - dist...  7.37 us
    ppermute x4, waiting for transfers between devices, passed_along(): lax.ppermute(block, axis, [(i - distance, i) for i in devices if i - dist...  5.2 us
    pallas_call x2, Pallas kernels, packed(): pl.pallas_call(functools.partial(pack_kernel, fold_counts, len(after)), i...  4.34 us
    unnamed x15, local copies, waits for them, and re-layouts  2.53 us
    pallas_call x2, Pallas kernels, unpacked(): pl.pallas_call(functools.partial(unpack_kernel, chips, fold_count), in_sp...  2.38 us
  transfers between devices with their start and end apart: 22, of which 10 were waited for; matrix products, arithmetic and copies ran while one was open for 0% of the time, Pallas kernels for 17%

profile of v3, /device:TPU:0, one launch (start us, length us, event | category | flops | bytes accessed | tf_op | source)
XLA Modules:
  0.0 73.6 jit_solution(9762685447328307235)
XLA Ops:
  0.6 1.2 %shard_map.94 = (bf16[2,2,128,128]{3,2,1,0:T(8,128)(2,1)S(1)}, bf16[2,2,128,128]{3,2,1,0:T(8,128)(2,1)S(1)}, bf16[2,2,128,128]{3,2,1,0:T(8,128)(2,1)S(1)}, bf16[...) custom-call(s32[1]{0:T(128)} %bitcast.me_ref, bf16[128,8,128]{2,1,0:T(8,128)(2,1)} %refs_0_.2, ...), custom_call_target="tpu_custom_call" | custom-call | tf_op jit(solution)/shard_map/pallas_call | solution.py:156
  2.3 1.2 %collective-permute-done.refs_4_ = bf16[4,2,128,128]{3,2,1,0:T(8,128)(2,1)S(1)} collective-permute-done((bf16[4,2,128,128]{3,2,1,0:T(8,128)(2,1)S(1)}, bf16[4,2,128,128]{3,2,1,0:T(8,128)(2,1)S(1)}, u32[]{:S(2)}, u32[]{:S(2)}) %collective-permute-start) | collective-permute-done | bytes 262176 | tf_op jit(solution)/shard_map/ppermute | solution.py:310
  3.5 3.2 %shard_map.96 = (bf16[2,8,128,128]{3,2,1,0:T(8,128)(2,1)S(1)}, bf16[1,8,128,128]{3,2,1,0:T(8,128)(2,1)}, bf16[1,8,128,128]{3,2,1,0:T(8,128)(2,1)}, bf16[2,8,128,...) custom-call(s32[1]{0:T(128)} %bitcast.me_ref, bf16[128,32,128]{2,1,0:T(8,128)(2,1)} %refs_0_.3, ...), custom_call_target="tpu_custom_call" | custom-call | tf_op jit(solution)/shard_map/pallas_call | solution.py:156
  7.2 2.6 %collective-permute-start.2 = (bf16[2,2,128,128]{3,2,1,0:T(8,128)(2,1)S(1)}, bf16[2,2,128,128]{3,2,1,0:T(8,128)(2,1)S(1)}, u32[]{:S(2)}, u32[]{:S(2)}) collective-permute-start(bf16[2,2,128,128]{3,2,1,0:T(8,128)(2,1)S(1)} %get-tuple-element.47), channel_id=1, source_target_pairs={{0,8},{4,12},{8,0},{12,4},{16,24},{20,28},{24,16},{28,20},{1,9},{5... | collective-permute-start | bytes 393224 | tf_op jit(solution)/shard_map/ppermute | solution.py:310
  9.8 1.5 %collective-permute-start.3 = (bf16[2,2,128,128]{3,2,1,0:T(8,128)(2,1)S(1)}, bf16[2,2,128,128]{3,2,1,0:T(8,128)(2,1)S(1)}, u32[]{:S(2)}, u32[]{:S(2)}) collective-permute-start(bf16[2,2,128,128]{3,2,1,0:T(8,128)(2,1)S(1)} %get-tuple-element.48), channel_id=1, source_target_pairs={{0,16},{4,20},{8,24},{12,28},{16,0},{20,4},{24,8},{28,12},{1,17},{... | collective-permute-start | bytes 393224 | tf_op jit(solution)/shard_map/ppermute | solution.py:310
  11.3 2.6 %collective-permute-done.2.refs_3_.refs_1_ = bf16[2,2,128,128]{3,2,1,0:T(8,128)(2,1)S(1)} collective-permute-done((bf16[2,2,128,128]{3,2,1,0:T(8,128)(2,1)S(1)}, bf16[2,2,128,128]{3,2,1,0:T(8,128)(2,1)S(1)}, u32[]{:S(2)}, u32[]{:S(2)}) %collective-permute-start.2) | collective-permute-done | bytes 131104 | tf_op jit(solution)/shard_map/ppermute | solution.py:310
  13.9 4.2 %collective-permute-done.3.refs_4_.refs_2_ = bf16[2,2,128,128]{3,2,1,0:T(8,128)(2,1)S(1)} collective-permute-done((bf16[2,2,128,128]{3,2,1,0:T(8,128)(2,1)S(1)}, bf16[2,2,128,128]{3,2,1,0:T(8,128)(2,1)S(1)}, u32[]{:S(2)}, u32[]{:S(2)}) %collective-permute-start.3) | collective-permute-done | bytes 131104 | tf_op jit(solution)/shard_map/ppermute | solution.py:310
  19.6 1.5 %collective-permute-start.5 = (bf16[2,8,128,128]{3,2,1,0:T(8,128)(2,1)S(1)}, bf16[2,8,128,128]{3,2,1,0:T(8,128)(2,1)S(1)}, u32[]{:S(2)}, u32[]{:S(2)}) collective-permute-start(bf16[2,8,128,128]{3,2,1,0:T(8,128)(2,1)S(1)} %get-tuple-element.51), channel_id=1, source_target_pairs={{0,24},{4,28},{8,16},{12,20},{16,8},{20,12},{24,0},{28,4},{1,25},{... | collective-permute-start | bytes 1572872 | tf_op jit(solution)/shard_map/ppermute | solution.py:310
  21.1 3.5 %collective-permute-start.6 = (bf16[8,2,128,128]{3,2,1,0:T(8,128)(2,1)S(1)}, bf16[8,2,128,128]{3,2,1,0:T(8,128)(2,1)S(1)}, u32[]{:S(2)}, u32[]{:S(2)}) collective-permute-start(bf16[8,2,128,128]{3,2,1,0:T(8,128)(2,1)S(1)} %shard_map.99.refs_2_), channel_id=1, source_target_pairs={{0,1},{1,2},{2,3},{4,5},{5,6},{6,7},{8,9},{9,10},{10,11},{12,13},{... | collective-permute-start | bytes 1572872 | tf_op jit(solution)/shard_map/ppermute | solution.py:304
  24.7 1.5 %collective-permute-start.9 = (bf16[1,8,128,128]{3,2,1,0:T(8,128)(2,1)}, bf16[1,8,128,128]{3,2,1,0:T(8,128)(2,1)S(1)}, u32[]{:S(2)}, u32[]{:S(2)}) collective-permute-start(bf16[1,8,128,128]{3,2,1,0:T(8,128)(2,1)} %get-tuple-element.55), channel_id=1, source_target_pairs={{0,8},{4,12},{8,0},{12,4},{16,24},{20,28},{24,16},{28,20},{1,9},{5... | collective-permute-start | bytes 786440 | tf_op jit(solution)/shard_map/ppermute | solution.py:310
  26.7 1.2 %collective-permute-start.7 = (bf16[1,8,128,128]{3,2,1,0:T(8,128)(2,1)}, bf16[1,8,128,128]{3,2,1,0:T(8,128)(2,1)S(1)}, u32[]{:S(2)}, u32[]{:S(2)}) collective-permute-start(bf16[1,8,128,128]{3,2,1,0:T(8,128)(2,1)} %copy-done.5), channel_id=1, source_target_pairs={{0,8},{4,12},{8,0},{12,4},{16,24},{20,28},{24,16},{28,20},{1,9},{5... | collective-permute-start | bytes 786440 | tf_op jit(solution)/shard_map/ppermute | solution.py:310
  27.9 7.4 %collective-permute-done.5.refs_0_ = bf16[2,8,128,128]{3,2,1,0:T(8,128)(2,1)S(1)} collective-permute-done((bf16[2,8,128,128]{3,2,1,0:T(8,128)(2,1)S(1)}, bf16[2,8,128,128]{3,2,1,0:T(8,128)(2,1)S(1)}, u32[]{:S(2)}, u32[]{:S(2)}) %collective-permute-start.5) | collective-permute-done | bytes 524320 | tf_op jit(solution)/shard_map/ppermute | solution.py:310
  35.4 1.5 %collective-permute-start.8 = (bf16[1,8,128,128]{3,2,1,0:T(8,128)(2,1)}, bf16[1,8,128,128]{3,2,1,0:T(8,128)(2,1)S(1)}, u32[]{:S(2)}, u32[]{:S(2)}) collective-permute-start(bf16[1,8,128,128]{3,2,1,0:T(8,128)(2,1)} %copy-done.4), channel_id=1, source_target_pairs={{0,16},{4,20},{8,24},{12,28},{16,0},{20,4},{24,8},{28,12},{1,17},{... | collective-permute-start | bytes 786440 | tf_op jit(solution)/shard_map/ppermute | solution.py:310
  36.9 1.0 %copy-done.3 = bf16[2,8,128,128]{3,2,1,0:T(8,128)(2,1)S(1)} copy-done((bf16[2,8,128,128]{3,2,1,0:T(8,128)(2,1)S(1)}, bf16[2,8,128,128]{3,2,1,0:T(8,128)(2,1)}, u32[]{:S(2)}) %copy-start.3) | copy-done | bytes 524312
  38.0 4.8 %shard_map.100 = (bf16[2,4,128,128]{3,2,1,0:T(8,128)(2,1)S(1)}, bf16[2,4,128,128]{3,2,1,0:T(8,128)(2,1)S(1)}, bf16[16,2,128,128]{3,2,1,0:T(8,128)(2,1)S(1)}, f32[16,2,128,128]{3,2,1,0:T(8,128)S(1)}) custom-call(s32[1]{0:T(128)} %bitcast.1.slab_ref, s32[1]{0:T(128)} %bitcast.me_ref, s32[32,5]{1,0:T(8,128)S(1)} %copy.17.keys_ref, f32[4,4096]{1,0:T(4,128)S(1)} %copy-done, ...), custom_call_target="tpu_custom_call" | custom-call | flops 1677721600 | bytes 8388608 | tf_op jit(solution)/shard_map/pallas_call | solution.py:115
  42.7 1.2 %collective-permute-start.13 = (bf16[2,4,128,128]{3,2,1,0:T(8,128)(2,1)S(1)}, bf16[2,4,128,128]{3,2,1,0:T(8,128)(2,1)S(1)}, u32[]{:S(2)}, u32[]{:S(2)}) collective-permute-start(bf16[2,4,128,128]{3,2,1,0:T(8,128)(2,1)S(1)} %get-tuple-element.64), channel_id=1, source_target_pairs={{0,24},{4,28},{8,16},{12,20},{16,8},{20,12},{24,0},{28,4},{1,25},{... | collective-permute-start | bytes 786440 | tf_op jit(solution)/shard_map/ppermute | solution.py:310
  44.0 2.9 %shard_map.101 = (bf16[1,4,128,128]{3,2,1,0:T(8,128)(2,1)S(1)}, bf16[1,4,128,128]{3,2,1,0:T(8,128)(2,1)S(1)}, f32[16,2,128,128]{3,2,1,0:T(8,128)S(1)}) custom-call(s32[1]{0:T(128)} %bitcast.1.slab_ref, s32[1]{0:T(128)} %bitcast.me_ref, s32[32,5]{1,0:T(8,128)S(1)} %copy.17.keys_ref, f32[4,4096]{1,0:T(4,128)S(1)} %copy-done, f32[4,4096]{1,0:T(4,128)S(1)} %copy-done.1, ...), custom_call_target="tpu_custom_call" | custom-call | flops 838860800 | bytes 8388608 | tf_op jit(solution)/shard_map/pallas_call | solution.py:115
  46.9 3.1 %shard_map.102 = (bf16[2,4,128,128]{3,2,1,0:T(8,128)(2,1)S(1)}, bf16[2,4,128,128]{3,2,1,0:T(8,128)(2,1)S(1)}, f32[8,2,128,128]{3,2,1,0:T(8,128)S(1)}, bf16[2,2,1...) custom-call(s32[1]{0:T(128)} %bitcast.1.slab_ref, ...), custom_call_target="tpu_custom_call" | custom-call | flops 838860800 | bytes 8388608 | tf_op jit(solution)/shard_map/pallas_call | solution.py:115
  50.0 1.3 %collective-permute-start.17 = (bf16[2,2,128,128]{3,2,1,0:T(8,128)(2,1)S(1)}, bf16[2,2,128,128]{3,2,1,0:T(8,128)(2,1)S(1)}, u32[]{:S(2)}, u32[]{:S(2)}) collective-permute-start(bf16[2,2,128,128]{3,2,1,0:T(8,128)(2,1)S(1)} %get-tuple-element.68), channel_id=1, source_target_pairs={{1,0},{2,1},{3,2},{5,4},{6,5},{7,6},{9,8},{10,9},{11,10},{13,12},{... | collective-permute-start | bytes 393224 | tf_op jit(solution)/shard_map/ppermute | solution.py:304
  51.3 1.3 %collective-permute-start.11 = (bf16[2,4,128,128]{3,2,1,0:T(8,128)(2,1)S(1)}, bf16[2,4,128,128]{3,2,1,0:T(8,128)(2,1)S(1)}, u32[]{:S(2)}, u32[]{:S(2)}) collective-permute-start(bf16[2,4,128,128]{3,2,1,0:T(8,128)(2,1)S(1)} %get-tuple-element.62), channel_id=1, source_target_pairs={{0,8},{4,12},{8,0},{12,4},{16,24},{20,28},{24,16},{28,20},{1,9},{5... | collective-permute-start | bytes 786440 | tf_op jit(solution)/shard_map/ppermute | solution.py:310
  52.6 1.1 %collective-permute-start.12 = (bf16[2,4,128,128]{3,2,1,0:T(8,128)(2,1)S(1)}, bf16[2,4,128,128]{3,2,1,0:T(8,128)(2,1)S(1)}, u32[]{:S(2)}, u32[]{:S(2)}) collective-permute-start(bf16[2,4,128,128]{3,2,1,0:T(8,128)(2,1)S(1)} %get-tuple-element.63), channel_id=1, source_target_pairs={{0,16},{4,20},{8,24},{12,28},{16,0},{20,4},{24,8},{28,12},{1,17},{... | collective-permute-start | bytes 786440 | tf_op jit(solution)/shard_map/ppermute | solution.py:310
  53.7 1.3 %collective-permute-start.16 = (bf16[4,2,128,128]{3,2,1,0:T(8,128)(2,1)S(1)}, bf16[4,2,128,128]{3,2,1,0:T(8,128)(2,1)S(1)}, u32[]{:S(2)}, u32[]{:S(2)}) collective-permute-start(bf16[4,2,128,128]{3,2,1,0:T(8,128)(2,1)S(1)} %get-tuple-element.67), channel_id=1, source_target_pairs={{1,0},{2,1},{3,2},{5,4},{6,5},{7,6},{9,8},{10,9},{11,10},{13,12},{... | collective-permute-start | bytes 786440 | tf_op jit(solution)/shard_map/ppermute | solution.py:304
  55.0 1.9 %collective-permute-done.17.back = bf16[2,2,128,128]{3,2,1,0:T(8,128)(2,1)S(1)} collective-permute-done((bf16[2,2,128,128]{3,2,1,0:T(8,128)(2,1)S(1)}, bf16[2,2,128,128]{3,2,1,0:T(8,128)(2,1)S(1)}, u32[]{:S(2)}, u32[]{:S(2)}) %collective-permute-start.17) | collective-permute-done | bytes 131104 | tf_op jit(solution)/shard_map/ppermute | solution.py:304
  56.9 1.8 %collective-permute-start.18 = (bf16[2,2,128,128]{3,2,1,0:T(8,128)(2,1)S(1)}, bf16[2,2,128,128]{3,2,1,0:T(8,128)(2,1)S(1)}, u32[]{:S(2)}, u32[]{:S(2)}) collective-permute-start(bf16[2,2,128,128]{3,2,1,0:T(8,128)(2,1)S(1)} %shard_map.105), channel_id=1, source_target_pairs={{0,24},{4,28},{8,16},{12,20},{16,8},{20,12},{24,0},{28,4},{1,25},{... | collective-permute-start | bytes 393224 | tf_op jit(solution)/shard_map/ppermute | solution.py:310
  58.7 1.3 %collective-permute-start.15 = (bf16[2,2,128,128]{3,2,1,0:T(8,128)(2,1)S(1)}, bf16[2,2,128,128]{3,2,1,0:T(8,128)(2,1)S(1)}, u32[]{:S(2)}, u32[]{:S(2)}) collective-permute-start(bf16[2,2,128,128]{3,2,1,0:T(8,128)(2,1)S(1)} %get-tuple-element.66), channel_id=1, source_target_pairs={{1,0},{2,1},{3,2},{5,4},{6,5},{7,6},{9,8},{10,9},{11,10},{13,12},{... | collective-permute-start | bytes 393224 | tf_op jit(solution)/shard_map/ppermute | solution.py:304
  60.0 1.0 %collective-permute-done.12.refs_2_.refs_1_ = bf16[2,4,128,128]{3,2,1,0:T(8,128)(2,1)S(1)} collective-permute-done((bf16[2,4,128,128]{3,2,1,0:T(8,128)(2,1)S(1)}, bf16[2,4,128,128]{3,2,1,0:T(8,128)(2,1)S(1)}, u32[]{:S(2)}, u32[]{:S(2)}) %collective-permute-start.12) | collective-permute-done | bytes 262176 | tf_op jit(solution)/shard_map/ppermute | solution.py:310
  61.1 3.3 %collective-permute-done.16.back = bf16[4,2,128,128]{3,2,1,0:T(8,128)(2,1)S(1)} collective-permute-done((bf16[4,2,128,128]{3,2,1,0:T(8,128)(2,1)S(1)}, bf16[4,2,128,128]{3,2,1,0:T(8,128)(2,1)S(1)}, u32[]{:S(2)}, u32[]{:S(2)}) %collective-permute-start.16) | collective-permute-done | bytes 262176 | tf_op jit(solution)/shard_map/ppermute | solution.py:304
  64.5 1.5 %collective-permute-start.19 = (bf16[2,2,128,128]{3,2,1,0:T(8,128)(2,1)S(1)}, bf16[2,2,128,128]{3,2,1,0:T(8,128)(2,1)S(1)}, u32[]{:S(2)}, u32[]{:S(2)}) collective-permute-start(bf16[2,2,128,128]{3,2,1,0:T(8,128)(2,1)S(1)} %get-tuple-element.69), channel_id=1, source_target_pairs={{0,8},{4,12},{8,0},{12,4},{16,24},{20,28},{24,16},{28,20},{1,9},{5... | collective-permute-start | bytes 393224 | tf_op jit(solution)/shard_map/ppermute | solution.py:310
  66.4 1.5 %shard_map.104.refs_2_ = bf16[128,32,128]{2,1,0:T(8,128)(2,1)} custom-call(s32[1]{0:T(128)} %bitcast.me_ref, bf16[2,4,128,128]{3,2,1,0:T(8,128)(2,1)S(1)} %get-tuple-element.52.refs_0_, bf16[2,4,128,128]{3,2,1,0:T(8,128)(2,1)S(1)} %collective-permute-done.11.refs_1_.refs_0_, bf16[2,4,128,128]{3,2,1,0:T(8,128)(2,1)S(1)} %collective-permute-done.12.refs_2_.refs_1_, ...), custom_call_target="tpu_custom_call" | custom-call | tf_op jit(solution)/shard_map/pallas_call | solution.py:290
  67.9 1.7 %collective-permute-done.19.refs_0_.refs_1_ = bf16[2,2,128,128]{3,2,1,0:T(8,128)(2,1)S(1)} collective-permute-done((bf16[2,2,128,128]{3,2,1,0:T(8,128)(2,1)S(1)}, bf16[2,2,128,128]{3,2,1,0:T(8,128)(2,1)S(1)}, u32[]{:S(2)}, u32[]{:S(2)}) %collective-permute-start.19) | collective-permute-done | bytes 131104 | tf_op jit(solution)/shard_map/ppermute | solution.py:310
  69.6 1.5 %collective-permute-done.20.refs_1_.refs_2_ = bf16[2,2,128,128]{3,2,1,0:T(8,128)(2,1)S(1)} collective-permute-done((bf16[2,2,128,128]{3,2,1,0:T(8,128)(2,1)S(1)}, bf16[2,2,128,128]{3,2,1,0:T(8,128)(2,1)S(1)}, u32[]{:S(2)}, u32[]{:S(2)}) %collective-permute-start.20) | collective-permute-done | bytes 131104 | tf_op jit(solution)/shard_map/ppermute | solution.py:310
  71.2 1.5 %collective-permute-done.21.refs_4_ = bf16[4,2,128,128]{3,2,1,0:T(8,128)(2,1)S(1)} collective-permute-done((bf16[4,2,128,128]{3,2,1,0:T(8,128)(2,1)S(1)}, bf16[4,2,128,128]{3,2,1,0:T(8,128)(2,1)S(1)}, u32[]{:S(2)}, u32[]{:S(2)}) %collective-permute-start.21) | collective-permute-done | bytes 262176 | tf_op jit(solution)/shard_map/ppermute | solution.py:310
  (43 shorter events, 4.7 us)
Async XLA Ops:
  1.8 1.7 %collective-permute-start = (bf16[4,2,128,128]{3,2,1,0:T(8,128)(2,1)S(1)}, bf16[4,2,128,128]{3,2,1,0:T(8,128)(2,1)S(1)}, u32[]{:S(2)}, u32[]{:S(2)}) collective-permute-start(bf16[4,2,128,128]{3,2,1,0:T(8,128)(2,1)S(1)} %get-tuple-element.42), channel_id=1, source_target_pairs={{0,4},{4,0},{8,12},{12,8},{16,20},{20,16},{24,28},{28,24},{1,5},{5... | collective-permute-start | bytes 786440 | tf_op jit(solution)/shard_map/ppermute | solution.py:310
  6.7 17.9 %copy-start.6 = (s32[32,5]{0,1:T(8,128)S(1)}, s32[32,5]{0,1:T(8,128)}, u32[]{:S(2)}) copy-start(s32[32,5]{0,1:T(8,128)} %param.13) | copy-start | bytes 1924
  6.7 11.4 %collective-permute-start.1 = (bf16[4,8,128,128]{3,2,1,0:T(8,128)(2,1)S(1)}, bf16[4,8,128,128]{3,2,1,0:T(8,128)(2,1)S(1)}, u32[]{:S(2)}, u32[]{:S(2)}) collective-permute-start(bf16[4,8,128,128]{3,2,1,0:T(8,128)(2,1)S(1)} %get-tuple-element.46), channel_id=1, source_target_pairs={{0,4},{4,0},{8,12},{12,8},{16,20},{20,16},{24,28},{28,24},{1,5},{5... | collective-permute-start | bytes 3145736 | tf_op jit(solution)/shard_map/ppermute | solution.py:310
  7.2 6.7 %collective-permute-start.2 = (bf16[2,2,128,128]{3,2,1,0:T(8,128)(2,1)S(1)}, bf16[2,2,128,128]{3,2,1,0:T(8,128)(2,1)S(1)}, u32[]{:S(2)}, u32[]{:S(2)}) collective-permute-start(bf16[2,2,128,128]{3,2,1,0:T(8,128)(2,1)S(1)} %get-tuple-element.47), channel_id=1, source_target_pairs={{0,8},{4,12},{8,0},{12,4},{16,24},{20,28},{24,16},{28,20},{1,9},{5... | collective-permute-start | bytes 393224 | tf_op jit(solution)/shard_map/ppermute | solution.py:310
  9.8 8.3 %collective-permute-start.3 = (bf16[2,2,128,128]{3,2,1,0:T(8,128)(2,1)S(1)}, bf16[2,2,128,128]{3,2,1,0:T(8,128)(2,1)S(1)}, u32[]{:S(2)}, u32[]{:S(2)}) collective-permute-start(bf16[2,2,128,128]{3,2,1,0:T(8,128)(2,1)S(1)} %get-tuple-element.48), channel_id=1, source_target_pairs={{0,16},{4,20},{8,24},{12,28},{16,0},{20,4},{24,8},{28,12},{1,17},{... | collective-permute-start | bytes 393224 | tf_op jit(solution)/shard_map/ppermute | solution.py:310
  11.3 6.8 %collective-permute-start.4 = (bf16[2,2,128,128]{3,2,1,0:T(8,128)(2,1)S(1)}, bf16[2,2,128,128]{3,2,1,0:T(8,128)(2,1)S(1)}, u32[]{:S(2)}, u32[]{:S(2)}) collective-permute-start(bf16[2,2,128,128]{3,2,1,0:T(8,128)(2,1)S(1)} %get-tuple-element.49), channel_id=1, source_target_pairs={{0,24},{4,28},{8,16},{12,20},{16,8},{20,12},{24,0},{28,4},{1,25},{... | collective-permute-start | bytes 393224 | tf_op jit(solution)/shard_map/ppermute | solution.py:310
  18.2 0.7 copy-start.4
  18.8 0.7 copy-start.5
  19.6 15.8 %collective-permute-start.5 = (bf16[2,8,128,128]{3,2,1,0:T(8,128)(2,1)S(1)}, bf16[2,8,128,128]{3,2,1,0:T(8,128)(2,1)S(1)}, u32[]{:S(2)}, u32[]{:S(2)}) collective-permute-start(bf16[2,8,128,128]{3,2,1,0:T(8,128)(2,1)S(1)} %get-tuple-element.51), channel_id=1, source_target_pairs={{0,24},{4,28},{8,16},{12,20},{16,8},{20,12},{24,0},{28,4},{1,25},{... | collective-permute-start | bytes 1572872 | tf_op jit(solution)/shard_map/ppermute | solution.py:310
  21.1 15.8 %collective-permute-start.6 = (bf16[8,2,128,128]{3,2,1,0:T(8,128)(2,1)S(1)}, bf16[8,2,128,128]{3,2,1,0:T(8,128)(2,1)S(1)}, u32[]{:S(2)}, u32[]{:S(2)}) collective-permute-start(bf16[8,2,128,128]{3,2,1,0:T(8,128)(2,1)S(1)} %shard_map.99.refs_2_), channel_id=1, source_target_pairs={{0,1},{1,2},{2,3},{4,5},{5,6},{6,7},{8,9},{9,10},{10,11},{12,13},{... | collective-permute-start | bytes 1572872 | tf_op jit(solution)/shard_map/ppermute | solution.py:304
  24.7 19.3 %collective-permute-start.9 = (bf16[1,8,128,128]{3,2,1,0:T(8,128)(2,1)}, bf16[1,8,128,128]{3,2,1,0:T(8,128)(2,1)S(1)}, u32[]{:S(2)}, u32[]{:S(2)}) collective-permute-start(bf16[1,8,128,128]{3,2,1,0:T(8,128)(2,1)} %get-tuple-element.55), channel_id=1, source_target_pairs={{0,8},{4,12},{8,0},{12,4},{16,24},{20,28},{24,16},{28,20},{1,9},{5... | collective-permute-start | bytes 786440 | tf_op jit(solution)/shard_map/ppermute | solution.py:310
  26.2 17.8 %collective-permute-start.10 = (bf16[1,8,128,128]{3,2,1,0:T(8,128)(2,1)}, bf16[1,8,128,128]{3,2,1,0:T(8,128)(2,1)S(1)}, u32[]{:S(2)}, u32[]{:S(2)}) collective-permute-start(bf16[1,8,128,128]{3,2,1,0:T(8,128)(2,1)} %get-tuple-element.56), channel_id=1, source_target_pairs={{0,16},{4,20},{8,24},{12,28},{16,0},{20,4},{24,8},{28,12},{1,17},{... | collective-permute-start | bytes 786440 | tf_op jit(solution)/shard_map/ppermute | solution.py:310
  26.7 20.2 %collective-permute-start.7 = (bf16[1,8,128,128]{3,2,1,0:T(8,128)(2,1)}, bf16[1,8,128,128]{3,2,1,0:T(8,128)(2,1)S(1)}, u32[]{:S(2)}, u32[]{:S(2)}) collective-permute-start(bf16[1,8,128,128]{3,2,1,0:T(8,128)(2,1)} %copy-done.5), channel_id=1, source_target_pairs={{0,8},{4,12},{8,0},{12,4},{16,24},{20,28},{24,16},{28,20},{1,9},{5... | collective-permute-start | bytes 786440 | tf_op jit(solution)/shard_map/ppermute | solution.py:310
  35.4 1.5 %copy-start.2 = (bf16[2,8,128,128]{3,2,1,0:T(8,128)(2,1)}, bf16[2,8,128,128]{3,2,1,0:T(8,128)(2,1)S(1)}, u32[]{:S(2)}) copy-start(bf16[2,8,128,128]{3,2,1,0:T(8,128)(2,1)S(1)} %collective-permute-done.5.refs_0_) | copy-start | bytes 1572868
  35.4 1.5 %copy-start = (f32[4,4096]{1,0:T(4,128)S(1)}, f32[4,4096]{1,0:T(4,128)}, u32[]{:S(2)}) copy-start(f32[4,4096]{1,0:T(4,128)} %lse_ref.5) | copy-start | bytes 196612
  35.4 1.5 %copy-start.1 = (f32[4,4096]{1,0:T(4,128)S(1)}, f32[4,4096]{1,0:T(4,128)}, u32[]{:S(2)}) copy-start(f32[4,4096]{1,0:T(4,128)} %delta_ref.5) | copy-start | bytes 196612
  35.4 11.6 %collective-permute-start.8 = (bf16[1,8,128,128]{3,2,1,0:T(8,128)(2,1)}, bf16[1,8,128,128]{3,2,1,0:T(8,128)(2,1)S(1)}, u32[]{:S(2)}, u32[]{:S(2)}) collective-permute-start(bf16[1,8,128,128]{3,2,1,0:T(8,128)(2,1)} %copy-done.4), channel_id=1, source_target_pairs={{0,16},{4,20},{8,24},{12,28},{16,0},{20,4},{24,8},{28,12},{1,17},{... | collective-permute-start | bytes 786440 | tf_op jit(solution)/shard_map/ppermute | solution.py:310
  36.9 1.0 %copy-start.3 = (bf16[2,8,128,128]{3,2,1,0:T(8,128)(2,1)S(1)}, bf16[2,8,128,128]{3,2,1,0:T(8,128)(2,1)}, u32[]{:S(2)}) copy-start(bf16[2,8,128,128]{3,2,1,0:T(8,128)(2,1)} %shard_map.98.refs_1_) | copy-start | bytes 1572868
  42.7 14.1 %collective-permute-start.13 = (bf16[2,4,128,128]{3,2,1,0:T(8,128)(2,1)S(1)}, bf16[2,4,128,128]{3,2,1,0:T(8,128)(2,1)S(1)}, u32[]{:S(2)}, u32[]{:S(2)}) collective-permute-start(bf16[2,4,128,128]{3,2,1,0:T(8,128)(2,1)S(1)} %get-tuple-element.64), channel_id=1, source_target_pairs={{0,24},{4,28},{8,16},{12,20},{16,8},{20,12},{24,0},{28,4},{1,25},{... | collective-permute-start | bytes 786440 | tf_op jit(solution)/shard_map/ppermute | solution.py:310
  50.0 6.9 %collective-permute-start.17 = (bf16[2,2,128,128]{3,2,1,0:T(8,128)(2,1)S(1)}, bf16[2,2,128,128]{3,2,1,0:T(8,128)(2,1)S(1)}, u32[]{:S(2)}, u32[]{:S(2)}) collective-permute-start(bf16[2,2,128,128]{3,2,1,0:T(8,128)(2,1)S(1)} %get-tuple-element.68), channel_id=1, source_target_pairs={{1,0},{2,1},{3,2},{5,4},{6,5},{7,6},{9,8},{10,9},{11,10},{13,12},{... | collective-permute-start | bytes 393224 | tf_op jit(solution)/shard_map/ppermute | solution.py:304
  51.3 8.7 %collective-permute-start.11 = (bf16[2,4,128,128]{3,2,1,0:T(8,128)(2,1)S(1)}, bf16[2,4,128,128]{3,2,1,0:T(8,128)(2,1)S(1)}, u32[]{:S(2)}, u32[]{:S(2)}) collective-permute-start(bf16[2,4,128,128]{3,2,1,0:T(8,128)(2,1)S(1)} %get-tuple-element.62), channel_id=1, source_target_pairs={{0,8},{4,12},{8,0},{12,4},{16,24},{20,28},{24,16},{28,20},{1,9},{5... | collective-permute-start | bytes 786440 | tf_op jit(solution)/shard_map/ppermute | solution.py:310
  52.6 8.4 %collective-permute-start.12 = (bf16[2,4,128,128]{3,2,1,0:T(8,128)(2,1)S(1)}, bf16[2,4,128,128]{3,2,1,0:T(8,128)(2,1)S(1)}, u32[]{:S(2)}, u32[]{:S(2)}) collective-permute-start(bf16[2,4,128,128]{3,2,1,0:T(8,128)(2,1)S(1)} %get-tuple-element.63), channel_id=1, source_target_pairs={{0,16},{4,20},{8,24},{12,28},{16,0},{20,4},{24,8},{28,12},{1,17},{... | collective-permute-start | bytes 786440 | tf_op jit(solution)/shard_map/ppermute | solution.py:310
  53.7 10.8 %collective-permute-start.16 = (bf16[4,2,128,128]{3,2,1,0:T(8,128)(2,1)S(1)}, bf16[4,2,128,128]{3,2,1,0:T(8,128)(2,1)S(1)}, u32[]{:S(2)}, u32[]{:S(2)}) collective-permute-start(bf16[4,2,128,128]{3,2,1,0:T(8,128)(2,1)S(1)} %get-tuple-element.67), channel_id=1, source_target_pairs={{1,0},{2,1},{3,2},{5,4},{6,5},{7,6},{9,8},{10,9},{11,10},{13,12},{... | collective-permute-start | bytes 786440 | tf_op jit(solution)/shard_map/ppermute | solution.py:304
  56.9 7.6 %collective-permute-start.18 = (bf16[2,2,128,128]{3,2,1,0:T(8,128)(2,1)S(1)}, bf16[2,2,128,128]{3,2,1,0:T(8,128)(2,1)S(1)}, u32[]{:S(2)}, u32[]{:S(2)}) collective-permute-start(bf16[2,2,128,128]{3,2,1,0:T(8,128)(2,1)S(1)} %shard_map.105), channel_id=1, source_target_pairs={{0,24},{4,28},{8,16},{12,20},{16,8},{20,12},{24,0},{28,4},{1,25},{... | collective-permute-start | bytes 393224 | tf_op jit(solution)/shard_map/ppermute | solution.py:310
  58.7 9.2 %collective-permute-start.15 = (bf16[2,2,128,128]{3,2,1,0:T(8,128)(2,1)S(1)}, bf16[2,2,128,128]{3,2,1,0:T(8,128)(2,1)S(1)}, u32[]{:S(2)}, u32[]{:S(2)}) collective-permute-start(bf16[2,2,128,128]{3,2,1,0:T(8,128)(2,1)S(1)} %get-tuple-element.66), channel_id=1, source_target_pairs={{1,0},{2,1},{3,2},{5,4},{6,5},{7,6},{9,8},{10,9},{11,10},{13,12},{... | collective-permute-start | bytes 393224 | tf_op jit(solution)/shard_map/ppermute | solution.py:304
  61.1 5.3 %collective-permute-start.14 = (bf16[4,4,128,128]{3,2,1,0:T(8,128)(2,1)S(1)}, bf16[4,4,128,128]{3,2,1,0:T(8,128)(2,1)S(1)}, u32[]{:S(2)}, u32[]{:S(2)}) collective-permute-start(bf16[4,4,128,128]{3,2,1,0:T(8,128)(2,1)S(1)} %shard_map.103), channel_id=1, source_target_pairs={{0,4},{4,0},{8,12},{12,8},{16,20},{20,16},{24,28},{28,24},{1,5},{5... | collective-permute-start | bytes 1572872 | tf_op jit(solution)/shard_map/ppermute | solution.py:310
  64.5 5.0 %collective-permute-start.19 = (bf16[2,2,128,128]{3,2,1,0:T(8,128)(2,1)S(1)}, bf16[2,2,128,128]{3,2,1,0:T(8,128)(2,1)S(1)}, u32[]{:S(2)}, u32[]{:S(2)}) collective-permute-start(bf16[2,2,128,128]{3,2,1,0:T(8,128)(2,1)S(1)} %get-tuple-element.69), channel_id=1, source_target_pairs={{0,8},{4,12},{8,0},{12,4},{16,24},{20,28},{24,16},{28,20},{1,9},{5... | collective-permute-start | bytes 393224 | tf_op jit(solution)/shard_map/ppermute | solution.py:310
  66.0 5.0 %collective-permute-start.20 = (bf16[2,2,128,128]{3,2,1,0:T(8,128)(2,1)S(1)}, bf16[2,2,128,128]{3,2,1,0:T(8,128)(2,1)S(1)}, u32[]{:S(2)}, u32[]{:S(2)}) collective-permute-start(bf16[2,2,128,128]{3,2,1,0:T(8,128)(2,1)S(1)} %get-tuple-element.70), channel_id=1, source_target_pairs={{0,16},{4,20},{8,24},{12,28},{16,0},{20,4},{24,8},{28,12},{1,17},{... | collective-permute-start | bytes 393224 | tf_op jit(solution)/shard_map/ppermute | solution.py:310
  71.1 1.6 %collective-permute-start.21 = (bf16[4,2,128,128]{3,2,1,0:T(8,128)(2,1)S(1)}, bf16[4,2,128,128]{3,2,1,0:T(8,128)(2,1)S(1)}, u32[]{:S(2)}, u32[]{:S(2)}) collective-permute-start(bf16[4,2,128,128]{3,2,1,0:T(8,128)(2,1)S(1)} %shard_map.108), channel_id=1, source_target_pairs={{0,4},{4,0},{8,12},{12,8},{16,20},{20,16},{24,28},{28,24},{1,5},{5... | collective-permute-start | bytes 786440 | tf_op jit(solution)/shard_map/ppermute | solution.py:310

commit v4 on v3

--- a/solution.py
+++ b/solution.py
@@ -123,14 +123,14 @@
     )(slab, me, block_keys, *operands)
 
 
-def pack_kernel(fold_counts, after_count, me_ref, *refs):
+def pack_kernel(devices, fold_counts, kept, given, after_count, me_ref, *refs):
     count = len(fold_counts)
-    chips = refs[-1 - 2 * count - 1].shape[0]
     sources, refs = refs[:count], refs[count + after_count :]
-    pieces, give, refs = refs[:chips], refs[chips], refs[chips + 1 :]
+    pieces, gives, refs = refs[: len(kept)], refs[len(kept) : len(kept) + len(given)], refs[len(kept) + len(given) :]
     by_token, by_head, sems = refs[:count], refs[count : 2 * count], refs[-1]
-    devices = 2 * chips
     me = me_ref[0]
+    targets = [(piece.at[0], 2 * m) for piece, m in zip(pieces, kept)]
+    targets += [(give.at[i], 2 * m + 1) for give, group in zip(gives, given) for i, m in enumerate(group)]
     copies = [pltpu.make_async_copy(sources[i], by_token[i], sems.at[i]) for i in range(count)]
     for copy in copies:
         copy.start()
@@ -139,23 +139,23 @@
         copy.wait()
         target[...] = jnp.swapaxes(source[...], 0, 1)
         heads = target.shape[0] * fold_count // devices
-        for m in range(chips):
-            for out, j in ((pieces[m].at[0], 0), (give.at[m], 1)):
-                device = me ^ (2 * m + j)
-                out[at : at + heads] = target[pl.ds(device // fold_count * heads, heads)]
+        for out, slot in targets:
+            device = me ^ slot
+            out[at : at + heads] = target[pl.ds(device // fold_count * heads, heads)]
         at += heads
 
 
-def packed(me, arrays, fold_counts, uly_count, whole, after):
+def packed(me, arrays, fold_counts, uly_count, kept, rows, given, after):
     tokens, _, head_dim = arrays[0].shape
-    chips = uly_count // 2
     tiles = sum(x.shape[1] * fold_count for x, fold_count in zip(arrays, fold_counts)) // uly_count
     vmem = pl.BlockSpec(memory_space=pltpu.VMEM)
-    shapes = [jax.ShapeDtypeStruct((2 if m in whole else 1, tiles, tokens, head_dim), arrays[0].dtype) for m in range(chips)]
-    shapes.append(jax.ShapeDtypeStruct((chips, tiles, tokens, head_dim), arrays[0].dtype))
-    *pieces, give = pl.pallas_call(
-        functools.partial(pack_kernel, fold_counts, len(after)),
-        in_specs=[pl.BlockSpec(memory_space=pltpu.SMEM)] + [pl.BlockSpec(memory_space=pltpu.HBM)] * len(arrays) + [pl.BlockSpec(memory_space=pl.ANY)] * len(after),
+    counts = [rows] * len(kept) + [len(group) for group in given]
+    shapes = [jax.ShapeDtypeStruct((count, tiles, tokens, head_dim), arrays[0].dtype) for count in counts]
+    return pl.pallas_call(
+        functools.partial(pack_kernel, uly_count, fold_counts, kept, given, len(after)),
+        in_specs=[pl.BlockSpec(memory_space=pltpu.SMEM)]
+        + [pl.BlockSpec(memory_space=pltpu.HBM)] * len(arrays)
+        + [pl.BlockSpec(memory_space=pl.ANY)] * len(after),
         out_specs=[vmem] * len(shapes),
         out_shape=shapes,
         scratch_shapes=[pltpu.VMEM(x.shape, x.dtype) for x in arrays]
@@ -163,31 +163,25 @@
         + [pltpu.SemaphoreType.DMA((len(arrays),))],
         compiler_params=pltpu.CompilerParams(vmem_limit_bytes=8 * 1024 * 1024),
     )(me, *[pltpu.with_memory_space_constraint(x, pltpu.HBM) for x in arrays], *after)
-    return pieces, give
-
-
-def merge_kernel(whole, chips, count, *refs):
-    got, outs = refs[len(whole)], refs[-count:]
-    for m, out in zip(whole, outs):
-        out[1] = got[m]
-    for m, out in zip([m for m in range(chips) if m not in whole], outs[len(whole) :]):
-        out[0] = got[m]
-
-
-def merged(pieces, whole, got, after):
-    chips = got.shape[0]
-    apart = chips - len(whole)
-    vmem = pl.BlockSpec(memory_space=pltpu.VMEM)
-    shapes = [jax.ShapeDtypeStruct(pieces[m].shape, got.dtype) for m in whole]
-    shapes += [jax.ShapeDtypeStruct((1, *got.shape[1:]), got.dtype)] * apart
-    return pl.pallas_call(
-        functools.partial(merge_kernel, whole, chips, len(shapes)),
-        in_specs=[vmem] * (len(whole) + 1) + [pl.BlockSpec(memory_space=pl.ANY)] * len(after),
-        out_specs=[vmem] * chips,
-        out_shape=shapes,
-        input_output_aliases={i: i for i in range(len(whole))},
+
+
+def merge_kernel(count, *refs):
+    got, outs = refs[count], refs[-count:]
+    for i, out in enumerate(outs):
+        out[1] = got[i]
+
+
+def merged(pieces, got, after):
+    count = len(pieces)
+    vmem = pl.BlockSpec(memory_space=pltpu.VMEM)
+    return pl.pallas_call(
+        functools.partial(merge_kernel, count),
+        in_specs=[vmem] * (count + 1) + [pl.BlockSpec(memory_space=pl.ANY)] * len(after),
+        out_specs=[vmem] * count,
+        out_shape=[jax.ShapeDtypeStruct(x.shape, x.dtype) for x in pieces],
+        input_output_aliases={i: i for i in range(count)},
         compiler_params=pltpu.CompilerParams(vmem_limit_bytes=8 * 1024 * 1024),
-    )(*[held(pieces[m]) for m in whole], got, *after)
+    )(*map(held, pieces), got, *after)
 
 
 def landed_kernel(*refs):
@@ -321,15 +315,17 @@
     slab = lax.axis_index("blk").reshape(1)
 
     every, ends, mids = list(range(chips)), [0, far], list(range(1, far))
-    kv_pieces, give_kv = packed(me, [keys, values], [fold_count] * 2, uly_count, every, [])
-    merged_kv = merged(kv_pieces, every, swapped(give_kv, 1), [])
+    *kv_pieces, give_kv = packed(me, [keys, values], [fold_count] * 2, uly_count, every, 2, [every], [])
+    merged_kv = merged(kv_pieces, swapped(give_kv, 1), [])
     kv_pieces = [swapped(piece, 2 * m) for m, piece in enumerate(merged_kv)]
     own = joined(kv_pieces)
-    qd_pieces, give_qd = packed(me, [queries, grad_out], [1] * 2, uly_count, ends, merged_kv[:1])
-    qd_here, qd_far, *seconds = merged(qd_pieces, ends, swapped(give_qd, 1), kv_pieces[1:])
+    pack = functools.partial(packed, me, [queries, grad_out], [1] * 2, uly_count)
+    *qd_ends, give_ends, give_mids = pack(ends, 2, [ends, mids], merged_kv[:1])
+    qd_here, qd_far = merged(qd_ends, swapped(give_ends, 1), kv_pieces[1:])
     qd_far = landed(swapped(qd_far, 2 * far), [], SHORT)
-    firsts = [swapped(qd_pieces[m], 2 * m) for m in mids]
-    seconds = [swapped(piece, 2 * m) for m, piece in zip(mids, seconds)]
+    got_mids = swapped(give_mids, 1)
+    firsts = [swapped(piece, 2 * m) for m, piece in zip(mids, pack(mids, 1, [], [own]))]
+    seconds = [swapped(got_mids[i : i + 1], 2 * m) for i, m in enumerate(mids)]
     prev = passed_along(own, "blk", 1)
 
     grads = functools.partial(block_grads, slab=slab, me=me, block_keys=block_keys, lse=lse, delta=delta)

time: 73.9 us -> 71.1 us (0.962)
  waiting for transfers between devices: 26.2 us -> 21.5 us
  Pallas kernels: 17.8 us -> 20.4 us
  local copies, waits for them, and re-layouts: 2.53 us -> 1.17 us
    ppermute x18 -> x19, waiting for transfers between devices: 21 us -> 16.8 us  [swapped(): lax.ppermute(block, 'uly', [(i, i ^ k) for i in range(lax.axis_size('uly'...]
    unnamed x15 -> x7, local copies, waits for them, and re-layouts: 2.53 us -> 0.1 us
    pallas_call x4 -> x5, Pallas kernels: 4.43 us -> 6.64 us  [the longest x3 6.58 us: packed(): pl.pallas_call(functools.partial(pack_kernel, uly_count, fold_counts, kep...]
    slice x0 -> x1, local copies, waits for them, and re-layouts: none -> 1.07 us  [shards(): seconds = [swapped(got_mids[i:i + 1], 2 * m) for i, m in enumerate(mids)]]
    ppermute x18 -> x19, starting transfers between devices: 18.8 us -> 19.5 us  [swapped(): lax.ppermute(block, 'uly', [(i, i ^ k) for i in range(lax.axis_size('uly'...]
  transfers between devices with their start and end apart: 22 -> 23, of which waited for: 10 -> 10; matrix products, arithmetic and copies ran while one was open for 0% -> 2% of each run, Pallas kernels for 17% -> 22%
where the time goes in v4:
time: 71.1 us; the launch traced here: 70.8 us
  starting transfers between devices  26.9 us (38%)
  waiting for transfers between devices  21.5 us (30%)
  Pallas kernels  20.4 us (29%)
  local copies, waits for them, and re-layouts  1.17 us (2%)
  between operations  0.85 us (1%)
    ppermute x19, starting transfers between devices, swapped(): lax.ppermute(block, 'uly', [(i, i ^ k) for i in range(lax.axis_size('uly'...  19.5 us
    ppermute x19, waiting for transfers between devices, swapped(): lax.ppermute(block, 'uly', [(i, i ^ k) for i in range(lax.axis_size('uly'...  16.8 us
    pallas_call x3, Pallas kernels, block_grads(): pl.pallas_call(functools.partial(block_kernel, blocks, len(out_rows), len...  11.1 us
    ppermute x4, starting transfers between devices, passed_along(): lax.ppermute(block, axis, [(i - distance, i) for i in devices if i - dist...  7.37 us
    pallas_call x3, Pallas kernels, packed(): pl.pallas_call(functools.partial(pack_kernel, uly_count, fold_counts, kep...  6.58 us
    ppermute x4, waiting for transfers between devices, passed_along(): lax.ppermute(block, axis, [(i - distance, i) for i in devices if i - dist...  4.7 us
    pallas_call x2, Pallas kernels, unpacked(): pl.pallas_call(functools.partial(unpack_kernel, chips, fold_count), in_sp...  2.38 us
  transfers between devices with their start and end apart: 23, of which 10 were waited for; matrix products, arithmetic and copies ran while one was open for 2% of the time, Pallas kernels for 22%

profile of v4, /device:TPU:0, one launch (start us, length us, event | category | flops | bytes accessed | tf_op | source)
XLA Modules:
  0.0 70.8 jit_solution(8803215455504264655)
XLA Ops:
  0.6 1.2 %shard_map.94 = (bf16[2,2,128,128]{3,2,1,0:T(8,128)(2,1)S(1)}, bf16[2,2,128,128]{3,2,1,0:T(8,128)(2,1)S(1)}, bf16[2,2,128,128]{3,2,1,0:T(8,128)(2,1)S(1)}, bf16[...) custom-call(s32[1]{0:T(128)} %bitcast.me_ref, bf16[128,8,128]{2,1,0:T(8,128)(2,1)} %refs_0_.3, ...), custom_call_target="tpu_custom_call" | custom-call | tf_op jit(solution)/shard_map/pallas_call | solution.py:154
  2.3 1.2 %collective-permute-done.refs_4_ = bf16[4,2,128,128]{3,2,1,0:T(8,128)(2,1)S(1)} collective-permute-done((bf16[4,2,128,128]{3,2,1,0:T(8,128)(2,1)S(1)}, bf16[4,2,128,128]{3,2,1,0:T(8,128)(2,1)S(1)}, u32[]{:S(2)}, u32[]{:S(2)}) %collective-permute-start) | collective-permute-done | bytes 262176 | tf_op jit(solution)/shard_map/ppermute | solution.py:304
  3.5 2.3 %shard_map.96 = (bf16[2,8,128,128]{3,2,1,0:T(8,128)(2,1)S(1)}, bf16[2,8,128,128]{3,2,1,0:T(8,128)(2,1)S(1)}, bf16[2,8,128,128]{3,2,1,0:T(8,128)(2,1)S(1)}, bf16[2,8,128,128]{3,2,1,0:T(8,128)(2,1)S(1)}) custom-call(s32[1]{0:T(128)} %bitcast.me_ref, bf16[128,32,128]{2,1,0:T(8,128)(2,1)} %refs_0_.5, bf16[128,32,128]{2,1,0:T(8,128)(2,1)} %refs_1_.5, ...), custom_call_target="tpu_custom_call" | custom-call | tf_op jit(solution)/shard_map/pallas_call | solution.py:154
  6.5 2.9 %collective-permute-start.2 = (bf16[2,2,128,128]{3,2,1,0:T(8,128)(2,1)S(1)}, bf16[2,2,128,128]{3,2,1,0:T(8,128)(2,1)S(1)}, u32[]{:S(2)}, u32[]{:S(2)}) collective-permute-start(bf16[2,2,128,128]{3,2,1,0:T(8,128)(2,1)S(1)} %get-tuple-element.46), channel_id=1, source_target_pairs={{0,8},{4,12},{8,0},{12,4},{16,24},{20,28},{24,16},{28,20},{1,9},{5... | collective-permute-start | bytes 393224 | tf_op jit(solution)/shard_map/ppermute | solution.py:304
  9.3 1.5 %collective-permute-start.3 = (bf16[2,2,128,128]{3,2,1,0:T(8,128)(2,1)S(1)}, bf16[2,2,128,128]{3,2,1,0:T(8,128)(2,1)S(1)}, u32[]{:S(2)}, u32[]{:S(2)}) collective-permute-start(bf16[2,2,128,128]{3,2,1,0:T(8,128)(2,1)S(1)} %get-tuple-element.47), channel_id=1, source_target_pairs={{0,16},{4,20},{8,24},{12,28},{16,0},{20,4},{24,8},{28,12},{1,17},{... | collective-permute-start | bytes 393224 | tf_op jit(solution)/shard_map/ppermute | solution.py:304
  10.9 2.4 %collective-permute-done.2.refs_3_.refs_1_ = bf16[2,2,128,128]{3,2,1,0:T(8,128)(2,1)S(1)} collective-permute-done((bf16[2,2,128,128]{3,2,1,0:T(8,128)(2,1)S(1)}, bf16[2,2,128,128]{3,2,1,0:T(8,128)(2,1)S(1)}, u32[]{:S(2)}, u32[]{:S(2)}) %collective-permute-start.2) | collective-permute-done | bytes 131104 | tf_op jit(solution)/shard_map/ppermute | solution.py:304
  13.2 4.2 %collective-permute-done.3.refs_4_.refs_2_ = bf16[2,2,128,128]{3,2,1,0:T(8,128)(2,1)S(1)} collective-permute-done((bf16[2,2,128,128]{3,2,1,0:T(8,128)(2,1)S(1)}, bf16[2,2,128,128]{3,2,1,0:T(8,128)(2,1)S(1)}, u32[]{:S(2)}, u32[]{:S(2)}) %collective-permute-start.3) | collective-permute-done | bytes 131104 | tf_op jit(solution)/shard_map/ppermute | solution.py:304
  17.4 1.6 %collective-permute-start.5 = (bf16[2,8,128,128]{3,2,1,0:T(8,128)(2,1)S(1)}, bf16[2,8,128,128]{3,2,1,0:T(8,128)(2,1)}, u32[]{:S(2)}, u32[]{:S(2)}) collective-permute-start(bf16[2,8,128,128]{3,2,1,0:T(8,128)(2,1)S(1)} %get-tuple-element.50), channel_id=1, source_target_pairs={{0,24},{4,28},{8,16},{12,20},{16,8},{20,12},{24,0},{28,4},{1,25},{... | collective-permute-start | bytes 1572872 | tf_op jit(solution)/shard_map/ppermute | solution.py:304
  19.0 3.5 %collective-permute-start.6 = (bf16[8,2,128,128]{3,2,1,0:T(8,128)(2,1)S(1)}, bf16[8,2,128,128]{3,2,1,0:T(8,128)(2,1)S(1)}, u32[]{:S(2)}, u32[]{:S(2)}) collective-permute-start(bf16[8,2,128,128]{3,2,1,0:T(8,128)(2,1)S(1)} %shard_map.99.refs_2_), channel_id=1, source_target_pairs={{0,1},{1,2},{2,3},{4,5},{5,6},{6,7},{8,9},{9,10},{10,11},{12,13},{... | collective-permute-start | bytes 1572872 | tf_op jit(solution)/shard_map/ppermute | solution.py:298
  22.7 3.1 %shard_map.101 = (bf16[1,8,128,128]{3,2,1,0:T(8,128)(2,1)}, bf16[1,8,128,128]{3,2,1,0:T(8,128)(2,1)}) custom-call(s32[1]{0:T(128)} %bitcast.me_ref, bf16[128,32,128]{2,1,0:T(8,128)(2,1)} %refs_0_.5, bf16[128,32,128]{2,1,0:T(8,128)(2,1)} %refs_1_.5, bf16[8,2,128,128]{3,2,1,0:T(8,128)(2,1)S(1)} %shard_map.99.refs_2_), custom_call_target="tpu_custom_call" | custom-call | tf_op jit(solution)/shard_map/pallas_call | solution.py:154
  25.7 1.6 %collective-permute-start.10 = (bf16[1,8,128,128]{3,2,1,0:T(8,128)(2,1)}, bf16[1,8,128,128]{3,2,1,0:T(8,128)(2,1)S(1)}, u32[]{:S(2)}, u32[]{:S(2)}) collective-permute-start(bf16[1,8,128,128]{3,2,1,0:T(8,128)(2,1)} %get-tuple-element.53), channel_id=1, source_target_pairs={{0,8},{4,12},{8,0},{12,4},{16,24},{20,28},{24,16},{28,20},{1,9},{5... | collective-permute-start | bytes 786440 | tf_op jit(solution)/shard_map/ppermute | solution.py:304
  27.8 1.1 %fusion = (bf16[1,8,128,128]{3,2,1,0:T(8,128)(2,1)S(1)}, bf16[1,8,128,128]{3,2,1,0:T(8,128)(2,1)S(1)}) fusion(bf16[2,8,128,128]{3,2,1,0:T(8,128)(2,1)} %collective-permute-done.7), kind=kLoop, calls=%fused_computation | loop fusion | bytes 1048576 | tf_op jit(solution)/shard_map/slice | solution.py:328
  28.9 1.6 %collective-permute-start.9 = (bf16[1,8,128,128]{3,2,1,0:T(8,128)(2,1)S(1)}, bf16[1,8,128,128]{3,2,1,0:T(8,128)(2,1)S(1)}, u32[]{:S(2)}, u32[]{:S(2)}) collective-permute-start(bf16[1,8,128,128]{3,2,1,0:T(8,128)(2,1)S(1)} %get-tuple-element.71), channel_id=1, source_target_pairs={{0,16},{4,20},{8,24},{12,28},{16,0},{20,4},{24,8},{28,12},{1,17},{... | collective-permute-start | bytes 786440 | tf_op jit(solution)/shard_map/ppermute | solution.py:304
  30.5 2.9 %collective-permute-done.5.refs_0_ = bf16[2,8,128,128]{3,2,1,0:T(8,128)(2,1)} collective-permute-done((bf16[2,8,128,128]{3,2,1,0:T(8,128)(2,1)S(1)}, bf16[2,8,128,128]{3,2,1,0:T(8,128)(2,1)}, u32[]{:S(2)}, u32[]{:S(2)}) %collective-permute-start.5) | collective-permute-done | bytes 524320 | tf_op jit(solution)/shard_map/ppermute | solution.py:304
  33.4 1.3 %collective-permute-start.8 = (bf16[1,8,128,128]{3,2,1,0:T(8,128)(2,1)S(1)}, bf16[1,8,128,128]{3,2,1,0:T(8,128)(2,1)S(1)}, u32[]{:S(2)}, u32[]{:S(2)}) collective-permute-start(bf16[1,8,128,128]{3,2,1,0:T(8,128)(2,1)S(1)} %get-tuple-element.72), channel_id=1, source_target_pairs={{0,8},{4,12},{8,0},{12,4},{16,24},{20,28},{24,16},{28,20},{1,9},{5... | collective-permute-start | bytes 786440 | tf_op jit(solution)/shard_map/ppermute | solution.py:304
  34.7 5.1 %shard_map.100 = (bf16[2,4,128,128]{3,2,1,0:T(8,128)(2,1)S(1)}, bf16[2,4,128,128]{3,2,1,0:T(8,128)(2,1)S(1)}, bf16[16,2,128,128]{3,2,1,0:T(8,128)(2,1)S(1)}, f32[16,2,128,128]{3,2,1,0:T(8,128)S(1)}) custom-call(s32[1]{0:T(128)} %bitcast.1.slab_ref, s32[1]{0:T(128)} %bitcast.me_ref, s32[32,5]{1,0:T(8,128)S(1)} %copy.17.keys_ref, f32[4,4096]{1,0:T(4,128)S(1)} %copy-done, ...), custom_call_target="tpu_custom_call" | custom-call | flops 1677721600 | bytes 8388608 | tf_op jit(solution)/shard_map/pallas_call | solution.py:115
  39.8 1.8 %collective-permute-start.14 = (bf16[2,4,128,128]{3,2,1,0:T(8,128)(2,1)S(1)}, bf16[2,4,128,128]{3,2,1,0:T(8,128)(2,1)S(1)}, u32[]{:S(2)}, u32[]{:S(2)}) collective-permute-start(bf16[2,4,128,128]{3,2,1,0:T(8,128)(2,1)S(1)} %get-tuple-element.62), channel_id=1, source_target_pairs={{0,24},{4,28},{8,16},{12,20},{16,8},{20,12},{24,0},{28,4},{1,25},{... | collective-permute-start | bytes 786440 | tf_op jit(solution)/shard_map/ppermute | solution.py:304
  41.6 3.0 %shard_map.102 = (bf16[1,4,128,128]{3,2,1,0:T(8,128)(2,1)S(1)}, bf16[1,4,128,128]{3,2,1,0:T(8,128)(2,1)S(1)}, f32[16,2,128,128]{3,2,1,0:T(8,128)S(1)}) custom-call(s32[1]{0:T(128)} %bitcast.1.slab_ref, s32[1]{0:T(128)} %bitcast.me_ref, s32[32,5]{1,0:T(8,128)S(1)} %copy.17.keys_ref, f32[4,4096]{1,0:T(4,128)S(1)} %copy-done, f32[4,4096]{1,0:T(4,128)S(1)} %copy-done.1, ...), custom_call_target="tpu_custom_call" | custom-call | flops 838860800 | bytes 8388608 | tf_op jit(solution)/shard_map/pallas_call | solution.py:115
  44.6 3.1 %shard_map.103 = (bf16[2,4,128,128]{3,2,1,0:T(8,128)(2,1)S(1)}, bf16[2,4,128,128]{3,2,1,0:T(8,128)(2,1)S(1)}, f32[8,2,128,128]{3,2,1,0:T(8,128)S(1)}, bf16[2,2,1...) custom-call(s32[1]{0:T(128)} %bitcast.1.slab_ref, ...), custom_call_target="tpu_custom_call" | custom-call | flops 838860800 | bytes 8388608 | tf_op jit(solution)/shard_map/pallas_call | solution.py:115
  47.7 1.3 %collective-permute-start.18 = (bf16[2,2,128,128]{3,2,1,0:T(8,128)(2,1)S(1)}, bf16[2,2,128,128]{3,2,1,0:T(8,128)(2,1)S(1)}, u32[]{:S(2)}, u32[]{:S(2)}) collective-permute-start(bf16[2,2,128,128]{3,2,1,0:T(8,128)(2,1)S(1)} %get-tuple-element.66), channel_id=1, source_target_pairs={{1,0},{2,1},{3,2},{5,4},{6,5},{7,6},{9,8},{10,9},{11,10},{13,12},{... | collective-permute-start | bytes 393224 | tf_op jit(solution)/shard_map/ppermute | solution.py:298
  49.0 1.2 %collective-permute-start.12 = (bf16[2,4,128,128]{3,2,1,0:T(8,128)(2,1)S(1)}, bf16[2,4,128,128]{3,2,1,0:T(8,128)(2,1)S(1)}, u32[]{:S(2)}, u32[]{:S(2)}) collective-permute-start(bf16[2,4,128,128]{3,2,1,0:T(8,128)(2,1)S(1)} %get-tuple-element.60), channel_id=1, source_target_pairs={{0,8},{4,12},{8,0},{12,4},{16,24},{20,28},{24,16},{28,20},{1,9},{5... | collective-permute-start | bytes 786440 | tf_op jit(solution)/shard_map/ppermute | solution.py:304
  51.0 1.3 %collective-permute-start.17 = (bf16[4,2,128,128]{3,2,1,0:T(8,128)(2,1)S(1)}, bf16[4,2,128,128]{3,2,1,0:T(8,128)(2,1)S(1)}, u32[]{:S(2)}, u32[]{:S(2)}) collective-permute-start(bf16[4,2,128,128]{3,2,1,0:T(8,128)(2,1)S(1)} %get-tuple-element.65), channel_id=1, source_target_pairs={{1,0},{2,1},{3,2},{5,4},{6,5},{7,6},{9,8},{10,9},{11,10},{13,12},{... | collective-permute-start | bytes 786440 | tf_op jit(solution)/shard_map/ppermute | solution.py:298
  52.3 2.3 %collective-permute-done.18.back = bf16[2,2,128,128]{3,2,1,0:T(8,128)(2,1)S(1)} collective-permute-done((bf16[2,2,128,128]{3,2,1,0:T(8,128)(2,1)S(1)}, bf16[2,2,128,128]{3,2,1,0:T(8,128)(2,1)S(1)}, u32[]{:S(2)}, u32[]{:S(2)}) %collective-permute-start.18) | collective-permute-done | bytes 131104 | tf_op jit(solution)/shard_map/ppermute | solution.py:298
  54.6 1.5 %collective-permute-start.19 = (bf16[2,2,128,128]{3,2,1,0:T(8,128)(2,1)S(1)}, bf16[2,2,128,128]{3,2,1,0:T(8,128)(2,1)S(1)}, u32[]{:S(2)}, u32[]{:S(2)}) collective-permute-start(bf16[2,2,128,128]{3,2,1,0:T(8,128)(2,1)S(1)} %shard_map.106), channel_id=1, source_target_pairs={{0,24},{4,28},{8,16},{12,20},{16,8},{20,12},{24,0},{28,4},{1,25},{... | collective-permute-start | bytes 393224 | tf_op jit(solution)/shard_map/ppermute | solution.py:304
  56.1 1.3 %collective-permute-start.16 = (bf16[2,2,128,128]{3,2,1,0:T(8,128)(2,1)S(1)}, bf16[2,2,128,128]{3,2,1,0:T(8,128)(2,1)S(1)}, u32[]{:S(2)}, u32[]{:S(2)}) collective-permute-start(bf16[2,2,128,128]{3,2,1,0:T(8,128)(2,1)S(1)} %get-tuple-element.64), channel_id=1, source_target_pairs={{1,0},{2,1},{3,2},{5,4},{6,5},{7,6},{9,8},{10,9},{11,10},{13,12},{... | collective-permute-start | bytes 393224 | tf_op jit(solution)/shard_map/ppermute | solution.py:298
  57.4 1.7 %collective-permute-done.13.refs_2_.refs_1_ = bf16[2,4,128,128]{3,2,1,0:T(8,128)(2,1)S(1)} collective-permute-done((bf16[2,4,128,128]{3,2,1,0:T(8,128)(2,1)S(1)}, bf16[2,4,128,128]{3,2,1,0:T(8,128)(2,1)S(1)}, u32[]{:S(2)}, u32[]{:S(2)}) %collective-permute-start.13) | collective-permute-done | bytes 262176 | tf_op jit(solution)/shard_map/ppermute | solution.py:304
  59.1 2.4 %collective-permute-done.17.back = bf16[4,2,128,128]{3,2,1,0:T(8,128)(2,1)S(1)} collective-permute-done((bf16[4,2,128,128]{3,2,1,0:T(8,128)(2,1)S(1)}, bf16[4,2,128,128]{3,2,1,0:T(8,128)(2,1)S(1)}, u32[]{:S(2)}, u32[]{:S(2)}) %collective-permute-start.17) | collective-permute-done | bytes 262176 | tf_op jit(solution)/shard_map/ppermute | solution.py:298
  61.7 1.6 %collective-permute-start.20 = (bf16[2,2,128,128]{3,2,1,0:T(8,128)(2,1)S(1)}, bf16[2,2,128,128]{3,2,1,0:T(8,128)(2,1)S(1)}, u32[]{:S(2)}, u32[]{:S(2)}) collective-permute-start(bf16[2,2,128,128]{3,2,1,0:T(8,128)(2,1)S(1)} %get-tuple-element.67), channel_id=1, source_target_pairs={{0,8},{4,12},{8,0},{12,4},{16,24},{20,28},{24,16},{28,20},{1,9},{5... | collective-permute-start | bytes 393224 | tf_op jit(solution)/shard_map/ppermute | solution.py:304
  63.8 1.5 %shard_map.105.refs_2_ = bf16[128,32,128]{2,1,0:T(8,128)(2,1)} custom-call(s32[1]{0:T(128)} %bitcast.me_ref, bf16[2,4,128,128]{3,2,1,0:T(8,128)(2,1)S(1)} %get-tuple-element.51.refs_0_, bf16[2,4,128,128]{3,2,1,0:T(8,128)(2,1)S(1)} %collective-permute-done.12.refs_1_.refs_0_, bf16[2,4,128,128]{3,2,1,0:T(8,128)(2,1)S(1)} %collective-permute-done.13.refs_2_.refs_1_, ...), custom_call_target="tpu_custom_call" | custom-call | tf_op jit(solution)/shard_map/pallas_call | solution.py:284
  65.3 1.4 %collective-permute-done.20.refs_0_.refs_1_ = bf16[2,2,128,128]{3,2,1,0:T(8,128)(2,1)S(1)} collective-permute-done((bf16[2,2,128,128]{3,2,1,0:T(8,128)(2,1)S(1)}, bf16[2,2,128,128]{3,2,1,0:T(8,128)(2,1)S(1)}, u32[]{:S(2)}, u32[]{:S(2)}) %collective-permute-start.20) | collective-permute-done | bytes 131104 | tf_op jit(solution)/shard_map/ppermute | solution.py:304
  66.7 1.5 %collective-permute-done.21.refs_1_.refs_2_ = bf16[2,2,128,128]{3,2,1,0:T(8,128)(2,1)S(1)} collective-permute-done((bf16[2,2,128,128]{3,2,1,0:T(8,128)(2,1)S(1)}, bf16[2,2,128,128]{3,2,1,0:T(8,128)(2,1)S(1)}, u32[]{:S(2)}, u32[]{:S(2)}) %collective-permute-start.21) | collective-permute-done | bytes 131104 | tf_op jit(solution)/shard_map/ppermute | solution.py:304
  68.4 1.5 %collective-permute-done.22.refs_4_ = bf16[4,2,128,128]{3,2,1,0:T(8,128)(2,1)S(1)} collective-permute-done((bf16[4,2,128,128]{3,2,1,0:T(8,128)(2,1)S(1)}, bf16[4,2,128,128]{3,2,1,0:T(8,128)(2,1)S(1)}, u32[]{:S(2)}, u32[]{:S(2)}) %collective-permute-start.22) | collective-permute-done | bytes 262176 | tf_op jit(solution)/shard_map/ppermute | solution.py:304
  (39 shorter events, 4.5 us)
Async XLA Ops:
  1.8 1.7 %collective-permute-start = (bf16[4,2,128,128]{3,2,1,0:T(8,128)(2,1)S(1)}, bf16[4,2,128,128]{3,2,1,0:T(8,128)(2,1)S(1)}, u32[]{:S(2)}, u32[]{:S(2)}) collective-permute-start(bf16[4,2,128,128]{3,2,1,0:T(8,128)(2,1)S(1)} %get-tuple-element.41), channel_id=1, source_target_pairs={{0,4},{4,0},{8,12},{12,8},{16,20},{20,16},{24,28},{28,24},{1,5},{5... | collective-permute-start | bytes 786440 | tf_op jit(solution)/shard_map/ppermute | solution.py:304
  3.5 19.0 %copy-start.2 = (s32[32,5]{0,1:T(8,128)S(1)}, s32[32,5]{0,1:T(8,128)}, u32[]{:S(2)}) copy-start(s32[32,5]{0,1:T(8,128)} %param.13) | copy-start | bytes 1924
  5.9 11.5 %collective-permute-start.1 = (bf16[2,8,128,128]{3,2,1,0:T(8,128)(2,1)S(1)}, bf16[2,8,128,128]{3,2,1,0:T(8,128)(2,1)S(1)}, u32[]{:S(2)}, u32[]{:S(2)}) collective-permute-start(bf16[2,8,128,128]{3,2,1,0:T(8,128)(2,1)S(1)} %get-tuple-element.45), channel_id=1, source_target_pairs={{0,4},{4,0},{8,12},{12,8},{16,20},{20,16},{24,28},{28,24},{1,5},{5... | collective-permute-start | bytes 1572872 | tf_op jit(solution)/shard_map/ppermute | solution.py:304
  6.3 21.5 %collective-permute-start.7 = (bf16[2,8,128,128]{3,2,1,0:T(8,128)(2,1)S(1)}, bf16[2,8,128,128]{3,2,1,0:T(8,128)(2,1)}, u32[]{:S(2)}, u32[]{:S(2)}) collective-permute-start(bf16[2,8,128,128]{3,2,1,0:T(8,128)(2,1)S(1)} %get-tuple-element.52), channel_id=1, source_target_pairs={{0,4},{4,0},{8,12},{12,8},{16,20},{20,16},{24,28},{28,24},{1,5},{5... | collective-permute-start | bytes 1572872 | tf_op jit(solution)/shard_map/ppermute | solution.py:304
  6.5 6.7 %collective-permute-start.2 = (bf16[2,2,128,128]{3,2,1,0:T(8,128)(2,1)S(1)}, bf16[2,2,128,128]{3,2,1,0:T(8,128)(2,1)S(1)}, u32[]{:S(2)}, u32[]{:S(2)}) collective-permute-start(bf16[2,2,128,128]{3,2,1,0:T(8,128)(2,1)S(1)} %get-tuple-element.46), channel_id=1, source_target_pairs={{0,8},{4,12},{8,0},{12,4},{16,24},{20,28},{24,16},{28,20},{1,9},{5... | collective-permute-start | bytes 393224 | tf_op jit(solution)/shard_map/ppermute | solution.py:304
  9.3 8.1 %collective-permute-start.3 = (bf16[2,2,128,128]{3,2,1,0:T(8,128)(2,1)S(1)}, bf16[2,2,128,128]{3,2,1,0:T(8,128)(2,1)S(1)}, u32[]{:S(2)}, u32[]{:S(2)}) collective-permute-start(bf16[2,2,128,128]{3,2,1,0:T(8,128)(2,1)S(1)} %get-tuple-element.47), channel_id=1, source_target_pairs={{0,16},{4,20},{8,24},{12,28},{16,0},{20,4},{24,8},{28,12},{1,17},{... | collective-permute-start | bytes 393224 | tf_op jit(solution)/shard_map/ppermute | solution.py:304
  10.8 6.5 %collective-permute-start.4 = (bf16[2,2,128,128]{3,2,1,0:T(8,128)(2,1)S(1)}, bf16[2,2,128,128]{3,2,1,0:T(8,128)(2,1)S(1)}, u32[]{:S(2)}, u32[]{:S(2)}) collective-permute-start(bf16[2,2,128,128]{3,2,1,0:T(8,128)(2,1)S(1)} %get-tuple-element.48), channel_id=1, source_target_pairs={{0,24},{4,28},{8,16},{12,20},{16,8},{20,12},{24,0},{28,4},{1,25},{... | collective-permute-start | bytes 393224 | tf_op jit(solution)/shard_map/ppermute | solution.py:304
  17.4 15.9 %collective-permute-start.5 = (bf16[2,8,128,128]{3,2,1,0:T(8,128)(2,1)S(1)}, bf16[2,8,128,128]{3,2,1,0:T(8,128)(2,1)}, u32[]{:S(2)}, u32[]{:S(2)}) collective-permute-start(bf16[2,8,128,128]{3,2,1,0:T(8,128)(2,1)S(1)} %get-tuple-element.50), channel_id=1, source_target_pairs={{0,24},{4,28},{8,16},{12,20},{16,8},{20,12},{24,0},{28,4},{1,25},{... | collective-permute-start | bytes 1572872 | tf_op jit(solution)/shard_map/ppermute | solution.py:304
  19.0 15.6 %collective-permute-start.6 = (bf16[8,2,128,128]{3,2,1,0:T(8,128)(2,1)S(1)}, bf16[8,2,128,128]{3,2,1,0:T(8,128)(2,1)S(1)}, u32[]{:S(2)}, u32[]{:S(2)}) collective-permute-start(bf16[8,2,128,128]{3,2,1,0:T(8,128)(2,1)S(1)} %shard_map.99.refs_2_), channel_id=1, source_target_pairs={{0,1},{1,2},{2,3},{4,5},{5,6},{6,7},{8,9},{9,10},{10,11},{12,13},{... | collective-permute-start | bytes 1572872 | tf_op jit(solution)/shard_map/ppermute | solution.py:298
  25.7 15.8 %collective-permute-start.10 = (bf16[1,8,128,128]{3,2,1,0:T(8,128)(2,1)}, bf16[1,8,128,128]{3,2,1,0:T(8,128)(2,1)S(1)}, u32[]{:S(2)}, u32[]{:S(2)}) collective-permute-start(bf16[1,8,128,128]{3,2,1,0:T(8,128)(2,1)} %get-tuple-element.53), channel_id=1, source_target_pairs={{0,8},{4,12},{8,0},{12,4},{16,24},{20,28},{24,16},{28,20},{1,9},{5... | collective-permute-start | bytes 786440 | tf_op jit(solution)/shard_map/ppermute | solution.py:304
  27.3 14.3 %collective-permute-start.11 = (bf16[1,8,128,128]{3,2,1,0:T(8,128)(2,1)}, bf16[1,8,128,128]{3,2,1,0:T(8,128)(2,1)S(1)}, u32[]{:S(2)}, u32[]{:S(2)}) collective-permute-start(bf16[1,8,128,128]{3,2,1,0:T(8,128)(2,1)} %get-tuple-element.54), channel_id=1, source_target_pairs={{0,16},{4,20},{8,24},{12,28},{16,0},{20,4},{24,8},{28,12},{1,17},{... | collective-permute-start | bytes 786440 | tf_op jit(solution)/shard_map/ppermute | solution.py:304
  28.9 15.7 %collective-permute-start.9 = (bf16[1,8,128,128]{3,2,1,0:T(8,128)(2,1)S(1)}, bf16[1,8,128,128]{3,2,1,0:T(8,128)(2,1)S(1)}, u32[]{:S(2)}, u32[]{:S(2)}) collective-permute-start(bf16[1,8,128,128]{3,2,1,0:T(8,128)(2,1)S(1)} %get-tuple-element.71), channel_id=1, source_target_pairs={{0,16},{4,20},{8,24},{12,28},{16,0},{20,4},{24,8},{28,12},{1,17},{... | collective-permute-start | bytes 786440 | tf_op jit(solution)/shard_map/ppermute | solution.py:304
  33.4 1.3 %copy-start = (f32[4,4096]{1,0:T(4,128)S(1)}, f32[4,4096]{1,0:T(4,128)}, u32[]{:S(2)}) copy-start(f32[4,4096]{1,0:T(4,128)} %lse_ref.5) | copy-start | bytes 196612
  33.4 1.3 %copy-start.1 = (f32[4,4096]{1,0:T(4,128)S(1)}, f32[4,4096]{1,0:T(4,128)}, u32[]{:S(2)}) copy-start(f32[4,4096]{1,0:T(4,128)} %delta_ref.5) | copy-start | bytes 196612
  33.4 11.2 %collective-permute-start.8 = (bf16[1,8,128,128]{3,2,1,0:T(8,128)(2,1)S(1)}, bf16[1,8,128,128]{3,2,1,0:T(8,128)(2,1)S(1)}, u32[]{:S(2)}, u32[]{:S(2)}) collective-permute-start(bf16[1,8,128,128]{3,2,1,0:T(8,128)(2,1)S(1)} %get-tuple-element.72), channel_id=1, source_target_pairs={{0,8},{4,12},{8,0},{12,4},{16,24},{20,28},{24,16},{28,20},{1,9},{5... | collective-permute-start | bytes 786440 | tf_op jit(solution)/shard_map/ppermute | solution.py:304
  39.8 14.8 %collective-permute-start.14 = (bf16[2,4,128,128]{3,2,1,0:T(8,128)(2,1)S(1)}, bf16[2,4,128,128]{3,2,1,0:T(8,128)(2,1)S(1)}, u32[]{:S(2)}, u32[]{:S(2)}) collective-permute-start(bf16[2,4,128,128]{3,2,1,0:T(8,128)(2,1)S(1)} %get-tuple-element.62), channel_id=1, source_target_pairs={{0,24},{4,28},{8,16},{12,20},{16,8},{20,12},{24,0},{28,4},{1,25},{... | collective-permute-start | bytes 786440 | tf_op jit(solution)/shard_map/ppermute | solution.py:304
  47.7 6.9 %collective-permute-start.18 = (bf16[2,2,128,128]{3,2,1,0:T(8,128)(2,1)S(1)}, bf16[2,2,128,128]{3,2,1,0:T(8,128)(2,1)S(1)}, u32[]{:S(2)}, u32[]{:S(2)}) collective-permute-start(bf16[2,2,128,128]{3,2,1,0:T(8,128)(2,1)S(1)} %get-tuple-element.66), channel_id=1, source_target_pairs={{1,0},{2,1},{3,2},{5,4},{6,5},{7,6},{9,8},{10,9},{11,10},{13,12},{... | collective-permute-start | bytes 393224 | tf_op jit(solution)/shard_map/ppermute | solution.py:298
  49.0 8.3 %collective-permute-start.12 = (bf16[2,4,128,128]{3,2,1,0:T(8,128)(2,1)S(1)}, bf16[2,4,128,128]{3,2,1,0:T(8,128)(2,1)S(1)}, u32[]{:S(2)}, u32[]{:S(2)}) collective-permute-start(bf16[2,4,128,128]{3,2,1,0:T(8,128)(2,1)S(1)} %get-tuple-element.60), channel_id=1, source_target_pairs={{0,8},{4,12},{8,0},{12,4},{16,24},{20,28},{24,16},{28,20},{1,9},{5... | collective-permute-start | bytes 786440 | tf_op jit(solution)/shard_map/ppermute | solution.py:304
  50.2 8.9 %collective-permute-start.13 = (bf16[2,4,128,128]{3,2,1,0:T(8,128)(2,1)S(1)}, bf16[2,4,128,128]{3,2,1,0:T(8,128)(2,1)S(1)}, u32[]{:S(2)}, u32[]{:S(2)}) collective-permute-start(bf16[2,4,128,128]{3,2,1,0:T(8,128)(2,1)S(1)} %get-tuple-element.61), channel_id=1, source_target_pairs={{0,16},{4,20},{8,24},{12,28},{16,0},{20,4},{24,8},{28,12},{1,17},{... | collective-permute-start | bytes 786440 | tf_op jit(solution)/shard_map/ppermute | solution.py:304
  51.0 10.6 %collective-permute-start.17 = (bf16[4,2,128,128]{3,2,1,0:T(8,128)(2,1)S(1)}, bf16[4,2,128,128]{3,2,1,0:T(8,128)(2,1)S(1)}, u32[]{:S(2)}, u32[]{:S(2)}) collective-permute-start(bf16[4,2,128,128]{3,2,1,0:T(8,128)(2,1)S(1)} %get-tuple-element.65), channel_id=1, source_target_pairs={{1,0},{2,1},{3,2},{5,4},{6,5},{7,6},{9,8},{10,9},{11,10},{13,12},{... | collective-permute-start | bytes 786440 | tf_op jit(solution)/shard_map/ppermute | solution.py:298
  54.6 7.0 %collective-permute-start.19 = (bf16[2,2,128,128]{3,2,1,0:T(8,128)(2,1)S(1)}, bf16[2,2,128,128]{3,2,1,0:T(8,128)(2,1)S(1)}, u32[]{:S(2)}, u32[]{:S(2)}) collective-permute-start(bf16[2,2,128,128]{3,2,1,0:T(8,128)(2,1)S(1)} %shard_map.106), channel_id=1, source_target_pairs={{0,24},{4,28},{8,16},{12,20},{16,8},{20,12},{24,0},{28,4},{1,25},{... | collective-permute-start | bytes 393224 | tf_op jit(solution)/shard_map/ppermute | solution.py:304
  56.1 9.2 %collective-permute-start.16 = (bf16[2,2,128,128]{3,2,1,0:T(8,128)(2,1)S(1)}, bf16[2,2,128,128]{3,2,1,0:T(8,128)(2,1)S(1)}, u32[]{:S(2)}, u32[]{:S(2)}) collective-permute-start(bf16[2,2,128,128]{3,2,1,0:T(8,128)(2,1)S(1)} %get-tuple-element.64), channel_id=1, source_target_pairs={{1,0},{2,1},{3,2},{5,4},{6,5},{7,6},{9,8},{10,9},{11,10},{13,12},{... | collective-permute-start | bytes 393224 | tf_op jit(solution)/shard_map/ppermute | solution.py:298
  59.1 4.7 %collective-permute-start.15 = (bf16[4,4,128,128]{3,2,1,0:T(8,128)(2,1)S(1)}, bf16[4,4,128,128]{3,2,1,0:T(8,128)(2,1)S(1)}, u32[]{:S(2)}, u32[]{:S(2)}) collective-permute-start(bf16[4,4,128,128]{3,2,1,0:T(8,128)(2,1)S(1)} %shard_map.104), channel_id=1, source_target_pairs={{0,4},{4,0},{8,12},{12,8},{16,20},{20,16},{24,28},{28,24},{1,5},{5... | collective-permute-start | bytes 1572872 | tf_op jit(solution)/shard_map/ppermute | solution.py:304
  61.7 5.0 %collective-permute-start.20 = (bf16[2,2,128,128]{3,2,1,0:T(8,128)(2,1)S(1)}, bf16[2,2,128,128]{3,2,1,0:T(8,128)(2,1)S(1)}, u32[]{:S(2)}, u32[]{:S(2)}) collective-permute-start(bf16[2,2,128,128]{3,2,1,0:T(8,128)(2,1)S(1)} %get-tuple-element.67), channel_id=1, source_target_pairs={{0,8},{4,12},{8,0},{12,4},{16,24},{20,28},{24,16},{28,20},{1,9},{5... | collective-permute-start | bytes 393224 | tf_op jit(solution)/shard_map/ppermute | solution.py:304
  63.2 5.0 %collective-permute-start.21 = (bf16[2,2,128,128]{3,2,1,0:T(8,128)(2,1)S(1)}, bf16[2,2,128,128]{3,2,1,0:T(8,128)(2,1)S(1)}, u32[]{:S(2)}, u32[]{:S(2)}) collective-permute-start(bf16[2,2,128,128]{3,2,1,0:T(8,128)(2,1)S(1)} %get-tuple-element.68), channel_id=1, source_target_pairs={{0,16},{4,20},{8,24},{12,28},{16,0},{20,4},{24,8},{28,12},{1,17},{... | collective-permute-start | bytes 393224 | tf_op jit(solution)/shard_map/ppermute | solution.py:304
  68.3 1.6 %collective-permute-start.22 = (bf16[4,2,128,128]{3,2,1,0:T(8,128)(2,1)S(1)}, bf16[4,2,128,128]{3,2,1,0:T(8,128)(2,1)S(1)}, u32[]{:S(2)}, u32[]{:S(2)}) collective-permute-start(bf16[4,2,128,128]{3,2,1,0:T(8,128)(2,1)S(1)} %shard_map.109), channel_id=1, source_target_pairs={{0,4},{4,0},{8,12},{12,8},{16,20},{20,16},{24,28},{28,24},{1,5},{5... | collective-permute-start | bytes 786440 | tf_op jit(solution)/shard_map/ppermute | solution.py:304

commit v5 on v4

--- a/solution.py
+++ b/solution.py
@@ -11,7 +11,7 @@
 BLOCK = 128
 LOG2E = 1.4426950408889634
 FIRST, NEXT, LAST = range(3)
-SHORT, ADD_COST = 2 * 10**9, 10**11
+SHORT, JOIN_COST, ADD_COST = 2 * 10**9, 10**10, 10**11
 
 
 def contract(a, b, a_dim, b_dim):
@@ -69,9 +69,9 @@
         dp = contract(cat_v[...], do, 1, 1)
         p_parts = []
         for j in range(select):
-            p = jnp.exp2(s[j * BLOCK : (j + 1) * BLOCK] * (scale * LOG2E) - lse)
-            allowed = causal if j == 0 else entries[j] >= 0
-            p_parts.append(jnp.where(allowed, p, 0.0))
+            taken = lse if j == 0 else lse + jnp.where(entries[j] >= 0, 0.0, 1e30)
+            p = jnp.exp2(s[j * BLOCK : (j + 1) * BLOCK] * (scale * LOG2E) - taken)
+            p_parts.append(jnp.where(causal, p, 0.0) if j == 0 else p)
         p = jnp.concatenate(p_parts, 0)
         ds = (p * (dp - delta)).astype(jnp.bfloat16)
         dv = contract(p.astype(jnp.bfloat16), do, 1, 0)
@@ -176,7 +176,7 @@
     vmem = pl.BlockSpec(memory_space=pltpu.VMEM)
     return pl.pallas_call(
         functools.partial(merge_kernel, count),
-        in_specs=[vmem] * (count + 1) + [pl.BlockSpec(memory_space=pl.ANY)] * len(after),
+        in_specs=[vmem] * (count + 1 + len(after)),
         out_specs=[vmem] * count,
         out_shape=[jax.ShapeDtypeStruct(x.shape, x.dtype) for x in pieces],
         input_output_aliases={i: i for i in range(count)},
@@ -214,7 +214,7 @@
         out_specs=vmem,
         out_shape=jax.ShapeDtypeStruct((2 * len(pieces), *pieces[0].shape[1:]), pieces[0].dtype),
         compiler_params=pltpu.CompilerParams(vmem_limit_bytes=16 * 1024 * 1024),
-        cost_estimate=pl.CostEstimate(flops=2**20, bytes_accessed=2**20, transcendentals=0),
+        cost_estimate=pl.CostEstimate(flops=JOIN_COST, bytes_accessed=2**20, transcendentals=0),
     )(*pieces)
 
 
@@ -321,7 +321,7 @@
     own = joined(kv_pieces)
     pack = functools.partial(packed, me, [queries, grad_out], [1] * 2, uly_count)
     *qd_ends, give_ends, give_mids = pack(ends, 2, [ends, mids], merged_kv[:1])
-    qd_here, qd_far = merged(qd_ends, swapped(give_ends, 1), kv_pieces[1:])
+    qd_here, qd_far = merged(qd_ends, swapped(give_ends, 1), [own])
     qd_far = landed(swapped(qd_far, 2 * far), [], SHORT)
     got_mids = swapped(give_mids, 1)
     firsts = [swapped(piece, 2 * m) for m, piece in zip(mids, pack(mids, 1, [], [own]))]

time: 71.1 us -> 68.3 us (0.961)
  waiting for transfers between devices: 21.5 us -> 18.8 us
    ppermute x19, waiting for transfers between devices: 16.8 us -> 14.1 us  [swapped(): lax.ppermute(block, 'uly', [(i, i ^ k) for i in range(lax.axis_size('uly'...]
  transfers between devices with their start and end apart: 23 -> 23, of which waited for: 10 -> 11; matrix products, arithmetic and copies ran while one was open for 2% -> 2% of each run, Pallas kernels for 22% -> 27%
where the time goes in v5:
time: 68.3 us; the launch traced here: 68 us
  starting transfers between devices  26.9 us (39%)
  Pallas kernels  20.2 us (30%)
  waiting for transfers between devices  18.8 us (28%)
  local copies, waits for them, and re-layouts  1.17 us (2%)
  between operations  0.86 us (1%)
    ppermute x19, starting transfers between devices, swapped(): lax.ppermute(block, 'uly', [(i, i ^ k) for i in range(lax.axis_size('uly'...  19.6 us
    ppermute x19, waiting for transfers between devices, swapped(): lax.ppermute(block, 'uly', [(i, i ^ k) for i in range(lax.axis_size('uly'...  14.1 us
    pallas_call x3, Pallas kernels, block_grads(): pl.pallas_call(functools.partial(block_kernel, blocks, len(out_rows), len...  11 us
    ppermute x4, starting transfers between devices, passed_along(): lax.ppermute(block, axis, [(i - distance, i) for i in devices if i - dist...  7.35 us
    pallas_call x3, Pallas kernels, packed(): pl.pallas_call(functools.partial(pack_kernel, uly_count, fold_counts, kep...  6.58 us
    ppermute x4, waiting for transfers between devices, passed_along(): lax.ppermute(block, axis, [(i - distance, i) for i in devices if i - dist...  4.71 us
    pallas_call x2, Pallas kernels, unpacked(): pl.pallas_call(functools.partial(unpack_kernel, chips, fold_count), in_sp...  2.38 us
  transfers between devices with their start and end apart: 23, of which 11 were waited for; matrix products, arithmetic and copies ran while one was open for 2% of the time, Pallas kernels for 27%

profile of v5, /device:TPU:0, one launch (start us, length us, event | category | flops | bytes accessed | tf_op | source)
XLA Modules:
  0.0 68.0 jit_solution(18338064101178952979)
XLA Ops:
  0.6 1.2 %shard_map.94 = (bf16[2,2,128,128]{3,2,1,0:T(8,128)(2,1)S(1)}, bf16[2,2,128,128]{3,2,1,0:T(8,128)(2,1)S(1)}, bf16[2,2,128,128]{3,2,1,0:T(8,128)(2,1)S(1)}, bf16[...) custom-call(s32[1]{0:T(128)} %bitcast.me_ref, bf16[128,8,128]{2,1,0:T(8,128)(2,1)} %refs_0_.3, ...), custom_call_target="tpu_custom_call" | custom-call | tf_op jit(solution)/shard_map/pallas_call | solution.py:154
  2.3 1.2 %collective-permute-done.refs_4_ = bf16[4,2,128,128]{3,2,1,0:T(8,128)(2,1)S(1)} collective-permute-done((bf16[4,2,128,128]{3,2,1,0:T(8,128)(2,1)S(1)}, bf16[4,2,128,128]{3,2,1,0:T(8,128)(2,1)S(1)}, u32[]{:S(2)}, u32[]{:S(2)}) %collective-permute-start) | collective-permute-done | bytes 262176 | tf_op jit(solution)/shard_map/ppermute | solution.py:304
  3.5 2.9 %collective-permute-start.2 = (bf16[2,2,128,128]{3,2,1,0:T(8,128)(2,1)S(1)}, bf16[2,2,128,128]{3,2,1,0:T(8,128)(2,1)S(1)}, u32[]{:S(2)}, u32[]{:S(2)}) collective-permute-start(bf16[2,2,128,128]{3,2,1,0:T(8,128)(2,1)S(1)} %get-tuple-element.46), channel_id=1, source_target_pairs={{0,8},{4,12},{8,0},{12,4},{16,24},{20,28},{24,16},{28,20},{1,9},{5... | collective-permute-start | bytes 393224 | tf_op jit(solution)/shard_map/ppermute | solution.py:304
  6.4 1.5 %collective-permute-start.3 = (bf16[2,2,128,128]{3,2,1,0:T(8,128)(2,1)S(1)}, bf16[2,2,128,128]{3,2,1,0:T(8,128)(2,1)S(1)}, u32[]{:S(2)}, u32[]{:S(2)}) collective-permute-start(bf16[2,2,128,128]{3,2,1,0:T(8,128)(2,1)S(1)} %get-tuple-element.47), channel_id=1, source_target_pairs={{0,16},{4,20},{8,24},{12,28},{16,0},{20,4},{24,8},{28,12},{1,17},{... | collective-permute-start | bytes 393224 | tf_op jit(solution)/shard_map/ppermute | solution.py:304
  8.0 2.3 %shard_map.96 = (bf16[2,8,128,128]{3,2,1,0:T(8,128)(2,1)S(1)}, bf16[2,8,128,128]{3,2,1,0:T(8,128)(2,1)S(1)}, bf16[2,8,128,128]{3,2,1,0:T(8,128)(2,1)S(1)}, bf16[2,8,128,128]{3,2,1,0:T(8,128)(2,1)S(1)}) custom-call(s32[1]{0:T(128)} %bitcast.me_ref, bf16[128,32,128]{2,1,0:T(8,128)(2,1)} %refs_0_.5, bf16[128,32,128]{2,1,0:T(8,128)(2,1)} %refs_1_.5, ...), custom_call_target="tpu_custom_call" | custom-call | tf_op jit(solution)/shard_map/pallas_call | solution.py:154
  10.9 3.6 %collective-permute-done.3.refs_2_ = bf16[2,2,128,128]{3,2,1,0:T(8,128)(2,1)S(1)} collective-permute-done((bf16[2,2,128,128]{3,2,1,0:T(8,128)(2,1)S(1)}, bf16[2,2,128,128]{3,2,1,0:T(8,128)(2,1)S(1)}, u32[]{:S(2)}, u32[]{:S(2)}) %collective-permute-start.3) | collective-permute-done | bytes 131104 | tf_op jit(solution)/shard_map/ppermute | solution.py:304
  14.6 1.6 %collective-permute-start.5 = (bf16[2,8,128,128]{3,2,1,0:T(8,128)(2,1)S(1)}, bf16[2,8,128,128]{3,2,1,0:T(8,128)(2,1)}, u32[]{:S(2)}, u32[]{:S(2)}) collective-permute-start(bf16[2,8,128,128]{3,2,1,0:T(8,128)(2,1)S(1)} %get-tuple-element.50), channel_id=1, source_target_pairs={{0,24},{4,28},{8,16},{12,20},{16,8},{20,12},{24,0},{28,4},{1,25},{... | collective-permute-start | bytes 1572872 | tf_op jit(solution)/shard_map/ppermute | solution.py:304
  16.2 3.5 %collective-permute-start.6 = (bf16[8,2,128,128]{3,2,1,0:T(8,128)(2,1)S(1)}, bf16[8,2,128,128]{3,2,1,0:T(8,128)(2,1)S(1)}, u32[]{:S(2)}, u32[]{:S(2)}) collective-permute-start(bf16[8,2,128,128]{3,2,1,0:T(8,128)(2,1)S(1)} %shard_map.97.refs_3_.refs_2_), channel_id=1, source_target_pairs={{0,1},{1,2},{2,3},{4,5},{5,6},{6,7},{8,9},{9,10},{10,11},{12,13},{... | collective-permute-start | bytes 1572872 | tf_op jit(solution)/shard_map/ppermute | solution.py:298
  19.8 3.1 %shard_map.101 = (bf16[1,8,128,128]{3,2,1,0:T(8,128)(2,1)}, bf16[1,8,128,128]{3,2,1,0:T(8,128)(2,1)}) custom-call(s32[1]{0:T(128)} %bitcast.me_ref, bf16[128,32,128]{2,1,0:T(8,128)(2,1)} %refs_0_.5, bf16[128,32,128]{2,1,0:T(8,128)(2,1)} %refs_1_.5, bf16[8,2,128,128]{3,2,1,0:T(8,128)(2,1)S(1)} %shard_map.97.refs_3_.refs_2_), custom_call_target="tpu_custom_call" | custom-call | tf_op jit(solution)/shard_map/pallas_call | solution.py:154
  22.9 1.6 %collective-permute-start.10 = (bf16[1,8,128,128]{3,2,1,0:T(8,128)(2,1)}, bf16[1,8,128,128]{3,2,1,0:T(8,128)(2,1)S(1)}, u32[]{:S(2)}, u32[]{:S(2)}) collective-permute-start(bf16[1,8,128,128]{3,2,1,0:T(8,128)(2,1)} %get-tuple-element.53), channel_id=1, source_target_pairs={{0,8},{4,12},{8,0},{12,4},{16,24},{20,28},{24,16},{28,20},{1,9},{5... | collective-permute-start | bytes 786440 | tf_op jit(solution)/shard_map/ppermute | solution.py:304
  24.9 1.1 %fusion = (bf16[1,8,128,128]{3,2,1,0:T(8,128)(2,1)S(1)}, bf16[1,8,128,128]{3,2,1,0:T(8,128)(2,1)S(1)}) fusion(bf16[2,8,128,128]{3,2,1,0:T(8,128)(2,1)} %collective-permute-done.7), kind=kLoop, calls=%fused_computation | loop fusion | bytes 1048576 | tf_op jit(solution)/shard_map/slice | solution.py:328
  26.0 1.6 %collective-permute-start.9 = (bf16[1,8,128,128]{3,2,1,0:T(8,128)(2,1)S(1)}, bf16[1,8,128,128]{3,2,1,0:T(8,128)(2,1)S(1)}, u32[]{:S(2)}, u32[]{:S(2)}) collective-permute-start(bf16[1,8,128,128]{3,2,1,0:T(8,128)(2,1)S(1)} %get-tuple-element.71), channel_id=1, source_target_pairs={{0,16},{4,20},{8,24},{12,28},{16,0},{20,4},{24,8},{28,12},{1,17},{... | collective-permute-start | bytes 786440 | tf_op jit(solution)/shard_map/ppermute | solution.py:304
  27.6 3.0 %collective-permute-done.5.refs_0_ = bf16[2,8,128,128]{3,2,1,0:T(8,128)(2,1)} collective-permute-done((bf16[2,8,128,128]{3,2,1,0:T(8,128)(2,1)S(1)}, bf16[2,8,128,128]{3,2,1,0:T(8,128)(2,1)}, u32[]{:S(2)}, u32[]{:S(2)}) %collective-permute-start.5) | collective-permute-done | bytes 524320 | tf_op jit(solution)/shard_map/ppermute | solution.py:304
  30.6 1.3 %collective-permute-start.8 = (bf16[1,8,128,128]{3,2,1,0:T(8,128)(2,1)S(1)}, bf16[1,8,128,128]{3,2,1,0:T(8,128)(2,1)S(1)}, u32[]{:S(2)}, u32[]{:S(2)}) collective-permute-start(bf16[1,8,128,128]{3,2,1,0:T(8,128)(2,1)S(1)} %get-tuple-element.72), channel_id=1, source_target_pairs={{0,8},{4,12},{8,0},{12,4},{16,24},{20,28},{24,16},{28,20},{1,9},{5... | collective-permute-start | bytes 786440 | tf_op jit(solution)/shard_map/ppermute | solution.py:304
  31.8 5.0 %shard_map.100 = (bf16[2,4,128,128]{3,2,1,0:T(8,128)(2,1)S(1)}, bf16[2,4,128,128]{3,2,1,0:T(8,128)(2,1)S(1)}, bf16[16,2,128,128]{3,2,1,0:T(8,128)(2,1)S(1)}, f32[16,2,128,128]{3,2,1,0:T(8,128)S(1)}) custom-call(s32[1]{0:T(128)} %bitcast.1.slab_ref, s32[1]{0:T(128)} %bitcast.me_ref, s32[32,5]{1,0:T(8,128)S(1)} %copy.17.keys_ref, f32[4,4096]{1,0:T(4,128)S(1)} %copy-done, ...), custom_call_target="tpu_custom_call" | custom-call | flops 1677721600 | bytes 8388608 | tf_op jit(solution)/shard_map/pallas_call | solution.py:115
  36.9 1.8 %collective-permute-start.14 = (bf16[2,4,128,128]{3,2,1,0:T(8,128)(2,1)S(1)}, bf16[2,4,128,128]{3,2,1,0:T(8,128)(2,1)S(1)}, u32[]{:S(2)}, u32[]{:S(2)}) collective-permute-start(bf16[2,4,128,128]{3,2,1,0:T(8,128)(2,1)S(1)} %get-tuple-element.62), channel_id=1, source_target_pairs={{0,24},{4,28},{8,16},{12,20},{16,8},{20,12},{24,0},{28,4},{1,25},{... | collective-permute-start | bytes 786440 | tf_op jit(solution)/shard_map/ppermute | solution.py:304
  38.7 2.9 %shard_map.102 = (bf16[1,4,128,128]{3,2,1,0:T(8,128)(2,1)S(1)}, bf16[1,4,128,128]{3,2,1,0:T(8,128)(2,1)S(1)}, f32[16,2,128,128]{3,2,1,0:T(8,128)S(1)}) custom-call(s32[1]{0:T(128)} %bitcast.1.slab_ref, s32[1]{0:T(128)} %bitcast.me_ref, s32[32,5]{1,0:T(8,128)S(1)} %copy.17.keys_ref, f32[4,4096]{1,0:T(4,128)S(1)} %copy-done, f32[4,4096]{1,0:T(4,128)S(1)} %copy-done.1, ...), custom_call_target="tpu_custom_call" | custom-call | flops 838860800 | bytes 8388608 | tf_op jit(solution)/shard_map/pallas_call | solution.py:115
  41.8 3.1 %shard_map.103 = (bf16[2,4,128,128]{3,2,1,0:T(8,128)(2,1)S(1)}, bf16[2,4,128,128]{3,2,1,0:T(8,128)(2,1)S(1)}, f32[8,2,128,128]{3,2,1,0:T(8,128)S(1)}, bf16[2,2,1...) custom-call(s32[1]{0:T(128)} %bitcast.1.slab_ref, ...), custom_call_target="tpu_custom_call" | custom-call | flops 838860800 | bytes 8388608 | tf_op jit(solution)/shard_map/pallas_call | solution.py:115
  44.9 1.3 %collective-permute-start.18 = (bf16[2,2,128,128]{3,2,1,0:T(8,128)(2,1)S(1)}, bf16[2,2,128,128]{3,2,1,0:T(8,128)(2,1)S(1)}, u32[]{:S(2)}, u32[]{:S(2)}) collective-permute-start(bf16[2,2,128,128]{3,2,1,0:T(8,128)(2,1)S(1)} %get-tuple-element.66), channel_id=1, source_target_pairs={{1,0},{2,1},{3,2},{5,4},{6,5},{7,6},{9,8},{10,9},{11,10},{13,12},{... | collective-permute-start | bytes 393224 | tf_op jit(solution)/shard_map/ppermute | solution.py:298
  46.2 1.1 %collective-permute-start.12 = (bf16[2,4,128,128]{3,2,1,0:T(8,128)(2,1)S(1)}, bf16[2,4,128,128]{3,2,1,0:T(8,128)(2,1)S(1)}, u32[]{:S(2)}, u32[]{:S(2)}) collective-permute-start(bf16[2,4,128,128]{3,2,1,0:T(8,128)(2,1)S(1)} %get-tuple-element.60), channel_id=1, source_target_pairs={{0,8},{4,12},{8,0},{12,4},{16,24},{20,28},{24,16},{28,20},{1,9},{5... | collective-permute-start | bytes 786440 | tf_op jit(solution)/shard_map/ppermute | solution.py:304
  48.2 1.3 %collective-permute-start.17 = (bf16[4,2,128,128]{3,2,1,0:T(8,128)(2,1)S(1)}, bf16[4,2,128,128]{3,2,1,0:T(8,128)(2,1)S(1)}, u32[]{:S(2)}, u32[]{:S(2)}) collective-permute-start(bf16[4,2,128,128]{3,2,1,0:T(8,128)(2,1)S(1)} %get-tuple-element.65), channel_id=1, source_target_pairs={{1,0},{2,1},{3,2},{5,4},{6,5},{7,6},{9,8},{10,9},{11,10},{13,12},{... | collective-permute-start | bytes 786440 | tf_op jit(solution)/shard_map/ppermute | solution.py:298
  49.5 2.3 %collective-permute-done.18.back = bf16[2,2,128,128]{3,2,1,0:T(8,128)(2,1)S(1)} collective-permute-done((bf16[2,2,128,128]{3,2,1,0:T(8,128)(2,1)S(1)}, bf16[2,2,128,128]{3,2,1,0:T(8,128)(2,1)S(1)}, u32[]{:S(2)}, u32[]{:S(2)}) %collective-permute-start.18) | collective-permute-done | bytes 131104 | tf_op jit(solution)/shard_map/ppermute | solution.py:298
  51.8 1.4 %collective-permute-start.19 = (bf16[2,2,128,128]{3,2,1,0:T(8,128)(2,1)S(1)}, bf16[2,2,128,128]{3,2,1,0:T(8,128)(2,1)S(1)}, u32[]{:S(2)}, u32[]{:S(2)}) collective-permute-start(bf16[2,2,128,128]{3,2,1,0:T(8,128)(2,1)S(1)} %shard_map.106), channel_id=1, source_target_pairs={{0,24},{4,28},{8,16},{12,20},{16,8},{20,12},{24,0},{28,4},{1,25},{... | collective-permute-start | bytes 393224 | tf_op jit(solution)/shard_map/ppermute | solution.py:304
  53.2 1.3 %collective-permute-start.16 = (bf16[2,2,128,128]{3,2,1,0:T(8,128)(2,1)S(1)}, bf16[2,2,128,128]{3,2,1,0:T(8,128)(2,1)S(1)}, u32[]{:S(2)}, u32[]{:S(2)}) collective-permute-start(bf16[2,2,128,128]{3,2,1,0:T(8,128)(2,1)S(1)} %get-tuple-element.64), channel_id=1, source_target_pairs={{1,0},{2,1},{3,2},{5,4},{6,5},{7,6},{9,8},{10,9},{11,10},{13,12},{... | collective-permute-start | bytes 393224 | tf_op jit(solution)/shard_map/ppermute | solution.py:298
  54.5 1.7 %collective-permute-done.13.refs_2_.refs_1_ = bf16[2,4,128,128]{3,2,1,0:T(8,128)(2,1)S(1)} collective-permute-done((bf16[2,4,128,128]{3,2,1,0:T(8,128)(2,1)S(1)}, bf16[2,4,128,128]{3,2,1,0:T(8,128)(2,1)S(1)}, u32[]{:S(2)}, u32[]{:S(2)}) %collective-permute-start.13) | collective-permute-done | bytes 262176 | tf_op jit(solution)/shard_map/ppermute | solution.py:304
  56.4 2.4 %collective-permute-done.17.back = bf16[4,2,128,128]{3,2,1,0:T(8,128)(2,1)S(1)} collective-permute-done((bf16[4,2,128,128]{3,2,1,0:T(8,128)(2,1)S(1)}, bf16[4,2,128,128]{3,2,1,0:T(8,128)(2,1)S(1)}, u32[]{:S(2)}, u32[]{:S(2)}) %collective-permute-start.17) | collective-permute-done | bytes 262176 | tf_op jit(solution)/shard_map/ppermute | solution.py:298
  58.9 1.6 %collective-permute-start.20 = (bf16[2,2,128,128]{3,2,1,0:T(8,128)(2,1)S(1)}, bf16[2,2,128,128]{3,2,1,0:T(8,128)(2,1)S(1)}, u32[]{:S(2)}, u32[]{:S(2)}) collective-permute-start(bf16[2,2,128,128]{3,2,1,0:T(8,128)(2,1)S(1)} %get-tuple-element.67), channel_id=1, source_target_pairs={{0,8},{4,12},{8,0},{12,4},{16,24},{20,28},{24,16},{28,20},{1,9},{5... | collective-permute-start | bytes 393224 | tf_op jit(solution)/shard_map/ppermute | solution.py:304
  61.0 1.5 %shard_map.105.refs_2_ = bf16[128,32,128]{2,1,0:T(8,128)(2,1)} custom-call(s32[1]{0:T(128)} %bitcast.me_ref, bf16[2,4,128,128]{3,2,1,0:T(8,128)(2,1)S(1)} %get-tuple-element.51.refs_0_, bf16[2,4,128,128]{3,2,1,0:T(8,128)(2,1)S(1)} %collective-permute-done.12.refs_1_.refs_0_, bf16[2,4,128,128]{3,2,1,0:T(8,128)(2,1)S(1)} %collective-permute-done.13.refs_2_.refs_1_, ...), custom_call_target="tpu_custom_call" | custom-call | tf_op jit(solution)/shard_map/pallas_call | solution.py:284
  62.5 1.4 %collective-permute-done.20.refs_0_.refs_1_ = bf16[2,2,128,128]{3,2,1,0:T(8,128)(2,1)S(1)} collective-permute-done((bf16[2,2,128,128]{3,2,1,0:T(8,128)(2,1)S(1)}, bf16[2,2,128,128]{3,2,1,0:T(8,128)(2,1)S(1)}, u32[]{:S(2)}, u32[]{:S(2)}) %collective-permute-start.20) | collective-permute-done | bytes 131104 | tf_op jit(solution)/shard_map/ppermute | solution.py:304
  63.9 1.5 %collective-permute-done.21.refs_1_.refs_2_ = bf16[2,2,128,128]{3,2,1,0:T(8,128)(2,1)S(1)} collective-permute-done((bf16[2,2,128,128]{3,2,1,0:T(8,128)(2,1)S(1)}, bf16[2,2,128,128]{3,2,1,0:T(8,128)(2,1)S(1)}, u32[]{:S(2)}, u32[]{:S(2)}) %collective-permute-start.21) | collective-permute-done | bytes 131104 | tf_op jit(solution)/shard_map/ppermute | solution.py:304
  65.6 1.5 %collective-permute-done.22.refs_4_ = bf16[4,2,128,128]{3,2,1,0:T(8,128)(2,1)S(1)} collective-permute-done((bf16[4,2,128,128]{3,2,1,0:T(8,128)(2,1)S(1)}, bf16[4,2,128,128]{3,2,1,0:T(8,128)(2,1)S(1)}, u32[]{:S(2)}, u32[]{:S(2)}) %collective-permute-start.22) | collective-permute-done | bytes 262176 | tf_op jit(solution)/shard_map/ppermute | solution.py:304
  67.1 0.9 %shard_map.110 = (bf16[128,8,128]{2,1,0:T(8,128)(2,1)}, bf16[128,8,128]{2,1,0:T(8,128)(2,1)}) custom-call(s32[1]{0:T(128)} %bitcast.me_ref, bf16[2,2,128,128]{3,2,1,0:T(8,128)(2,1)S(1)} %shard_map.108.refs_0_, bf16[2,2,128,128]{3,2,1,0:T(8,128)(2,1)S(1)} %collective-permute-done.20.refs_0_.refs_1_, ...), custom_call_target="tpu_custom_call" | custom-call | tf_op jit(solution)/shard_map/pallas_call | solution.py:284
  (39 shorter events, 3.7 us)
Async XLA Ops:
  1.8 1.7 %collective-permute-start = (bf16[4,2,128,128]{3,2,1,0:T(8,128)(2,1)S(1)}, bf16[4,2,128,128]{3,2,1,0:T(8,128)(2,1)S(1)}, u32[]{:S(2)}, u32[]{:S(2)}) collective-permute-start(bf16[4,2,128,128]{3,2,1,0:T(8,128)(2,1)S(1)} %get-tuple-element.41), channel_id=1, source_target_pairs={{0,4},{4,0},{8,12},{12,8},{16,20},{20,16},{24,28},{28,24},{1,5},{5... | collective-permute-start | bytes 786440 | tf_op jit(solution)/shard_map/ppermute | solution.py:304
  3.5 7.4 %collective-permute-start.2 = (bf16[2,2,128,128]{3,2,1,0:T(8,128)(2,1)S(1)}, bf16[2,2,128,128]{3,2,1,0:T(8,128)(2,1)S(1)}, u32[]{:S(2)}, u32[]{:S(2)}) collective-permute-start(bf16[2,2,128,128]{3,2,1,0:T(8,128)(2,1)S(1)} %get-tuple-element.46), channel_id=1, source_target_pairs={{0,8},{4,12},{8,0},{12,4},{16,24},{20,28},{24,16},{28,20},{1,9},{5... | collective-permute-start | bytes 393224 | tf_op jit(solution)/shard_map/ppermute | solution.py:304
  6.4 8.1 %collective-permute-start.3 = (bf16[2,2,128,128]{3,2,1,0:T(8,128)(2,1)S(1)}, bf16[2,2,128,128]{3,2,1,0:T(8,128)(2,1)S(1)}, u32[]{:S(2)}, u32[]{:S(2)}) collective-permute-start(bf16[2,2,128,128]{3,2,1,0:T(8,128)(2,1)S(1)} %get-tuple-element.47), channel_id=1, source_target_pairs={{0,16},{4,20},{8,24},{12,28},{16,0},{20,4},{24,8},{28,12},{1,17},{... | collective-permute-start | bytes 393224 | tf_op jit(solution)/shard_map/ppermute | solution.py:304
  8.0 6.5 %collective-permute-start.4 = (bf16[2,2,128,128]{3,2,1,0:T(8,128)(2,1)S(1)}, bf16[2,2,128,128]{3,2,1,0:T(8,128)(2,1)S(1)}, u32[]{:S(2)}, u32[]{:S(2)}) collective-permute-start(bf16[2,2,128,128]{3,2,1,0:T(8,128)(2,1)S(1)} %get-tuple-element.48), channel_id=1, source_target_pairs={{0,24},{4,28},{8,16},{12,20},{16,8},{20,12},{24,0},{28,4},{1,25},{... | collective-permute-start | bytes 393224 | tf_op jit(solution)/shard_map/ppermute | solution.py:304
  10.3 4.2 %collective-permute-start.1 = (bf16[2,8,128,128]{3,2,1,0:T(8,128)(2,1)S(1)}, bf16[2,8,128,128]{3,2,1,0:T(8,128)(2,1)S(1)}, u32[]{:S(2)}, u32[]{:S(2)}) collective-permute-start(bf16[2,8,128,128]{3,2,1,0:T(8,128)(2,1)S(1)} %get-tuple-element.45), channel_id=1, source_target_pairs={{0,4},{4,0},{8,12},{12,8},{16,20},{20,16},{24,28},{28,24},{1,5},{5... | collective-permute-start | bytes 1572872 | tf_op jit(solution)/shard_map/ppermute | solution.py:304
  10.4 14.5 %collective-permute-start.7 = (bf16[2,8,128,128]{3,2,1,0:T(8,128)(2,1)S(1)}, bf16[2,8,128,128]{3,2,1,0:T(8,128)(2,1)}, u32[]{:S(2)}, u32[]{:S(2)}) collective-permute-start(bf16[2,8,128,128]{3,2,1,0:T(8,128)(2,1)S(1)} %get-tuple-element.52), channel_id=1, source_target_pairs={{0,4},{4,0},{8,12},{12,8},{16,20},{20,16},{24,28},{28,24},{1,5},{5... | collective-permute-start | bytes 1572872 | tf_op jit(solution)/shard_map/ppermute | solution.py:304
  14.6 5.1 %copy-start.2 = (s32[32,5]{0,1:T(8,128)S(1)}, s32[32,5]{0,1:T(8,128)}, u32[]{:S(2)}) copy-start(s32[32,5]{0,1:T(8,128)} %param.13) | copy-start | bytes 1924
  14.6 15.9 %collective-permute-start.5 = (bf16[2,8,128,128]{3,2,1,0:T(8,128)(2,1)S(1)}, bf16[2,8,128,128]{3,2,1,0:T(8,128)(2,1)}, u32[]{:S(2)}, u32[]{:S(2)}) collective-permute-start(bf16[2,8,128,128]{3,2,1,0:T(8,128)(2,1)S(1)} %get-tuple-element.50), channel_id=1, source_target_pairs={{0,24},{4,28},{8,16},{12,20},{16,8},{20,12},{24,0},{28,4},{1,25},{... | collective-permute-start | bytes 1572872 | tf_op jit(solution)/shard_map/ppermute | solution.py:304
  16.2 15.7 %collective-permute-start.6 = (bf16[8,2,128,128]{3,2,1,0:T(8,128)(2,1)S(1)}, bf16[8,2,128,128]{3,2,1,0:T(8,128)(2,1)S(1)}, u32[]{:S(2)}, u32[]{:S(2)}) collective-permute-start(bf16[8,2,128,128]{3,2,1,0:T(8,128)(2,1)S(1)} %shard_map.97.refs_3_.refs_2_), channel_id=1, source_target_pairs={{0,1},{1,2},{2,3},{4,5},{5,6},{6,7},{8,9},{9,10},{10,11},{12,13},{... | collective-permute-start | bytes 1572872 | tf_op jit(solution)/shard_map/ppermute | solution.py:298
  22.9 15.8 %collective-permute-start.10 = (bf16[1,8,128,128]{3,2,1,0:T(8,128)(2,1)}, bf16[1,8,128,128]{3,2,1,0:T(8,128)(2,1)S(1)}, u32[]{:S(2)}, u32[]{:S(2)}) collective-permute-start(bf16[1,8,128,128]{3,2,1,0:T(8,128)(2,1)} %get-tuple-element.53), channel_id=1, source_target_pairs={{0,8},{4,12},{8,0},{12,4},{16,24},{20,28},{24,16},{28,20},{1,9},{5... | collective-permute-start | bytes 786440 | tf_op jit(solution)/shard_map/ppermute | solution.py:304
  24.4 14.3 %collective-permute-start.11 = (bf16[1,8,128,128]{3,2,1,0:T(8,128)(2,1)}, bf16[1,8,128,128]{3,2,1,0:T(8,128)(2,1)S(1)}, u32[]{:S(2)}, u32[]{:S(2)}) collective-permute-start(bf16[1,8,128,128]{3,2,1,0:T(8,128)(2,1)} %get-tuple-element.54), channel_id=1, source_target_pairs={{0,16},{4,20},{8,24},{12,28},{16,0},{20,4},{24,8},{28,12},{1,17},{... | collective-permute-start | bytes 786440 | tf_op jit(solution)/shard_map/ppermute | solution.py:304
  26.0 15.7 %collective-permute-start.9 = (bf16[1,8,128,128]{3,2,1,0:T(8,128)(2,1)S(1)}, bf16[1,8,128,128]{3,2,1,0:T(8,128)(2,1)S(1)}, u32[]{:S(2)}, u32[]{:S(2)}) collective-permute-start(bf16[1,8,128,128]{3,2,1,0:T(8,128)(2,1)S(1)} %get-tuple-element.71), channel_id=1, source_target_pairs={{0,16},{4,20},{8,24},{12,28},{16,0},{20,4},{24,8},{28,12},{1,17},{... | collective-permute-start | bytes 786440 | tf_op jit(solution)/shard_map/ppermute | solution.py:304
  30.6 1.3 %copy-start = (f32[4,4096]{1,0:T(4,128)S(1)}, f32[4,4096]{1,0:T(4,128)}, u32[]{:S(2)}) copy-start(f32[4,4096]{1,0:T(4,128)} %lse_ref.5) | copy-start | bytes 196612
  30.6 1.3 %copy-start.1 = (f32[4,4096]{1,0:T(4,128)S(1)}, f32[4,4096]{1,0:T(4,128)}, u32[]{:S(2)}) copy-start(f32[4,4096]{1,0:T(4,128)} %delta_ref.5) | copy-start | bytes 196612
  30.6 11.2 %collective-permute-start.8 = (bf16[1,8,128,128]{3,2,1,0:T(8,128)(2,1)S(1)}, bf16[1,8,128,128]{3,2,1,0:T(8,128)(2,1)S(1)}, u32[]{:S(2)}, u32[]{:S(2)}) collective-permute-start(bf16[1,8,128,128]{3,2,1,0:T(8,128)(2,1)S(1)} %get-tuple-element.72), channel_id=1, source_target_pairs={{0,8},{4,12},{8,0},{12,4},{16,24},{20,28},{24,16},{28,20},{1,9},{5... | collective-permute-start | bytes 786440 | tf_op jit(solution)/shard_map/ppermute | solution.py:304
  36.9 14.9 %collective-permute-start.14 = (bf16[2,4,128,128]{3,2,1,0:T(8,128)(2,1)S(1)}, bf16[2,4,128,128]{3,2,1,0:T(8,128)(2,1)S(1)}, u32[]{:S(2)}, u32[]{:S(2)}) collective-permute-start(bf16[2,4,128,128]{3,2,1,0:T(8,128)(2,1)S(1)} %get-tuple-element.62), channel_id=1, source_target_pairs={{0,24},{4,28},{8,16},{12,20},{16,8},{20,12},{24,0},{28,4},{1,25},{... | collective-permute-start | bytes 786440 | tf_op jit(solution)/shard_map/ppermute | solution.py:304
  44.9 6.9 %collective-permute-start.18 = (bf16[2,2,128,128]{3,2,1,0:T(8,128)(2,1)S(1)}, bf16[2,2,128,128]{3,2,1,0:T(8,128)(2,1)S(1)}, u32[]{:S(2)}, u32[]{:S(2)}) collective-permute-start(bf16[2,2,128,128]{3,2,1,0:T(8,128)(2,1)S(1)} %get-tuple-element.66), channel_id=1, source_target_pairs={{1,0},{2,1},{3,2},{5,4},{6,5},{7,6},{9,8},{10,9},{11,10},{13,12},{... | collective-permute-start | bytes 393224 | tf_op jit(solution)/shard_map/ppermute | solution.py:298
  46.2 8.3 %collective-permute-start.12 = (bf16[2,4,128,128]{3,2,1,0:T(8,128)(2,1)S(1)}, bf16[2,4,128,128]{3,2,1,0:T(8,128)(2,1)S(1)}, u32[]{:S(2)}, u32[]{:S(2)}) collective-permute-start(bf16[2,4,128,128]{3,2,1,0:T(8,128)(2,1)S(1)} %get-tuple-element.60), channel_id=1, source_target_pairs={{0,8},{4,12},{8,0},{12,4},{16,24},{20,28},{24,16},{28,20},{1,9},{5... | collective-permute-start | bytes 786440 | tf_op jit(solution)/shard_map/ppermute | solution.py:304
  47.3 8.9 %collective-permute-start.13 = (bf16[2,4,128,128]{3,2,1,0:T(8,128)(2,1)S(1)}, bf16[2,4,128,128]{3,2,1,0:T(8,128)(2,1)S(1)}, u32[]{:S(2)}, u32[]{:S(2)}) collective-permute-start(bf16[2,4,128,128]{3,2,1,0:T(8,128)(2,1)S(1)} %get-tuple-element.61), channel_id=1, source_target_pairs={{0,16},{4,20},{8,24},{12,28},{16,0},{20,4},{24,8},{28,12},{1,17},{... | collective-permute-start | bytes 786440 | tf_op jit(solution)/shard_map/ppermute | solution.py:304
  48.2 10.6 %collective-permute-start.17 = (bf16[4,2,128,128]{3,2,1,0:T(8,128)(2,1)S(1)}, bf16[4,2,128,128]{3,2,1,0:T(8,128)(2,1)S(1)}, u32[]{:S(2)}, u32[]{:S(2)}) collective-permute-start(bf16[4,2,128,128]{3,2,1,0:T(8,128)(2,1)S(1)} %get-tuple-element.65), channel_id=1, source_target_pairs={{1,0},{2,1},{3,2},{5,4},{6,5},{7,6},{9,8},{10,9},{11,10},{13,12},{... | collective-permute-start | bytes 786440 | tf_op jit(solution)/shard_map/ppermute | solution.py:298
  51.8 7.0 %collective-permute-start.19 = (bf16[2,2,128,128]{3,2,1,0:T(8,128)(2,1)S(1)}, bf16[2,2,128,128]{3,2,1,0:T(8,128)(2,1)S(1)}, u32[]{:S(2)}, u32[]{:S(2)}) collective-permute-start(bf16[2,2,128,128]{3,2,1,0:T(8,128)(2,1)S(1)} %shard_map.106), channel_id=1, source_target_pairs={{0,24},{4,28},{8,16},{12,20},{16,8},{20,12},{24,0},{28,4},{1,25},{... | collective-permute-start | bytes 393224 | tf_op jit(solution)/shard_map/ppermute | solution.py:304
  53.2 9.3 %collective-permute-start.16 = (bf16[2,2,128,128]{3,2,1,0:T(8,128)(2,1)S(1)}, bf16[2,2,128,128]{3,2,1,0:T(8,128)(2,1)S(1)}, u32[]{:S(2)}, u32[]{:S(2)}) collective-permute-start(bf16[2,2,128,128]{3,2,1,0:T(8,128)(2,1)S(1)} %get-tuple-element.64), channel_id=1, source_target_pairs={{1,0},{2,1},{3,2},{5,4},{6,5},{7,6},{9,8},{10,9},{11,10},{13,12},{... | collective-permute-start | bytes 393224 | tf_op jit(solution)/shard_map/ppermute | solution.py:298
  56.3 4.7 %collective-permute-start.15 = (bf16[4,4,128,128]{3,2,1,0:T(8,128)(2,1)S(1)}, bf16[4,4,128,128]{3,2,1,0:T(8,128)(2,1)S(1)}, u32[]{:S(2)}, u32[]{:S(2)}) collective-permute-start(bf16[4,4,128,128]{3,2,1,0:T(8,128)(2,1)S(1)} %shard_map.104), channel_id=1, source_target_pairs={{0,4},{4,0},{8,12},{12,8},{16,20},{20,16},{24,28},{28,24},{1,5},{5... | collective-permute-start | bytes 1572872 | tf_op jit(solution)/shard_map/ppermute | solution.py:304
  58.9 5.0 %collective-permute-start.20 = (bf16[2,2,128,128]{3,2,1,0:T(8,128)(2,1)S(1)}, bf16[2,2,128,128]{3,2,1,0:T(8,128)(2,1)S(1)}, u32[]{:S(2)}, u32[]{:S(2)}) collective-permute-start(bf16[2,2,128,128]{3,2,1,0:T(8,128)(2,1)S(1)} %get-tuple-element.67), channel_id=1, source_target_pairs={{0,8},{4,12},{8,0},{12,4},{16,24},{20,28},{24,16},{28,20},{1,9},{5... | collective-permute-start | bytes 393224 | tf_op jit(solution)/shard_map/ppermute | solution.py:304
  60.4 5.0 %collective-permute-start.21 = (bf16[2,2,128,128]{3,2,1,0:T(8,128)(2,1)S(1)}, bf16[2,2,128,128]{3,2,1,0:T(8,128)(2,1)S(1)}, u32[]{:S(2)}, u32[]{:S(2)}) collective-permute-start(bf16[2,2,128,128]{3,2,1,0:T(8,128)(2,1)S(1)} %get-tuple-element.68), channel_id=1, source_target_pairs={{0,16},{4,20},{8,24},{12,28},{16,0},{20,4},{24,8},{28,12},{1,17},{... | collective-permute-start | bytes 393224 | tf_op jit(solution)/shard_map/ppermute | solution.py:304
  65.5 1.6 %collective-permute-start.22 = (bf16[4,2,128,128]{3,2,1,0:T(8,128)(2,1)S(1)}, bf16[4,2,128,128]{3,2,1,0:T(8,128)(2,1)S(1)}, u32[]{:S(2)}, u32[]{:S(2)}) collective-permute-start(bf16[4,2,128,128]{3,2,1,0:T(8,128)(2,1)S(1)} %shard_map.109), channel_id=1, source_target_pairs={{0,4},{4,0},{8,12},{12,8},{16,20},{20,16},{24,28},{28,24},{1,5},{5... | collective-permute-start | bytes 786440 | tf_op jit(solution)/shard_map/ppermute | solution.py:304

commit v6 on v5

--- a/solution.py
+++ b/solution.py
@@ -33,8 +33,8 @@
             own_out, *prev_out, acc, cat_k, cat_v = refs
         else:
             acc, cat_k, cat_v = refs
-    for half, dq_ref in zip(halves, dq_refs):
-        dq_ref[0] = half[0]
+    for half, dq_ref in zip(halves, dq_refs if call == LAST else dq_refs[-half_count:]):
+        dq_ref[: half.shape[0]] = half[...]
     slab_blocks = acc.shape[0] // 2
     heads = dq_refs[0].shape[1]
     select = keys_ref.shape[1]
@@ -166,8 +166,9 @@
 
 
 def merge_kernel(count, *refs):
-    got, outs = refs[count], refs[-count:]
+    pieces, got, outs = refs[:count], refs[count], refs[-count:]
     for i, out in enumerate(outs):
+        out[0] = pieces[i][0]
         out[1] = got[i]
 
 
@@ -332,7 +333,7 @@
     blocks = [(2 * m + i, operand, i, operand, i) for operand, m in enumerate(ends) for i in range(2)]
     dq_here, dq_far, kv, acc = grads(blocks, [2, 2], pieces=[qd_here, qd_far], halves=[], kept=[own, prev], call=FIRST)
     blocks = [(2 * m, i, 0, i, 0) for i, m in enumerate(mids)]
-    *halves, acc = grads(blocks, [1] * len(mids), pieces=firsts, halves=[], kept=[kv, acc], call=NEXT)
+    *halves, dq_far, acc = grads(blocks, [1] * len(mids) + [2], pieces=firsts, halves=[dq_far], kept=[kv, acc], call=NEXT)
     blocks = [(2 * m + 1, i, 0, i, 1) for i, m in enumerate(mids)]
     outs = grads(blocks, [2] * len(mids), pieces=seconds, halves=halves, kept=[kv, acc], call=LAST)
     *dq_mid, own_grad, prev_here, prev_mid, prev_far = outs

time: 68.3 us -> 67.7 us (level)
  starting transfers between devices: 26.9 us -> 26 us
    ppermute x4, waiting for transfers between devices: 4.71 us -> 6.92 us  [passed_along(): lax.ppermute(block, axis, [(i - distance, i) for i in devices if i - dist...]
    ppermute x19, waiting for transfers between devices: 14.1 us -> 11.9 us  [swapped(): lax.ppermute(block, 'uly', [(i, i ^ k) for i in range(lax.axis_size('uly'...]
    ppermute x19, starting transfers between devices: 19.6 us -> 18.7 us  [swapped(): lax.ppermute(block, 'uly', [(i, i ^ k) for i in range(lax.axis_size('uly'...]
  transfers between devices with their start and end apart: 23 -> 23, of which waited for: 11 -> 9; matrix products, arithmetic and copies ran while one was open for 2% -> 2% of each run, Pallas kernels for 27% -> 27%
where the time goes in v6:
time: 67.7 us; the launch traced here: 67.3 us
  starting transfers between devices  26 us (38%)
  Pallas kernels  20.4 us (30%)
  waiting for transfers between devices  18.8 us (28%)
  local copies, waits for them, and re-layouts  1.17 us (2%)
  between operations  0.89 us (1%)
    ppermute x19, starting transfers between devices, swapped(): lax.ppermute(block, 'uly', [(i, i ^ k) for i in range(lax.axis_size('uly'...  18.7 us
    ppermute x19, waiting for transfers between devices, swapped(): lax.ppermute(block, 'uly', [(i, i ^ k) for i in range(lax.axis_size('uly'...  11.9 us
    pallas_call x3, Pallas kernels, block_grads(): pl.pallas_call(functools.partial(block_kernel, blocks, len(out_rows), len...  11 us
    ppermute x4, starting transfers between devices, passed_along(): lax.ppermute(block, axis, [(i - distance, i) for i in devices if i - dist...  7.35 us
    ppermute x4, waiting for transfers between devices, passed_along(): lax.ppermute(block, axis, [(i - distance, i) for i in devices if i - dist...  6.92 us
    pallas_call x3, Pallas kernels, packed(): pl.pallas_call(functools.partial(pack_kernel, uly_count, fold_counts, kep...  6.58 us
    pallas_call x2, Pallas kernels, unpacked(): pl.pallas_call(functools.partial(unpack_kernel, chips, fold_count), in_sp...  2.38 us
  transfers between devices with their start and end apart: 23, of which 9 were waited for; matrix products, arithmetic and copies ran while one was open for 2% of the time, Pallas kernels for 27%

profile of v6, /device:TPU:0, one launch (start us, length us, event | category | flops | bytes accessed | tf_op | source)
XLA Modules:
  0.0 67.3 jit_solution(12608478141828661908)
XLA Ops:
  0.6 1.2 %shard_map.94 = (bf16[2,2,128,128]{3,2,1,0:T(8,128)(2,1)S(1)}, bf16[2,2,128,128]{3,2,1,0:T(8,128)(2,1)S(1)}, bf16[2,2,128,128]{3,2,1,0:T(8,128)(2,1)S(1)}, bf16[...) custom-call(s32[1]{0:T(128)} %bitcast.me_ref, bf16[128,8,128]{2,1,0:T(8,128)(2,1)} %refs_0_.3, ...), custom_call_target="tpu_custom_call" | custom-call | tf_op jit(solution)/shard_map/pallas_call | solution.py:154
  2.3 1.2 %collective-permute-done.refs_4_ = bf16[4,2,128,128]{3,2,1,0:T(8,128)(2,1)S(1)} collective-permute-done((bf16[4,2,128,128]{3,2,1,0:T(8,128)(2,1)S(1)}, bf16[4,2,128,128]{3,2,1,0:T(8,128)(2,1)S(1)}, u32[]{:S(2)}, u32[]{:S(2)}) %collective-permute-start) | collective-permute-done | bytes 262176 | tf_op jit(solution)/shard_map/ppermute | solution.py:305
  3.6 2.9 %collective-permute-start.2 = (bf16[2,2,128,128]{3,2,1,0:T(8,128)(2,1)S(1)}, bf16[2,2,128,128]{3,2,1,0:T(8,128)(2,1)S(1)}, u32[]{:S(2)}, u32[]{:S(2)}) collective-permute-start(bf16[2,2,128,128]{3,2,1,0:T(8,128)(2,1)S(1)} %get-tuple-element.47), channel_id=1, source_target_pairs={{0,8},{4,12},{8,0},{12,4},{16,24},{20,28},{24,16},{28,20},{1,9},{5... | collective-permute-start | bytes 393224 | tf_op jit(solution)/shard_map/ppermute | solution.py:305
  6.5 1.5 %collective-permute-start.3 = (bf16[2,2,128,128]{3,2,1,0:T(8,128)(2,1)S(1)}, bf16[2,2,128,128]{3,2,1,0:T(8,128)(2,1)S(1)}, u32[]{:S(2)}, u32[]{:S(2)}) collective-permute-start(bf16[2,2,128,128]{3,2,1,0:T(8,128)(2,1)S(1)} %get-tuple-element.48), channel_id=1, source_target_pairs={{0,16},{4,20},{8,24},{12,28},{16,0},{20,4},{24,8},{28,12},{1,17},{... | collective-permute-start | bytes 393224 | tf_op jit(solution)/shard_map/ppermute | solution.py:305
  8.1 2.3 %shard_map.96 = (bf16[2,8,128,128]{3,2,1,0:T(8,128)(2,1)S(1)}, bf16[2,8,128,128]{3,2,1,0:T(8,128)(2,1)S(1)}, bf16[2,8,128,128]{3,2,1,0:T(8,128)(2,1)S(1)}, bf16[2,8,128,128]{3,2,1,0:T(8,128)(2,1)S(1)}) custom-call(s32[1]{0:T(128)} %bitcast.me_ref, bf16[128,32,128]{2,1,0:T(8,128)(2,1)} %refs_0_.5, bf16[128,32,128]{2,1,0:T(8,128)(2,1)} %refs_1_.5, ...), custom_call_target="tpu_custom_call" | custom-call | tf_op jit(solution)/shard_map/pallas_call | solution.py:154
  11.0 3.6 %collective-permute-done.3.refs_2_ = bf16[2,2,128,128]{3,2,1,0:T(8,128)(2,1)S(1)} collective-permute-done((bf16[2,2,128,128]{3,2,1,0:T(8,128)(2,1)S(1)}, bf16[2,2,128,128]{3,2,1,0:T(8,128)(2,1)S(1)}, u32[]{:S(2)}, u32[]{:S(2)}) %collective-permute-start.3) | collective-permute-done | bytes 131104 | tf_op jit(solution)/shard_map/ppermute | solution.py:305
  14.8 1.6 %collective-permute-start.5 = (bf16[2,8,128,128]{3,2,1,0:T(8,128)(2,1)S(1)}, bf16[2,8,128,128]{3,2,1,0:T(8,128)(2,1)}, u32[]{:S(2)}, u32[]{:S(2)}) collective-permute-start(bf16[2,8,128,128]{3,2,1,0:T(8,128)(2,1)S(1)} %get-tuple-element.51), channel_id=1, source_target_pairs={{0,24},{4,28},{8,16},{12,20},{16,8},{20,12},{24,0},{28,4},{1,25},{... | collective-permute-start | bytes 1572872 | tf_op jit(solution)/shard_map/ppermute | solution.py:305
  16.4 3.5 %collective-permute-start.6 = (bf16[8,2,128,128]{3,2,1,0:T(8,128)(2,1)S(1)}, bf16[8,2,128,128]{3,2,1,0:T(8,128)(2,1)S(1)}, u32[]{:S(2)}, u32[]{:S(2)}) collective-permute-start(bf16[8,2,128,128]{3,2,1,0:T(8,128)(2,1)S(1)} %shard_map.97.refs_3_.refs_2_), channel_id=1, source_target_pairs={{0,1},{1,2},{2,3},{4,5},{5,6},{6,7},{8,9},{9,10},{10,11},{12,13},{... | collective-permute-start | bytes 1572872 | tf_op jit(solution)/shard_map/ppermute | solution.py:299
  20.0 3.1 %shard_map.101 = (bf16[1,8,128,128]{3,2,1,0:T(8,128)(2,1)}, bf16[1,8,128,128]{3,2,1,0:T(8,128)(2,1)}) custom-call(s32[1]{0:T(128)} %bitcast.me_ref, bf16[128,32,128]{2,1,0:T(8,128)(2,1)} %refs_0_.5, bf16[128,32,128]{2,1,0:T(8,128)(2,1)} %refs_1_.5, bf16[8,2,128,128]{3,2,1,0:T(8,128)(2,1)S(1)} %shard_map.97.refs_3_.refs_2_), custom_call_target="tpu_custom_call" | custom-call | tf_op jit(solution)/shard_map/pallas_call | solution.py:154
  23.1 1.6 %collective-permute-start.10 = (bf16[1,8,128,128]{3,2,1,0:T(8,128)(2,1)}, bf16[1,8,128,128]{3,2,1,0:T(8,128)(2,1)S(1)}, u32[]{:S(2)}, u32[]{:S(2)}) collective-permute-start(bf16[1,8,128,128]{3,2,1,0:T(8,128)(2,1)} %get-tuple-element.54), channel_id=1, source_target_pairs={{0,8},{4,12},{8,0},{12,4},{16,24},{20,28},{24,16},{28,20},{1,9},{5... | collective-permute-start | bytes 786440 | tf_op jit(solution)/shard_map/ppermute | solution.py:305
  25.1 1.1 %fusion = (bf16[1,8,128,128]{3,2,1,0:T(8,128)(2,1)S(1)}, bf16[1,8,128,128]{3,2,1,0:T(8,128)(2,1)S(1)}) fusion(bf16[2,8,128,128]{3,2,1,0:T(8,128)(2,1)} %collective-permute-done.7), kind=kLoop, calls=%fused_computation | loop fusion | bytes 1048576 | tf_op jit(solution)/shard_map/slice | solution.py:329
  26.2 1.6 %collective-permute-start.9 = (bf16[1,8,128,128]{3,2,1,0:T(8,128)(2,1)S(1)}, bf16[1,8,128,128]{3,2,1,0:T(8,128)(2,1)S(1)}, u32[]{:S(2)}, u32[]{:S(2)}) collective-permute-start(bf16[1,8,128,128]{3,2,1,0:T(8,128)(2,1)S(1)} %get-tuple-element.73), channel_id=1, source_target_pairs={{0,16},{4,20},{8,24},{12,28},{16,0},{20,4},{24,8},{28,12},{1,17},{... | collective-permute-start | bytes 786440 | tf_op jit(solution)/shard_map/ppermute | solution.py:305
  27.8 3.0 %collective-permute-done.5.refs_0_ = bf16[2,8,128,128]{3,2,1,0:T(8,128)(2,1)} collective-permute-done((bf16[2,8,128,128]{3,2,1,0:T(8,128)(2,1)S(1)}, bf16[2,8,128,128]{3,2,1,0:T(8,128)(2,1)}, u32[]{:S(2)}, u32[]{:S(2)}) %collective-permute-start.5) | collective-permute-done | bytes 524320 | tf_op jit(solution)/shard_map/ppermute | solution.py:305
  30.8 1.3 %collective-permute-start.8 = (bf16[1,8,128,128]{3,2,1,0:T(8,128)(2,1)S(1)}, bf16[1,8,128,128]{3,2,1,0:T(8,128)(2,1)S(1)}, u32[]{:S(2)}, u32[]{:S(2)}) collective-permute-start(bf16[1,8,128,128]{3,2,1,0:T(8,128)(2,1)S(1)} %get-tuple-element.74), channel_id=1, source_target_pairs={{0,8},{4,12},{8,0},{12,4},{16,24},{20,28},{24,16},{28,20},{1,9},{5... | collective-permute-start | bytes 786440 | tf_op jit(solution)/shard_map/ppermute | solution.py:305
  32.0 5.0 %shard_map.100 = (bf16[2,4,128,128]{3,2,1,0:T(8,128)(2,1)S(1)}, bf16[2,4,128,128]{3,2,1,0:T(8,128)(2,1)S(1)}, bf16[16,2,128,128]{3,2,1,0:T(8,128)(2,1)S(1)}, f32[16,2,128,128]{3,2,1,0:T(8,128)S(1)}) custom-call(s32[1]{0:T(128)} %bitcast.1.slab_ref, s32[1]{0:T(128)} %bitcast.me_ref, s32[32,5]{1,0:T(8,128)S(1)} %copy.17.keys_ref, f32[4,4096]{1,0:T(4,128)S(1)} %copy-done, ...), custom_call_target="tpu_custom_call" | custom-call | flops 1677721600 | bytes 8388608 | tf_op jit(solution)/shard_map/pallas_call | solution.py:115
  37.1 2.9 %shard_map.102 = (bf16[1,4,128,128]{3,2,1,0:T(8,128)(2,1)S(1)}, bf16[1,4,128,128]{3,2,1,0:T(8,128)(2,1)S(1)}, bf16[2,4,128,128]{3,2,1,0:T(8,128)(2,1)S(1)}, f32[16,2,128,128]{3,2,1,0:T(8,128)S(1)}) custom-call(s32[1]{0:T(128)} %bitcast.1.slab_ref, s32[1]{0:T(128)} %bitcast.me_ref, s32[32,5]{1,0:T(8,128)S(1)} %copy.17.keys_ref, f32[4,4096]{1,0:T(4,128)S(1)} %copy-done, ...), custom_call_target="tpu_custom_call" | custom-call | flops 838860800 | bytes 8388608 | tf_op jit(solution)/shard_map/pallas_call | solution.py:115
  40.0 1.8 %collective-permute-start.14 = (bf16[2,4,128,128]{3,2,1,0:T(8,128)(2,1)S(1)}, bf16[2,4,128,128]{3,2,1,0:T(8,128)(2,1)S(1)}, u32[]{:S(2)}, u32[]{:S(2)}) collective-permute-start(bf16[2,4,128,128]{3,2,1,0:T(8,128)(2,1)S(1)} %get-tuple-element.64), channel_id=1, source_target_pairs={{0,24},{4,28},{8,16},{12,20},{16,8},{20,12},{24,0},{28,4},{1,25},{... | collective-permute-start | bytes 786440 | tf_op jit(solution)/shard_map/ppermute | solution.py:305
  41.8 3.1 %shard_map.103 = (bf16[2,4,128,128]{3,2,1,0:T(8,128)(2,1)S(1)}, bf16[2,4,128,128]{3,2,1,0:T(8,128)(2,1)S(1)}, f32[8,2,128,128]{3,2,1,0:T(8,128)S(1)}, bf16[2,2,1...) custom-call(s32[1]{0:T(128)} %bitcast.1.slab_ref, ...), custom_call_target="tpu_custom_call" | custom-call | flops 838860800 | bytes 8388608 | tf_op jit(solution)/shard_map/pallas_call | solution.py:115
  44.9 1.3 %collective-permute-start.18 = (bf16[2,2,128,128]{3,2,1,0:T(8,128)(2,1)S(1)}, bf16[2,2,128,128]{3,2,1,0:T(8,128)(2,1)S(1)}, u32[]{:S(2)}, u32[]{:S(2)}) collective-permute-start(bf16[2,2,128,128]{3,2,1,0:T(8,128)(2,1)S(1)} %get-tuple-element.68), channel_id=1, source_target_pairs={{1,0},{2,1},{3,2},{5,4},{6,5},{7,6},{9,8},{10,9},{11,10},{13,12},{... | collective-permute-start | bytes 393224 | tf_op jit(solution)/shard_map/ppermute | solution.py:299
  46.2 0.9 %collective-permute-start.12 = (bf16[2,4,128,128]{3,2,1,0:T(8,128)(2,1)S(1)}, bf16[2,4,128,128]{3,2,1,0:T(8,128)(2,1)S(1)}, u32[]{:S(2)}, u32[]{:S(2)}) collective-permute-start(bf16[2,4,128,128]{3,2,1,0:T(8,128)(2,1)S(1)} %get-tuple-element.62), channel_id=1, source_target_pairs={{0,8},{4,12},{8,0},{12,4},{16,24},{20,28},{24,16},{28,20},{1,9},{5... | collective-permute-start | bytes 786440 | tf_op jit(solution)/shard_map/ppermute | solution.py:305
  47.1 0.9 %collective-permute-start.13 = (bf16[2,4,128,128]{3,2,1,0:T(8,128)(2,1)S(1)}, bf16[2,4,128,128]{3,2,1,0:T(8,128)(2,1)S(1)}, u32[]{:S(2)}, u32[]{:S(2)}) collective-permute-start(bf16[2,4,128,128]{3,2,1,0:T(8,128)(2,1)S(1)} %get-tuple-element.63), channel_id=1, source_target_pairs={{0,16},{4,20},{8,24},{12,28},{16,0},{20,4},{24,8},{28,12},{1,17},{... | collective-permute-start | bytes 786440 | tf_op jit(solution)/shard_map/ppermute | solution.py:305
  48.0 1.3 %collective-permute-start.17 = (bf16[4,2,128,128]{3,2,1,0:T(8,128)(2,1)S(1)}, bf16[4,2,128,128]{3,2,1,0:T(8,128)(2,1)S(1)}, u32[]{:S(2)}, u32[]{:S(2)}) collective-permute-start(bf16[4,2,128,128]{3,2,1,0:T(8,128)(2,1)S(1)} %get-tuple-element.67), channel_id=1, source_target_pairs={{1,0},{2,1},{3,2},{5,4},{6,5},{7,6},{9,8},{10,9},{11,10},{13,12},{... | collective-permute-start | bytes 786440 | tf_op jit(solution)/shard_map/ppermute | solution.py:299
  49.3 3.6 %collective-permute-done.18.back = bf16[2,2,128,128]{3,2,1,0:T(8,128)(2,1)S(1)} collective-permute-done((bf16[2,2,128,128]{3,2,1,0:T(8,128)(2,1)S(1)}, bf16[2,2,128,128]{3,2,1,0:T(8,128)(2,1)S(1)}, u32[]{:S(2)}, u32[]{:S(2)}) %collective-permute-start.18) | collective-permute-done | bytes 131104 | tf_op jit(solution)/shard_map/ppermute | solution.py:299
  52.9 1.1 %collective-permute-start.19 = (bf16[2,2,128,128]{3,2,1,0:T(8,128)(2,1)S(1)}, bf16[2,2,128,128]{3,2,1,0:T(8,128)(2,1)S(1)}, u32[]{:S(2)}, u32[]{:S(2)}) collective-permute-start(bf16[2,2,128,128]{3,2,1,0:T(8,128)(2,1)S(1)} %shard_map.106), channel_id=1, source_target_pairs={{0,24},{4,28},{8,16},{12,20},{16,8},{20,12},{24,0},{28,4},{1,25},{... | collective-permute-start | bytes 393224 | tf_op jit(solution)/shard_map/ppermute | solution.py:305
  54.0 1.3 %collective-permute-start.16 = (bf16[2,2,128,128]{3,2,1,0:T(8,128)(2,1)S(1)}, bf16[2,2,128,128]{3,2,1,0:T(8,128)(2,1)S(1)}, u32[]{:S(2)}, u32[]{:S(2)}) collective-permute-start(bf16[2,2,128,128]{3,2,1,0:T(8,128)(2,1)S(1)} %get-tuple-element.66), channel_id=1, source_target_pairs={{1,0},{2,1},{3,2},{5,4},{6,5},{7,6},{9,8},{10,9},{11,10},{13,12},{... | collective-permute-start | bytes 393224 | tf_op jit(solution)/shard_map/ppermute | solution.py:299
  55.5 3.3 %collective-permute-done.17.back = bf16[4,2,128,128]{3,2,1,0:T(8,128)(2,1)S(1)} collective-permute-done((bf16[4,2,128,128]{3,2,1,0:T(8,128)(2,1)S(1)}, bf16[4,2,128,128]{3,2,1,0:T(8,128)(2,1)S(1)}, u32[]{:S(2)}, u32[]{:S(2)}) %collective-permute-start.17) | collective-permute-done | bytes 262176 | tf_op jit(solution)/shard_map/ppermute | solution.py:299
  58.9 0.9 %collective-permute-start.20 = (bf16[2,2,128,128]{3,2,1,0:T(8,128)(2,1)S(1)}, bf16[2,2,128,128]{3,2,1,0:T(8,128)(2,1)S(1)}, u32[]{:S(2)}, u32[]{:S(2)}) collective-permute-start(bf16[2,2,128,128]{3,2,1,0:T(8,128)(2,1)S(1)} %get-tuple-element.69), channel_id=1, source_target_pairs={{0,8},{4,12},{8,0},{12,4},{16,24},{20,28},{24,16},{28,20},{1,9},{5... | collective-permute-start | bytes 393224 | tf_op jit(solution)/shard_map/ppermute | solution.py:305
  59.8 0.9 %collective-permute-start.21 = (bf16[2,2,128,128]{3,2,1,0:T(8,128)(2,1)S(1)}, bf16[2,2,128,128]{3,2,1,0:T(8,128)(2,1)S(1)}, u32[]{:S(2)}, u32[]{:S(2)}) collective-permute-start(bf16[2,2,128,128]{3,2,1,0:T(8,128)(2,1)S(1)} %get-tuple-element.70), channel_id=1, source_target_pairs={{0,16},{4,20},{8,24},{12,28},{16,0},{20,4},{24,8},{28,12},{1,17},{... | collective-permute-start | bytes 393224 | tf_op jit(solution)/shard_map/ppermute | solution.py:305
  60.7 1.5 %shard_map.105.refs_2_ = bf16[128,32,128]{2,1,0:T(8,128)(2,1)} custom-call(s32[1]{0:T(128)} %bitcast.me_ref, bf16[2,4,128,128]{3,2,1,0:T(8,128)(2,1)S(1)} %get-tuple-element.52.refs_0_, bf16[2,4,128,128]{3,2,1,0:T(8,128)(2,1)S(1)} %collective-permute-done.12.refs_1_.refs_0_, bf16[2,4,128,128]{3,2,1,0:T(8,128)(2,1)S(1)} %collective-permute-done.13.refs_2_.refs_1_, ...), custom_call_target="tpu_custom_call" | custom-call | tf_op jit(solution)/shard_map/pallas_call | solution.py:285
  62.2 1.8 %collective-permute-done.20.refs_0_.refs_1_ = bf16[2,2,128,128]{3,2,1,0:T(8,128)(2,1)S(1)} collective-permute-done((bf16[2,2,128,128]{3,2,1,0:T(8,128)(2,1)S(1)}, bf16[2,2,128,128]{3,2,1,0:T(8,128)(2,1)S(1)}, u32[]{:S(2)}, u32[]{:S(2)}) %collective-permute-start.20) | collective-permute-done | bytes 131104 | tf_op jit(solution)/shard_map/ppermute | solution.py:305
  64.9 1.5 %collective-permute-done.22.refs_4_ = bf16[4,2,128,128]{3,2,1,0:T(8,128)(2,1)S(1)} collective-permute-done((bf16[4,2,128,128]{3,2,1,0:T(8,128)(2,1)S(1)}, bf16[4,2,128,128]{3,2,1,0:T(8,128)(2,1)S(1)}, u32[]{:S(2)}, u32[]{:S(2)}) %collective-permute-start.22) | collective-permute-done | bytes 262176 | tf_op jit(solution)/shard_map/ppermute | solution.py:305
  66.4 0.9 %shard_map.110 = (bf16[128,8,128]{2,1,0:T(8,128)(2,1)}, bf16[128,8,128]{2,1,0:T(8,128)(2,1)}) custom-call(s32[1]{0:T(128)} %bitcast.me_ref, bf16[2,2,128,128]{3,2,1,0:T(8,128)(2,1)S(1)} %shard_map.108.refs_0_, bf16[2,2,128,128]{3,2,1,0:T(8,128)(2,1)S(1)} %collective-permute-done.20.refs_0_.refs_1_, ...), custom_call_target="tpu_custom_call" | custom-call | tf_op jit(solution)/shard_map/pallas_call | solution.py:285
  (39 shorter events, 3.2 us)
Async XLA Ops:
  1.8 1.7 %collective-permute-start = (bf16[4,2,128,128]{3,2,1,0:T(8,128)(2,1)S(1)}, bf16[4,2,128,128]{3,2,1,0:T(8,128)(2,1)S(1)}, u32[]{:S(2)}, u32[]{:S(2)}) collective-permute-start(bf16[4,2,128,128]{3,2,1,0:T(8,128)(2,1)S(1)} %get-tuple-element.42), channel_id=1, source_target_pairs={{0,4},{4,0},{8,12},{12,8},{16,20},{20,16},{24,28},{28,24},{1,5},{5... | collective-permute-start | bytes 786440 | tf_op jit(solution)/shard_map/ppermute | solution.py:305
  3.6 7.4 %collective-permute-start.2 = (bf16[2,2,128,128]{3,2,1,0:T(8,128)(2,1)S(1)}, bf16[2,2,128,128]{3,2,1,0:T(8,128)(2,1)S(1)}, u32[]{:S(2)}, u32[]{:S(2)}) collective-permute-start(bf16[2,2,128,128]{3,2,1,0:T(8,128)(2,1)S(1)} %get-tuple-element.47), channel_id=1, source_target_pairs={{0,8},{4,12},{8,0},{12,4},{16,24},{20,28},{24,16},{28,20},{1,9},{5... | collective-permute-start | bytes 393224 | tf_op jit(solution)/shard_map/ppermute | solution.py:305
  6.5 8.1 %collective-permute-start.3 = (bf16[2,2,128,128]{3,2,1,0:T(8,128)(2,1)S(1)}, bf16[2,2,128,128]{3,2,1,0:T(8,128)(2,1)S(1)}, u32[]{:S(2)}, u32[]{:S(2)}) collective-permute-start(bf16[2,2,128,128]{3,2,1,0:T(8,128)(2,1)S(1)} %get-tuple-element.48), channel_id=1, source_target_pairs={{0,16},{4,20},{8,24},{12,28},{16,0},{20,4},{24,8},{28,12},{1,17},{... | collective-permute-start | bytes 393224 | tf_op jit(solution)/shard_map/ppermute | solution.py:305
  8.0 6.5 %collective-permute-start.4 = (bf16[2,2,128,128]{3,2,1,0:T(8,128)(2,1)S(1)}, bf16[2,2,128,128]{3,2,1,0:T(8,128)(2,1)S(1)}, u32[]{:S(2)}, u32[]{:S(2)}) collective-permute-start(bf16[2,2,128,128]{3,2,1,0:T(8,128)(2,1)S(1)} %get-tuple-element.49), channel_id=1, source_target_pairs={{0,24},{4,28},{8,16},{12,20},{16,8},{20,12},{24,0},{28,4},{1,25},{... | collective-permute-start | bytes 393224 | tf_op jit(solution)/shard_map/ppermute | solution.py:305
  10.4 4.2 %collective-permute-start.1 = (bf16[2,8,128,128]{3,2,1,0:T(8,128)(2,1)S(1)}, bf16[2,8,128,128]{3,2,1,0:T(8,128)(2,1)S(1)}, u32[]{:S(2)}, u32[]{:S(2)}) collective-permute-start(bf16[2,8,128,128]{3,2,1,0:T(8,128)(2,1)S(1)} %get-tuple-element.46), channel_id=1, source_target_pairs={{0,4},{4,0},{8,12},{12,8},{16,20},{20,16},{24,28},{28,24},{1,5},{5... | collective-permute-start | bytes 1572872 | tf_op jit(solution)/shard_map/ppermute | solution.py:305
  10.5 14.6 %collective-permute-start.7 = (bf16[2,8,128,128]{3,2,1,0:T(8,128)(2,1)S(1)}, bf16[2,8,128,128]{3,2,1,0:T(8,128)(2,1)}, u32[]{:S(2)}, u32[]{:S(2)}) collective-permute-start(bf16[2,8,128,128]{3,2,1,0:T(8,128)(2,1)S(1)} %get-tuple-element.53), channel_id=1, source_target_pairs={{0,4},{4,0},{8,12},{12,8},{16,20},{20,16},{24,28},{28,24},{1,5},{5... | collective-permute-start | bytes 1572872 | tf_op jit(solution)/shard_map/ppermute | solution.py:305
  14.6 5.3 %copy-start.2 = (s32[32,5]{0,1:T(8,128)S(1)}, s32[32,5]{0,1:T(8,128)}, u32[]{:S(2)}) copy-start(s32[32,5]{0,1:T(8,128)} %param.13) | copy-start | bytes 1924
  14.8 15.9 %collective-permute-start.5 = (bf16[2,8,128,128]{3,2,1,0:T(8,128)(2,1)S(1)}, bf16[2,8,128,128]{3,2,1,0:T(8,128)(2,1)}, u32[]{:S(2)}, u32[]{:S(2)}) collective-permute-start(bf16[2,8,128,128]{3,2,1,0:T(8,128)(2,1)S(1)} %get-tuple-element.51), channel_id=1, source_target_pairs={{0,24},{4,28},{8,16},{12,20},{16,8},{20,12},{24,0},{28,4},{1,25},{... | collective-permute-start | bytes 1572872 | tf_op jit(solution)/shard_map/ppermute | solution.py:305
  16.4 15.7 %collective-permute-start.6 = (bf16[8,2,128,128]{3,2,1,0:T(8,128)(2,1)S(1)}, bf16[8,2,128,128]{3,2,1,0:T(8,128)(2,1)S(1)}, u32[]{:S(2)}, u32[]{:S(2)}) collective-permute-start(bf16[8,2,128,128]{3,2,1,0:T(8,128)(2,1)S(1)} %shard_map.97.refs_3_.refs_2_), channel_id=1, source_target_pairs={{0,1},{1,2},{2,3},{4,5},{5,6},{6,7},{8,9},{9,10},{10,11},{12,13},{... | collective-permute-start | bytes 1572872 | tf_op jit(solution)/shard_map/ppermute | solution.py:299
  23.1 14.0 %collective-permute-start.10 = (bf16[1,8,128,128]{3,2,1,0:T(8,128)(2,1)}, bf16[1,8,128,128]{3,2,1,0:T(8,128)(2,1)S(1)}, u32[]{:S(2)}, u32[]{:S(2)}) collective-permute-start(bf16[1,8,128,128]{3,2,1,0:T(8,128)(2,1)} %get-tuple-element.54), channel_id=1, source_target_pairs={{0,8},{4,12},{8,0},{12,4},{16,24},{20,28},{24,16},{28,20},{1,9},{5... | collective-permute-start | bytes 786440 | tf_op jit(solution)/shard_map/ppermute | solution.py:305
  24.6 12.4 %collective-permute-start.11 = (bf16[1,8,128,128]{3,2,1,0:T(8,128)(2,1)}, bf16[1,8,128,128]{3,2,1,0:T(8,128)(2,1)S(1)}, u32[]{:S(2)}, u32[]{:S(2)}) collective-permute-start(bf16[1,8,128,128]{3,2,1,0:T(8,128)(2,1)} %get-tuple-element.55), channel_id=1, source_target_pairs={{0,16},{4,20},{8,24},{12,28},{16,0},{20,4},{24,8},{28,12},{1,17},{... | collective-permute-start | bytes 786440 | tf_op jit(solution)/shard_map/ppermute | solution.py:305
  26.2 15.6 %collective-permute-start.9 = (bf16[1,8,128,128]{3,2,1,0:T(8,128)(2,1)S(1)}, bf16[1,8,128,128]{3,2,1,0:T(8,128)(2,1)S(1)}, u32[]{:S(2)}, u32[]{:S(2)}) collective-permute-start(bf16[1,8,128,128]{3,2,1,0:T(8,128)(2,1)S(1)} %get-tuple-element.73), channel_id=1, source_target_pairs={{0,16},{4,20},{8,24},{12,28},{16,0},{20,4},{24,8},{28,12},{1,17},{... | collective-permute-start | bytes 786440 | tf_op jit(solution)/shard_map/ppermute | solution.py:305
  30.8 1.3 %copy-start = (f32[4,4096]{1,0:T(4,128)S(1)}, f32[4,4096]{1,0:T(4,128)}, u32[]{:S(2)}) copy-start(f32[4,4096]{1,0:T(4,128)} %lse_ref.5) | copy-start | bytes 196612
  30.8 1.3 %copy-start.1 = (f32[4,4096]{1,0:T(4,128)S(1)}, f32[4,4096]{1,0:T(4,128)}, u32[]{:S(2)}) copy-start(f32[4,4096]{1,0:T(4,128)} %delta_ref.5) | copy-start | bytes 196612
  30.8 11.1 %collective-permute-start.8 = (bf16[1,8,128,128]{3,2,1,0:T(8,128)(2,1)S(1)}, bf16[1,8,128,128]{3,2,1,0:T(8,128)(2,1)S(1)}, u32[]{:S(2)}, u32[]{:S(2)}) collective-permute-start(bf16[1,8,128,128]{3,2,1,0:T(8,128)(2,1)S(1)} %get-tuple-element.74), channel_id=1, source_target_pairs={{0,8},{4,12},{8,0},{12,4},{16,24},{20,28},{24,16},{28,20},{1,9},{5... | collective-permute-start | bytes 786440 | tf_op jit(solution)/shard_map/ppermute | solution.py:305
  40.0 12.9 %collective-permute-start.14 = (bf16[2,4,128,128]{3,2,1,0:T(8,128)(2,1)S(1)}, bf16[2,4,128,128]{3,2,1,0:T(8,128)(2,1)S(1)}, u32[]{:S(2)}, u32[]{:S(2)}) collective-permute-start(bf16[2,4,128,128]{3,2,1,0:T(8,128)(2,1)S(1)} %get-tuple-element.64), channel_id=1, source_target_pairs={{0,24},{4,28},{8,16},{12,20},{16,8},{20,12},{24,0},{28,4},{1,25},{... | collective-permute-start | bytes 786440 | tf_op jit(solution)/shard_map/ppermute | solution.py:305
  44.9 8.0 %collective-permute-start.18 = (bf16[2,2,128,128]{3,2,1,0:T(8,128)(2,1)S(1)}, bf16[2,2,128,128]{3,2,1,0:T(8,128)(2,1)S(1)}, u32[]{:S(2)}, u32[]{:S(2)}) collective-permute-start(bf16[2,2,128,128]{3,2,1,0:T(8,128)(2,1)S(1)} %get-tuple-element.68), channel_id=1, source_target_pairs={{1,0},{2,1},{3,2},{5,4},{6,5},{7,6},{9,8},{10,9},{11,10},{13,12},{... | collective-permute-start | bytes 393224 | tf_op jit(solution)/shard_map/ppermute | solution.py:299
  46.2 9.1 %collective-permute-start.12 = (bf16[2,4,128,128]{3,2,1,0:T(8,128)(2,1)S(1)}, bf16[2,4,128,128]{3,2,1,0:T(8,128)(2,1)S(1)}, u32[]{:S(2)}, u32[]{:S(2)}) collective-permute-start(bf16[2,4,128,128]{3,2,1,0:T(8,128)(2,1)S(1)} %get-tuple-element.62), channel_id=1, source_target_pairs={{0,8},{4,12},{8,0},{12,4},{16,24},{20,28},{24,16},{28,20},{1,9},{5... | collective-permute-start | bytes 786440 | tf_op jit(solution)/shard_map/ppermute | solution.py:305
  47.1 8.2 %collective-permute-start.13 = (bf16[2,4,128,128]{3,2,1,0:T(8,128)(2,1)S(1)}, bf16[2,4,128,128]{3,2,1,0:T(8,128)(2,1)S(1)}, u32[]{:S(2)}, u32[]{:S(2)}) collective-permute-start(bf16[2,4,128,128]{3,2,1,0:T(8,128)(2,1)S(1)} %get-tuple-element.63), channel_id=1, source_target_pairs={{0,16},{4,20},{8,24},{12,28},{16,0},{20,4},{24,8},{28,12},{1,17},{... | collective-permute-start | bytes 786440 | tf_op jit(solution)/shard_map/ppermute | solution.py:305
  48.0 10.8 %collective-permute-start.17 = (bf16[4,2,128,128]{3,2,1,0:T(8,128)(2,1)S(1)}, bf16[4,2,128,128]{3,2,1,0:T(8,128)(2,1)S(1)}, u32[]{:S(2)}, u32[]{:S(2)}) collective-permute-start(bf16[4,2,128,128]{3,2,1,0:T(8,128)(2,1)S(1)} %get-tuple-element.67), channel_id=1, source_target_pairs={{1,0},{2,1},{3,2},{5,4},{6,5},{7,6},{9,8},{10,9},{11,10},{13,12},{... | collective-permute-start | bytes 786440 | tf_op jit(solution)/shard_map/ppermute | solution.py:299
  52.9 5.9 %collective-permute-start.19 = (bf16[2,2,128,128]{3,2,1,0:T(8,128)(2,1)S(1)}, bf16[2,2,128,128]{3,2,1,0:T(8,128)(2,1)S(1)}, u32[]{:S(2)}, u32[]{:S(2)}) collective-permute-start(bf16[2,2,128,128]{3,2,1,0:T(8,128)(2,1)S(1)} %shard_map.106), channel_id=1, source_target_pairs={{0,24},{4,28},{8,16},{12,20},{16,8},{20,12},{24,0},{28,4},{1,25},{... | collective-permute-start | bytes 393224 | tf_op jit(solution)/shard_map/ppermute | solution.py:305
  54.0 8.1 %collective-permute-start.16 = (bf16[2,2,128,128]{3,2,1,0:T(8,128)(2,1)S(1)}, bf16[2,2,128,128]{3,2,1,0:T(8,128)(2,1)S(1)}, u32[]{:S(2)}, u32[]{:S(2)}) collective-permute-start(bf16[2,2,128,128]{3,2,1,0:T(8,128)(2,1)S(1)} %get-tuple-element.66), channel_id=1, source_target_pairs={{1,0},{2,1},{3,2},{5,4},{6,5},{7,6},{9,8},{10,9},{11,10},{13,12},{... | collective-permute-start | bytes 393224 | tf_op jit(solution)/shard_map/ppermute | solution.py:299
  55.4 5.3 %collective-permute-start.15 = (bf16[4,4,128,128]{3,2,1,0:T(8,128)(2,1)S(1)}, bf16[4,4,128,128]{3,2,1,0:T(8,128)(2,1)S(1)}, u32[]{:S(2)}, u32[]{:S(2)}) collective-permute-start(bf16[4,4,128,128]{3,2,1,0:T(8,128)(2,1)S(1)} %shard_map.104), channel_id=1, source_target_pairs={{0,4},{4,0},{8,12},{12,8},{16,20},{20,16},{24,28},{28,24},{1,5},{5... | collective-permute-start | bytes 1572872 | tf_op jit(solution)/shard_map/ppermute | solution.py:305
  58.9 5.0 %collective-permute-start.20 = (bf16[2,2,128,128]{3,2,1,0:T(8,128)(2,1)S(1)}, bf16[2,2,128,128]{3,2,1,0:T(8,128)(2,1)S(1)}, u32[]{:S(2)}, u32[]{:S(2)}) collective-permute-start(bf16[2,2,128,128]{3,2,1,0:T(8,128)(2,1)S(1)} %get-tuple-element.69), channel_id=1, source_target_pairs={{0,8},{4,12},{8,0},{12,4},{16,24},{20,28},{24,16},{28,20},{1,9},{5... | collective-permute-start | bytes 393224 | tf_op jit(solution)/shard_map/ppermute | solution.py:305
  59.8 5.0 %collective-permute-start.21 = (bf16[2,2,128,128]{3,2,1,0:T(8,128)(2,1)S(1)}, bf16[2,2,128,128]{3,2,1,0:T(8,128)(2,1)S(1)}, u32[]{:S(2)}, u32[]{:S(2)}) collective-permute-start(bf16[2,2,128,128]{3,2,1,0:T(8,128)(2,1)S(1)} %get-tuple-element.70), channel_id=1, source_target_pairs={{0,16},{4,20},{8,24},{12,28},{16,0},{20,4},{24,8},{28,12},{1,17},{... | collective-permute-start | bytes 393224 | tf_op jit(solution)/shard_map/ppermute | solution.py:305
  64.8 1.6 %collective-permute-start.22 = (bf16[4,2,128,128]{3,2,1,0:T(8,128)(2,1)S(1)}, bf16[4,2,128,128]{3,2,1,0:T(8,128)(2,1)S(1)}, u32[]{:S(2)}, u32[]{:S(2)}) collective-permute-start(bf16[4,2,128,128]{3,2,1,0:T(8,128)(2,1)S(1)} %shard_map.109), channel_id=1, source_target_pairs={{0,4},{4,0},{8,12},{12,8},{16,20},{20,16},{24,28},{28,24},{1,5},{5... | collective-permute-start | bytes 786440 | tf_op jit(solution)/shard_map/ppermute | solution.py:305
